TPU v7x, 32 devices: a whole 2x2x4 slice. The times are simulated.
32 devices in a mesh: tok: 8 (over y, x, core), head: 4 (over z).
Axes of the slice: x: 2, y: 2, z: 4, core: 2. Of those that a mesh axis runs over, the one named last changes fastest.
Arguments:
- queries: bfloat16 [32, 8192, 128], P('head', 'tok'), may hold values from -6 to 6
- keys: bfloat16 [4, 8192, 128], P('head', 'tok'), may hold values from -6 to 6
- values: bfloat16 [4, 8192, 128], P('head', 'tok'), may hold values from -6 to 6
- doc_lengths: int32 [8], replicated, may hold values from 1 to 4096, as said below
- tasks: int32 [128, 5], replicated, may hold values from 0 to 16, as said below
- w_out: bfloat16 [4096, 2048], P('head'), may hold values from -0.09375 to 0.09375
Outputs:
- projected: bfloat16 [8192, 2048], P('tok', 'head')
Inputs may be any that keep to these rules, and one draw needn't show every extreme that they name: `doc_lengths`: the documents lie end to end; their lengths sum to 8192, and one is exactly 4096 tokens long. `tasks`: row t = qb * 8 + j describes query block qb (tokens qb * 512 to qb * 512 + 511) and head j of every group: column 0 is qb, column 1 is j, column 2 is the block that holds the first token of the document of the block's first token, column 3 is qb + 1, column 4 is the server, a token shard. Rows of one token shard's blocks name one server at most 2 times, 2 is reached, and every server is named in exactly 16 rows.
All inputs are finite; a program needn't handle non-finite values.
Results may differ from a plain program's by a relative error of at most 0.012.
Values may be sent and summed in bfloat16 or wider, within the bound.
No kernel may reach another device: no remote copies, remote signals or barrier semaphores. Data moves between devices by JAX's collectives and lax.ppermute only.
A program may use at most 128 MiB of HBM per device.

v0:
```python
from functools import partial
import math

import jax
import jax.numpy as jnp
from jax import lax
from jax.experimental import pallas as pl
from jax.experimental.pallas import tpu as pltpu
from jax.sharding import PartitionSpec as P

FLOOR_SCORE = -1e30
CHUNKS = 4
LANES = 128


def attend_kernel(place, lengths, tasks, q_ref, *refs, spans, shard_rows, q_block, key_tile, pair):
    kv_refs = refs[: 2 * spans]
    out_ref, kv, acc, peak, total, q_split, sems = refs[2 * spans :]
    heads, rows, width = q_ref.shape
    units = heads // pair
    cols = pair * rows
    parity = place[0]
    copies = []
    for span in range(spans):
        for other in range(2):
            slot = 2 * span + (parity if other == 0 else 1 - parity)
            copy = pltpu.make_async_copy(
                kv_refs[2 * span + other], kv.at[slot], sems.at[2 * span + other]
            )
            copy.start()
            copies.append(copy)

    first_row = place[1]
    base = place[2]
    last_row = first_row + rows - 1
    one_head = first_row + lax.broadcasted_iota(jnp.int32, (1, rows), 1)
    begin = jnp.zeros((1, rows), jnp.int32)
    begin_first = jnp.int32(0)
    begin_last = jnp.int32(0)
    start = jnp.int32(0)
    for doc in range(lengths.shape[0]):
        begin = jnp.where(one_head >= start, jnp.maximum(begin, start), begin)
        begin_first = jnp.where(first_row >= start, jnp.maximum(begin_first, start), begin_first)
        begin_last = jnp.where(last_row >= start, jnp.maximum(begin_last, start), begin_last)
        start = start + lengths[doc]

    task = (first_row // q_block) * heads
    begins, ends = [], []
    low_least = low_most = high_least = high_most = None
    for head in range(heads):
        low = tasks[(task + head) * 5 + 2] * q_block
        high = tasks[(task + head) * 5 + 3] * q_block
        begins.append(jnp.maximum(begin, low))
        ends.append(jnp.minimum(one_head, high - 1))
        low_least = low if head == 0 else jnp.minimum(low_least, low)
        low_most = low if head == 0 else jnp.maximum(low_most, low)
        high_least = high if head == 0 else jnp.minimum(high_least, high)
        high_most = high if head == 0 else jnp.maximum(high_most, high)
    begins = [jnp.concatenate(begins[u * pair : (u + 1) * pair], axis=1) for u in range(units)]
    ends = [jnp.concatenate(ends[u * pair : (u + 1) * pair], axis=1) for u in range(units)]

    tiles = kv.shape[0] * shard_rows // key_tile
    lo = jnp.clip((jnp.maximum(low_least, begin_first) - base) // key_tile, 0, tiles)
    hi = jnp.clip(
        (jnp.minimum(high_most, last_row + 1) - base + key_tile - 1) // key_tile, lo, tiles
    )
    inner_lo = jnp.clip(
        (jnp.maximum(low_most, begin_last) - base + key_tile - 1) // key_tile, lo, hi
    )
    inner_hi = jnp.clip(
        (jnp.minimum(high_least, first_row + 1) - base) // key_tile, inner_lo, hi
    )

    acc[...] = jnp.zeros_like(acc)
    peak[...] = jnp.full_like(peak, FLOOR_SCORE)
    total[...] = jnp.zeros_like(total)
    factor = math.log2(math.e) / math.sqrt(width)
    for unit in range(units):
        scaled = q_ref[unit * pair : (unit + 1) * pair].reshape(cols, width).astype(jnp.float32)
        scaled = scaled * factor
        coarse = scaled.astype(jnp.bfloat16)
        q_split[unit, :, :width] = coarse
        q_split[unit, :, width:] = (scaled - coarse.astype(jnp.float32)).astype(jnp.bfloat16)
    for copy in copies:
        copy.wait()

    per_shard = shard_rows // key_tile

    def step(tile, masked):
        slot = tile // per_shard
        offset = pl.multiple_of((tile % per_shard) * key_tile, key_tile)
        keys = kv[slot, 0, pl.ds(offset, key_tile), :]
        keys = jnp.concatenate([keys, keys], axis=1)
        values = kv[slot, 1, pl.ds(offset, key_tile), :].T
        values = jnp.concatenate([values, jnp.ones((16, key_tile), jnp.bfloat16)], axis=0)
        key_pos = (
            base + tile * key_tile + lax.broadcasted_iota(jnp.int32, (key_tile, 1), 0)
            if masked
            else None
        )

        def scores_of(unit):
            return lax.dot_general(
                keys,
                q_split[unit],
                (((1,), (1,)), ((), ())),
                preferred_element_type=jnp.float32,
            )

        def weigh(unit, scores):
            if masked:
                visible = (key_pos >= begins[unit]) & (key_pos <= ends[unit])
                scores = jnp.where(visible, scores, FLOOR_SCORE)
            before = peak[unit]
            now = jnp.maximum(before, jnp.max(scores, axis=0, keepdims=True))
            peak[unit] = now
            return jnp.exp2(scores - now).astype(jnp.bfloat16), jnp.exp2(before - now)

        def gather(unit, weights, rescale):
            product = lax.dot_general(
                values, weights, (((1,), (0,)), ((), ())), preferred_element_type=jnp.float32
            )
            total[unit] = total[unit] * rescale + product[width : width + 1]
            acc[unit] = acc[unit] * rescale + product[:width]

        scores = scores_of(0)
        waiting = None
        for unit in range(units):
            ahead = scores_of(unit + 1) if unit + 1 < units else None
            weighed = weigh(unit, scores)
            if waiting is not None:
                gather(unit - 1, *waiting)
            waiting, scores = weighed, ahead
        gather(units - 1, *waiting)

    def inner(tile, carried):
        step(tile, False)
        return carried

    def edge(turn, carried):
        step(jnp.where(turn < inner_lo - lo, lo + turn, inner_hi + turn - (inner_lo - lo)), True)
        return carried

    lax.fori_loop(inner_lo, inner_hi, inner, 0)
    lax.fori_loop(0, (inner_lo - lo) + (hi - inner_hi), edge, 0)
    for unit in range(units):
        done = (acc[unit] / total[unit]).T.astype(jnp.bfloat16)
        for member in range(pair):
            head = unit * pair + member
            out_ref[:, head * width : (head + 1) * width] = done[member * rows : (member + 1) * rows]


def attend(place, lengths, tasks, queries, kvs, chunk, rows, q_block):
    heads, _, width = queries.shape
    _, shard_rows, _ = kvs[0].shape
    slots = len(kvs)
    pair = max(1, min(heads, 512 // rows))
    key_tile = min(512, shard_rows)
    units, cols = heads // pair, pair * rows
    return pl.pallas_call(
        partial(
            attend_kernel,
            spans=slots // 2,
            shard_rows=shard_rows,
            q_block=q_block,
            key_tile=key_tile,
            pair=pair,
        ),
        grid_spec=pltpu.PrefetchScalarGridSpec(
            num_scalar_prefetch=3,
            grid=(1,),
            in_specs=[pl.BlockSpec((heads, rows, width), lambda i, *_: (0, chunk, 0))]
            + [pl.BlockSpec(memory_space=pl.ANY)] * slots,
            out_specs=pl.BlockSpec((rows, heads * width), lambda i, *_: (0, 0)),
            scratch_shapes=[
                pltpu.VMEM((slots, 2, shard_rows, width), jnp.bfloat16),
                pltpu.VMEM((units, width, cols), jnp.float32),
                pltpu.VMEM((units, 1, cols), jnp.float32),
                pltpu.VMEM((units, 1, cols), jnp.float32),
                pltpu.VMEM((units, cols, 2 * width), jnp.bfloat16),
                pltpu.SemaphoreType.DMA((slots,)),
            ],
        ),
        out_shape=jax.ShapeDtypeStruct((rows, heads * width), jnp.bfloat16),
        compiler_params=pltpu.CompilerParams(vmem_limit_bytes=48 * 2**20),
        cost_estimate=pl.CostEstimate(
            flops=heads * rows * 4096 * width * 4,
            bytes_accessed=8 * 2**20,
            transcendentals=heads * rows * 4096,
        ),
    )(place, lengths, tasks, queries, *kvs)


def local(queries, keys, values, doc_lengths, tasks, w_out):
    heads, tok_dev, width = queries.shape
    n_tok = lax.axis_size("tok")
    n_head = lax.axis_size("head")
    me = lax.axis_index("tok")
    tokens = n_tok * tok_dev
    q_block = tokens * heads // tasks.shape[0]
    chips = n_tok // 2
    doc_most = tokens * 4 // doc_lengths.shape[0]
    back = min(chips - 1, -(-(doc_most - 1) // (2 * tok_dev)))

    own = jnp.concatenate([keys, values], axis=0)
    spans = []
    for hop in range(back, 0, -1):
        pairs = [(i, i + 2 * hop) for i in range(n_tok - 2 * hop)]
        spans.append(lax.ppermute(own, "tok", pairs))
    spans.append(own)

    z = lax.axis_index("head")
    out_cols = w_out.shape[1] // n_head
    flat_tasks = tasks.reshape(-1)
    rows = tok_dev // CHUNKS
    base = (me // 2 - back) * 2 * tok_dev

    def column(block):
        return lax.dynamic_slice_in_dim(w_out, block * out_cols, out_cols, 1)

    w_send = jnp.concatenate([column((z ^ 1) ^ 2), column(z ^ 1)], axis=1)
    w_keep = jnp.concatenate([column(z ^ 2), column(z)], axis=1)
    near = [(i, i ^ 1) for i in range(n_head)]
    far = [(i, i ^ 2) for i in range(n_head)]
    spans, w_send, w_keep, flat_tasks = lax.optimization_barrier(
        (spans, w_send, w_keep, flat_tasks)
    )
    swap = [(i, i ^ 1) for i in range(n_tok)]
    kvs = []
    for mine in spans:
        kvs += [mine, lax.ppermute(mine, "tok", swap)]

    def project(attended):
        sent = jnp.dot(attended, w_send, preferred_element_type=jnp.float32)
        return sent.astype(jnp.bfloat16)

    def hop(attended, arrived):
        kept = jnp.dot(attended, w_keep, preferred_element_type=jnp.float32)
        summed = kept + arrived.astype(jnp.float32)
        return summed[:, :out_cols].astype(jnp.bfloat16), summed[:, out_cols:]

    halves = []
    attended = sent = summed = None
    for chunk in range(CHUNKS):
        place = jnp.stack([me % 2, me * tok_dev + chunk * rows, base]).astype(jnp.int32)
        place, sent, summed = lax.optimization_barrier((place, sent, summed))
        arrived = None if sent is None else lax.ppermute(sent, "head", near)
        crossed = None if summed is None else lax.ppermute(summed[0], "head", far)
        ready = attend(place, doc_lengths, flat_tasks, queries, kvs, chunk, rows, q_block)
        sent, arrived, crossed = lax.optimization_barrier((project(ready), arrived, crossed))
        if crossed is not None:
            halves.append((summed[1], crossed))
        summed = None if arrived is None else hop(attended, arrived)
        attended = ready
    arrived = lax.ppermute(sent, "head", near)
    if summed is not None:
        halves.append((summed[1], lax.ppermute(summed[0], "head", far)))
    summed = hop(attended, arrived)
    halves.append((summed[1], lax.ppermute(summed[0], "head", far)))
    outs = [(held + crossed.astype(jnp.float32)).astype(jnp.bfloat16) for held, crossed in halves]
    return jnp.concatenate(outs, axis=0)


def solution(mesh):
    placed = (
        P("head", "tok", None),
        P("head", "tok", None),
        P("head", "tok", None),
        P(),
        P(),
        P("head", None),
    )
    return jax.shard_map(
        local, mesh=mesh, in_specs=placed, out_specs=P("tok", "head"), check_vma=False
    )
```

profile of v0, /device:TPU:5, one launch (start us, length us, event | category | flops | bytes accessed | tf_op | source)
XLA Modules:
  0.0 138.1 jit_solution(9764076824038374278)
XLA Ops:
  0.0 1.0 constant_dynamic-update-slice_fusion.1
  1.0 1.0 constant_dynamic-update-slice_fusion.refs_4_
  2.0 3.1 %collective-permute-start.1 = (bf16[2,1024,128]{2,1,0:T(8,128)(2,1)S(1)}, bf16[2,1024,128]{2,1,0:T(8,128)(2,1)S(1)}, u32[]{:S(2)}, u32[]{:S(2)}) collective-permute-start(bf16[2,1024,128]{2,1,0:T(8,128)(2,1)S(1)} %constant_dynamic-update-slice_fusion.refs_4_), channel_id=1, source_target_pairs={{0,8},{4,12},{8,16},{12,20},{16,24},{20,28},{1,9},{5,13},{9,17},{1... | collective-permute-start | bytes 1572872 | tf_op jit(solution)/shard_map/ppermute | solution.py:209
  5.1 1.3 collective-permute-start
  6.4 0.8 copy.7
  7.2 0.2 reshape.3.tasks
  7.4 2.5 %constant_dynamic-slice_fusion.1 = (bf16[1024,512]{1,0:T(8,128)(2,1)S(1)}, bf16[1024,512]{1,0:T(8,128)(2,1)S(1)}, bf16[1024,512]{1,0:T(8,128)(2,1)S(1)}, bf16[1024,512]{1,0:T(8,128)(2,1)S(1)}) fusion(bf16[1024,2048]{1,0:T(8,128)(2,1)} %param.11, s32[]{:T(128)S(6)} %select_n.33, s32[]{:T(128)S(6)} %select_n.32, s32[]{:T(128)S(6)} %select_n.31, s32[]{:T(128)S(6)} %select_n.34), kind=kLoop, calls=%fused_computation.24 | loop fusion | bytes 8388624 | tf_op jit(solution)/shard_map/dynamic_slice | solution.py:219
  9.9 2.6 %pad_maximum_fusion = (bf16[1024,1024]{1,0:T(8,128)(2,1)}, bf16[1024,1024]{1,0:T(8,128)(2,1)}) fusion(bf16[1024,512]{1,0:T(8,128)(2,1)S(1)} %get-tuple-element.54, bf16[1024,512]{1,0:T(8,128)(2,1)S(1)} %get-tuple-element.55, bf16[1024,512]{1,0:T(8,128)(2,1)S(1)} %get-tuple-element.56, bf16[1024,512]{1,0:T(8,128)(2,1)S(1)} %get-tuple-element.53), kind=kLoop, calls=%fused_computation | loop fusion | flops 8388608 | bytes 8388608 | tf_op jit(solution)/shard_map/concatenate | solution.py:221
  12.5 5.1 %collective-permute-done.1.refs_2_ = bf16[2,1024,128]{2,1,0:T(8,128)(2,1)S(1)} collective-permute-done((bf16[2,1024,128]{2,1,0:T(8,128)(2,1)S(1)}, bf16[2,1024,128]{2,1,0:T(8,128)(2,1)S(1)}, u32[]{:S(2)}, u32[]{:S(2)}) %collective-permute-start.1) | collective-permute-done | bytes 524320 | tf_op jit(solution)/shard_map/ppermute | solution.py:209
  17.6 12.3 %collective-permute-done.refs_0_ = bf16[2,1024,128]{2,1,0:T(8,128)(2,1)} collective-permute-done((bf16[2,1024,128]{2,1,0:T(8,128)(2,1)S(1)}, bf16[2,1024,128]{2,1,0:T(8,128)(2,1)}, u32[]{:S(2)}, u32[]{:S(2)}) %collective-permute-start) | collective-permute-done | bytes 524320 | tf_op jit(solution)/shard_map/ppermute | solution.py:209
  29.9 0.5 collective-permute-start.2
  30.4 0.0 collective-permute-start.3
  30.5 0.5 collective-permute-start.4
  30.9 0.1 add_add_fusion.2.place
  31.0 0.1 add_add_fusion.3.place
  31.1 0.1 add_add_fusion
  31.2 1.7 %collective-permute-done.2.refs_1_ = bf16[2,1024,128]{2,1,0:T(8,128)(2,1)} collective-permute-done((bf16[2,1024,128]{2,1,0:T(8,128)(2,1)}, bf16[2,1024,128]{2,1,0:T(8,128)(2,1)}, u32[]{:S(2)}, u32[]{:S(2)}) %collective-permute-start.2) | collective-permute-done | bytes 524320 | tf_op jit(solution)/shard_map/ppermute | solution.py:231
  32.9 0.7 collective-permute-done.4.refs_5_
  33.6 15.8 %shard_map.64 = bf16[256,1024]{1,0:T(8,128)(2,1)S(1)} custom-call(s32[3]{0:T(128)S(1)} %add_add_fusion.2.place, s32[8]{0:T(128)S(1)} %copy-done.1, s32[640]{0:T(1024)S(1)} %reshape.3.tasks, bf16[8,1024,128]{2,1,0:T(8,128)(2,1)S(1)} %copy-done, bf16[2,1024,128]{2,1,0:T(8,128)(2,1)} %collective-permute-done.refs_0_, ...), custom_call_target="tpu_custom_call" | custom-call | flops 4294967296 | bytes 8388608 | tf_op jit(solution)/shard_map/pallas_call | solution.py:160
  49.4 0.7 convolution_convert_fusion.3
  50.1 1.4 %collective-permute-start.5 = (bf16[256,1024]{1,0:T(8,128)(2,1)S(1)}, bf16[256,1024]{1,0:T(8,128)(2,1)S(1)}, u32[]{:S(2)}, u32[]{:S(2)}) collective-permute-start(bf16[256,1024]{1,0:T(8,128)(2,1)S(1)} %convolution_convert_fusion.3), channel_id=1, source_target_pairs={{0,1},{1,0},{2,3},{3,2},{4,5},{5,4},{6,7},{7,6},{8,9},{9,8},{10,11... | collective-permute-start | bytes 1572872 | tf_op jit(solution)/shard_map/ppermute | solution.py:247
  51.5 15.8 %shard_map.65 = bf16[256,1024]{1,0:T(8,128)(2,1)S(1)} custom-call(s32[3]{0:T(128)S(1)} %get-tuple-element.34.place, s32[8]{0:T(128)S(1)} %copy-done.1, s32[640]{0:T(1024)S(1)} %reshape.3.tasks, bf16[8,1024,128]{2,1,0:T(8,128)(2,1)S(1)} %copy-done, bf16[2,1024,128]{2,1,0:T(8,128)(2,1)} %collective-permute-done.refs_0_, ...), custom_call_target="tpu_custom_call" | custom-call | flops 4294967296 | bytes 8388608 | tf_op jit(solution)/shard_map/pallas_call | solution.py:160
  67.3 0.7 convolution_convert_fusion.2
  68.1 0.8 copy-done.2
  68.9 0.7 convolution_add_fusion.3
  69.7 2.4 %collective-permute-start.7 = (bf16[256,512]{1,0:T(8,128)(2,1)S(1)}, bf16[256,512]{1,0:T(8,128)(2,1)S(1)}, u32[]{:S(2)}, u32[]{:S(2)}) collective-permute-start(bf16[256,512]{1,0:T(8,128)(2,1)S(1)} %slice.57), channel_id=1, source_target_pairs={{0,2},{1,3},{2,0},{3,1},{4,6},{5,7},{6,4},{7,5},{8,10},{9,11},{10,... | collective-permute-start | bytes 786440 | tf_op jit(solution)/shard_map/ppermute | solution.py:248
  72.1 0.2 collective-permute-start.6
  72.3 20.5 %shard_map.66 = bf16[256,1024]{1,0:T(8,128)(2,1)S(1)} custom-call(s32[3]{0:T(128)S(1)} %get-tuple-element.40.place, s32[8]{0:T(128)S(1)} %copy-done.1, s32[640]{0:T(1024)S(1)} %reshape.3.tasks, bf16[8,1024,128]{2,1,0:T(8,128)(2,1)S(1)} %copy-done, bf16[2,1024,128]{2,1,0:T(8,128)(2,1)} %collective-permute-done.refs_0_, ...), custom_call_target="tpu_custom_call" | custom-call | flops 4294967296 | bytes 8388608 | tf_op jit(solution)/shard_map/pallas_call | solution.py:160
  92.8 0.7 convolution_convert_fusion.1
  93.5 0.7 convolution_add_fusion.2
  94.3 0.0 copy-start.4
  94.3 0.1 collective-permute-start.9
  94.5 1.3 collective-permute-start.8
  95.7 4.4 %shard_map.67 = bf16[256,1024]{1,0:T(8,128)(2,1)S(1)} custom-call(s32[3]{0:T(128)S(1)} %add_add_fusion.3.place, s32[8]{0:T(128)S(1)} %copy-done.1, s32[640]{0:T(1024)S(1)} %reshape.3.tasks, bf16[8,1024,128]{2,1,0:T(8,128)(2,1)S(1)} %copy-done, bf16[2,1024,128]{2,1,0:T(8,128)(2,1)} %collective-permute-done.refs_0_, ...), custom_call_target="tpu_custom_call" | custom-call | flops 4294967296 | bytes 8388608 | tf_op jit(solution)/shard_map/pallas_call | solution.py:160
  100.2 0.7 convolution_convert_fusion
  100.9 2.5 %collective-permute-done.9 = bf16[256,512]{1,0:T(8,128)(2,1)S(1)} collective-permute-done((bf16[256,512]{1,0:T(8,128)(2,1)S(1)}, bf16[256,512]{1,0:T(8,128)(2,1)S(1)}, u32[]{:S(2)}, u32[]{:S(2)}) %collective-permute-start.9) | collective-permute-done | bytes 262176 | tf_op jit(solution)/shard_map/ppermute | solution.py:248
  103.5 4.3 %collective-permute-done.8 = bf16[256,1024]{1,0:T(8,128)(2,1)S(1)} collective-permute-done((bf16[256,1024]{1,0:T(8,128)(2,1)S(1)}, bf16[256,1024]{1,0:T(8,128)(2,1)S(1)}, u32[]{:S(2)}, u32[]{:S(2)}) %collective-permute-start.8) | collective-permute-done | bytes 524320 | tf_op jit(solution)/shard_map/ppermute | solution.py:247
  107.7 0.1 add_convert_fusion.1
  107.8 0.7 convolution_add_fusion.1
  108.6 1.7 %collective-permute-start.10 = (bf16[256,512]{1,0:T(8,128)(2,1)S(1)}, bf16[256,512]{1,0:T(8,128)(2,1)S(1)}, u32[]{:S(2)}, u32[]{:S(2)}) collective-permute-start(bf16[256,512]{1,0:T(8,128)(2,1)S(1)} %slice.55), channel_id=1, source_target_pairs={{0,2},{1,3},{2,0},{3,1},{4,6},{5,7},{6,4},{7,5},{8,10},{9,11},{10,... | collective-permute-start | bytes 786440 | tf_op jit(solution)/shard_map/ppermute | solution.py:257
  110.3 12.3 %collective-permute-done.11 = bf16[256,1024]{1,0:T(8,128)(2,1)S(1)} collective-permute-done((bf16[256,1024]{1,0:T(8,128)(2,1)S(1)}, bf16[256,1024]{1,0:T(8,128)(2,1)S(1)}, u32[]{:S(2)}, u32[]{:S(2)}) %collective-permute-start.11) | collective-permute-done | bytes 524320 | tf_op jit(solution)/shard_map/ppermute | solution.py:255
  122.6 0.7 convolution_add_fusion
  123.4 1.1 collective-permute-start.12
  124.5 0.1 add_convert_fusion
  124.6 0.1 fusion.1
  124.7 12.2 %collective-permute-done.12 = bf16[256,512]{1,0:T(8,128)(2,1)S(1)} collective-permute-done((bf16[256,512]{1,0:T(8,128)(2,1)S(1)}, bf16[256,512]{1,0:T(8,128)(2,1)S(1)}, u32[]{:S(2)}, u32[]{:S(2)}) %collective-permute-start.12) | collective-permute-done | bytes 262176 | tf_op jit(solution)/shard_map/ppermute | solution.py:259
  136.9 0.1 fusion
  137.0 1.0 pad_maximum_fusion.2
  (24 shorter events, 0.2 us)
Async XLA Ops:
  2.0 15.6 %collective-permute-start.1 = (bf16[2,1024,128]{2,1,0:T(8,128)(2,1)S(1)}, bf16[2,1024,128]{2,1,0:T(8,128)(2,1)S(1)}, u32[]{:S(2)}, u32[]{:S(2)}) collective-permute-start(bf16[2,1024,128]{2,1,0:T(8,128)(2,1)S(1)} %constant_dynamic-update-slice_fusion.refs_4_), channel_id=1, source_target_pairs={{0,8},{4,12},{8,16},{12,20},{16,24},{20,28},{1,9},{5,13},{9,17},{1... | collective-permute-start | bytes 1572872 | tf_op jit(solution)/shard_map/ppermute | solution.py:209
  5.1 24.9 %collective-permute-start = (bf16[2,1024,128]{2,1,0:T(8,128)(2,1)S(1)}, bf16[2,1024,128]{2,1,0:T(8,128)(2,1)}, u32[]{:S(2)}, u32[]{:S(2)}) collective-permute-start(bf16[2,1024,128]{2,1,0:T(8,128)(2,1)S(1)} %constant_dynamic-update-slice_fusion.refs_4_), channel_id=1, source_target_pairs={{0,16},{4,20},{8,24},{12,28},{1,17},{5,21},{9,25},{13,29},{2,18},{... | collective-permute-start | bytes 1572872 | tf_op jit(solution)/shard_map/ppermute | solution.py:209
  9.9 23.7 %copy-start = (bf16[8,1024,128]{2,1,0:T(8,128)(2,1)S(1)}, bf16[8,1024,128]{2,1,0:T(8,128)(2,1)}, u32[]{:S(2)}) copy-start(bf16[8,1024,128]{2,1,0:T(8,128)(2,1)} %q_ref.7) | copy-start | bytes 6291460
  9.9 23.7 %copy-start.1 = (s32[8]{0:T(128)S(1)}, s32[8]{0:T(128)}, u32[]{:S(2)}) copy-start(s32[8]{0:T(128)} %lengths.7) | copy-start | bytes 100
  29.9 3.0 %collective-permute-start.2 = (bf16[2,1024,128]{2,1,0:T(8,128)(2,1)}, bf16[2,1024,128]{2,1,0:T(8,128)(2,1)}, u32[]{:S(2)}, u32[]{:S(2)}) collective-permute-start(bf16[2,1024,128]{2,1,0:T(8,128)(2,1)} %collective-permute-done.refs_0_), channel_id=1, source_target_pairs={{0,4},{4,0},{8,12},{12,8},{16,20},{20,16},{24,28},{28,24},{1,5},{5... | collective-permute-start | bytes 1572872 | tf_op jit(solution)/shard_map/ppermute | solution.py:231
  30.4 2.5 %collective-permute-start.3 = (bf16[2,1024,128]{2,1,0:T(8,128)(2,1)S(1)}, bf16[2,1024,128]{2,1,0:T(8,128)(2,1)}, u32[]{:S(2)}, u32[]{:S(2)}) collective-permute-start(bf16[2,1024,128]{2,1,0:T(8,128)(2,1)S(1)} %collective-permute-done.1.refs_2_), channel_id=1, source_target_pairs={{0,4},{4,0},{8,12},{12,8},{16,20},{20,16},{24,28},{28,24},{1,5},{5... | collective-permute-start | bytes 1572872 | tf_op jit(solution)/shard_map/ppermute | solution.py:231
  30.5 3.2 %collective-permute-start.4 = (bf16[2,1024,128]{2,1,0:T(8,128)(2,1)S(1)}, bf16[2,1024,128]{2,1,0:T(8,128)(2,1)}, u32[]{:S(2)}, u32[]{:S(2)}) collective-permute-start(bf16[2,1024,128]{2,1,0:T(8,128)(2,1)S(1)} %constant_dynamic-update-slice_fusion.refs_4_), channel_id=1, source_target_pairs={{0,4},{4,0},{8,12},{12,8},{16,20},{20,16},{24,28},{28,24},{1,5},{5... | collective-permute-start | bytes 1572872 | tf_op jit(solution)/shard_map/ppermute | solution.py:231
  31.2 18.2 %copy-start.5 = (bf16[1024,1024]{1,0:T(8,128)(2,1)S(1)}, bf16[1024,1024]{1,0:T(8,128)(2,1)}, u32[]{:S(2)}) copy-start(bf16[1024,1024]{1,0:T(8,128)(2,1)} %get-tuple-element.33) | copy-start | bytes 6291460
  50.1 18.0 %collective-permute-start.5 = (bf16[256,1024]{1,0:T(8,128)(2,1)S(1)}, bf16[256,1024]{1,0:T(8,128)(2,1)S(1)}, u32[]{:S(2)}, u32[]{:S(2)}) collective-permute-start(bf16[256,1024]{1,0:T(8,128)(2,1)S(1)} %convolution_convert_fusion.3), channel_id=1, source_target_pairs={{0,1},{1,0},{2,3},{3,2},{4,5},{5,4},{6,7},{7,6},{8,9},{9,8},{10,11... | collective-permute-start | bytes 1572872 | tf_op jit(solution)/shard_map/ppermute | solution.py:247
  67.3 1.6 %copy-start.2 = (bf16[1024,1024]{1,0:T(8,128)(2,1)S(1)}, bf16[1024,1024]{1,0:T(8,128)(2,1)}, u32[]{:S(2)}) copy-start(bf16[1024,1024]{1,0:T(8,128)(2,1)} %get-tuple-element.37) | copy-start | bytes 6291460
  69.7 23.1 %copy-start.3 = (f32[256,1024]{1,0:T(8,128)}, f32[256,1024]{1,0:T(8,128)S(1)}, u32[]{:S(2)}) copy-start(f32[256,1024]{1,0:T(8,128)S(1)} %convolution_add_fusion.3) | copy-start | bytes 3145732
  69.7 23.8 %collective-permute-start.7 = (bf16[256,512]{1,0:T(8,128)(2,1)S(1)}, bf16[256,512]{1,0:T(8,128)(2,1)S(1)}, u32[]{:S(2)}, u32[]{:S(2)}) collective-permute-start(bf16[256,512]{1,0:T(8,128)(2,1)S(1)} %slice.57), channel_id=1, source_target_pairs={{0,2},{1,3},{2,0},{3,1},{4,6},{5,7},{6,4},{7,5},{8,10},{9,11},{10,... | collective-permute-start | bytes 786440 | tf_op jit(solution)/shard_map/ppermute | solution.py:248
  72.1 21.4 %collective-permute-start.6 = (bf16[256,1024]{1,0:T(8,128)(2,1)S(1)}, bf16[256,1024]{1,0:T(8,128)(2,1)S(1)}, u32[]{:S(2)}, u32[]{:S(2)}) collective-permute-start(bf16[256,1024]{1,0:T(8,128)(2,1)S(1)} %convolution_convert_fusion.2), channel_id=1, source_target_pairs={{0,1},{1,0},{2,3},{3,2},{4,5},{5,4},{6,7},{7,6},{8,9},{9,8},{10,11... | collective-permute-start | bytes 1572872 | tf_op jit(solution)/shard_map/ppermute | solution.py:247
  94.3 5.9 %copy-start.4 = (f32[256,1024]{1,0:T(8,128)}, f32[256,1024]{1,0:T(8,128)S(1)}, u32[]{:S(2)}) copy-start(f32[256,1024]{1,0:T(8,128)S(1)} %convolution_add_fusion.2) | copy-start | bytes 3145732
  94.3 9.1 %collective-permute-start.9 = (bf16[256,512]{1,0:T(8,128)(2,1)S(1)}, bf16[256,512]{1,0:T(8,128)(2,1)S(1)}, u32[]{:S(2)}, u32[]{:S(2)}) collective-permute-start(bf16[256,512]{1,0:T(8,128)(2,1)S(1)} %slice.56), channel_id=1, source_target_pairs={{0,2},{1,3},{2,0},{3,1},{4,6},{5,7},{6,4},{7,5},{8,10},{9,11},{10,... | collective-permute-start | bytes 786440 | tf_op jit(solution)/shard_map/ppermute | solution.py:248
  94.5 13.3 %collective-permute-start.8 = (bf16[256,1024]{1,0:T(8,128)(2,1)S(1)}, bf16[256,1024]{1,0:T(8,128)(2,1)S(1)}, u32[]{:S(2)}, u32[]{:S(2)}) collective-permute-start(bf16[256,1024]{1,0:T(8,128)(2,1)S(1)} %convolution_convert_fusion.1), channel_id=1, source_target_pairs={{0,1},{1,0},{2,3},{3,2},{4,5},{5,4},{6,7},{7,6},{8,9},{9,8},{10,11... | collective-permute-start | bytes 1572872 | tf_op jit(solution)/shard_map/ppermute | solution.py:247
  100.2 7.6 %slice-start = ((f32[256,1024]{1,0:T(8,128)}), f32[256,512]{1,0:T(8,128)S(1)}, s32[]{:S(2)}) async-start(f32[256,1024]{1,0:T(8,128)} %copy-done.3), calls=%async_computation | async-start | bytes 1048576 | tf_op jit(solution)/shard_map/slice | solution.py:240
  107.7 14.9 %collective-permute-start.11 = (bf16[256,1024]{1,0:T(8,128)(2,1)S(1)}, bf16[256,1024]{1,0:T(8,128)(2,1)S(1)}, u32[]{:S(2)}, u32[]{:S(2)}) collective-permute-start(bf16[256,1024]{1,0:T(8,128)(2,1)S(1)} %convolution_convert_fusion), channel_id=1, source_target_pairs={{0,1},{1,0},{2,3},{3,2},{4,5},{5,4},{6,7},{7,6},{8,9},{9,8},{10,11... | collective-permute-start | bytes 1572872 | tf_op jit(solution)/shard_map/ppermute | solution.py:255
  108.6 15.9 %slice-start.1 = ((f32[256,1024]{1,0:T(8,128)}), f32[256,512]{1,0:T(8,128)S(1)}, s32[]{:S(2)}) async-start(f32[256,1024]{1,0:T(8,128)} %copy-done.4), calls=%async_computation.1 | async-start | bytes 1048576 | tf_op jit(solution)/shard_map/slice | solution.py:240
  108.6 16.0 %collective-permute-start.10 = (bf16[256,512]{1,0:T(8,128)(2,1)S(1)}, bf16[256,512]{1,0:T(8,128)(2,1)S(1)}, u32[]{:S(2)}, u32[]{:S(2)}) collective-permute-start(bf16[256,512]{1,0:T(8,128)(2,1)S(1)} %slice.55), channel_id=1, source_target_pairs={{0,2},{1,3},{2,0},{3,1},{4,6},{5,7},{6,4},{7,5},{8,10},{9,11},{10,... | collective-permute-start | bytes 786440 | tf_op jit(solution)/shard_map/ppermute | solution.py:257
  123.4 13.5 %collective-permute-start.12 = (bf16[256,512]{1,0:T(8,128)(2,1)S(1)}, bf16[256,512]{1,0:T(8,128)(2,1)S(1)}, u32[]{:S(2)}, u32[]{:S(2)}) collective-permute-start(bf16[256,512]{1,0:T(8,128)(2,1)S(1)} %slice.54), channel_id=1, source_target_pairs={{0,2},{1,3},{2,0},{3,1},{4,6},{5,7},{6,4},{7,5},{8,10},{9,11},{10,... | collective-permute-start | bytes 786440 | tf_op jit(solution)/shard_map/ppermute | solution.py:259
where the time goes:
time: 137 us; the launch traced here: 138 us
  Pallas kernels  56.5 us (41%)
  waiting for transfers between devices  51.2 us (37%)
  starting transfers between devices  13.6 us (10%)
  local copies, waits for them, and re-layouts  6.45 us (5%)
  matrix products  5.8 us (4%)
  other arithmetic  4.18 us (3%)
    pallas_call x4, Pallas kernels, attend(): pl.pallas_call(partial(attend_kernel, spans=slots // 2, shard_rows=shard_...  56.5 us
    ppermute x2, waiting for transfers between devices, local(): spans.append(lax.ppermute(own, 'tok', pairs))  17.4 us
    ppermute x1, waiting for transfers between devices, local(): arrived = lax.ppermute(sent, 'head', near)  12.3 us
    ppermute x2, waiting for transfers between devices, local(): halves.append((summed[1], lax.ppermute(summed[0], 'head', far)))  12.3 us
    ppermute x2, starting transfers between devices, local(): spans.append(lax.ppermute(own, 'tok', pairs))  4.41 us
    ppermute x3, waiting for transfers between devices, local(): arrived = None if sent is None else lax.ppermute(sent, 'head', near)  4.28 us
    dot_general x4, matrix products, hop(): kept = jnp.dot(attended, w_keep, preferred_element_type=jnp.float32)  2.93 us
    dot_general x4, matrix products, project(): sent = jnp.dot(attended, w_send, preferred_element_type=jnp.float32)  2.87 us
  transfers between devices with their start and end apart: 13, of which 8 were waited for; matrix products, arithmetic and copies ran while one was open for 7% of the time, Pallas kernels for 29%

commit v1 on v0

v1 whole, which is shorter than its diff:
```python
from functools import partial
import math

import jax
import jax.numpy as jnp
from jax import lax
from jax.experimental import pallas as pl
from jax.experimental.pallas import tpu as pltpu
from jax.sharding import PartitionSpec as P

FLOOR_SCORE = -1e30
CHUNKS = 4
SAFE_TOTAL = 2.0**100
KEY_TILE = 512
EDGE_TILE = 256


def attend_kernel(place, lengths, tasks, q_ref, *refs, spans, shard_rows, q_block, key_tile, edge_tile, pair, resume, suspend):
    key_refs, value_refs, refs = refs[: 2 * spans], refs[2 * spans : 4 * spans], refs[4 * spans :]
    states, refs = (refs[:3], refs[3:]) if resume else (None, refs)
    outs, refs = (refs[:3], refs[3:]) if suspend else (refs[:1], refs[1:])
    key_all, value_all, acc, peak, total, s_buf, p_buf, rescale_buf, sems = refs
    heads, rows, width = q_ref.shape
    units = heads // pair
    cols = pair * rows
    parity = place[0]
    copies = []

    for span in range(spans):
        for other in range(2):
            at = 2 * span + other
            slot = 2 * span + (parity if other == 0 else 1 - parity)
            copies.append(pltpu.make_async_copy(key_refs[at], key_all.at[slot], sems.at[2 * at]))
            copies.append(
                pltpu.make_async_copy(value_refs[at], value_all.at[slot], sems.at[2 * at + 1])
            )

    def fetch():
        for copy in copies:
            copy.start()

    if suspend:
        pl.when(pl.program_id(0) == 0)(fetch)
    else:
        fetch()

    first_row = place[1] + pl.program_id(0) * rows
    base = place[2]
    last_row = first_row + rows - 1
    one_head = first_row + lax.broadcasted_iota(jnp.int32, (1, rows), 1)
    begin = jnp.zeros((1, rows), jnp.int32)
    begin_first = jnp.int32(0)
    begin_last = jnp.int32(0)
    start = jnp.int32(0)
    for doc in range(lengths.shape[0]):
        begin = jnp.where(one_head >= start, jnp.maximum(begin, start), begin)
        begin_first = jnp.where(first_row >= start, jnp.maximum(begin_first, start), begin_first)
        begin_last = jnp.where(last_row >= start, jnp.maximum(begin_last, start), begin_last)
        start = start + lengths[doc]

    task = (first_row // q_block) * heads
    begins, ends = [], []
    low_least = low_most = high_least = high_most = None
    for head in range(heads):
        low = tasks[(task + head) * 5 + 2] * q_block
        high = tasks[(task + head) * 5 + 3] * q_block
        begins.append(jnp.maximum(begin, low))
        ends.append(jnp.minimum(one_head, high - 1))
        low_least = low if head == 0 else jnp.minimum(low_least, low)
        low_most = low if head == 0 else jnp.maximum(low_most, low)
        high_least = high if head == 0 else jnp.minimum(high_least, high)
        high_most = high if head == 0 else jnp.maximum(high_most, high)
    begins = [jnp.concatenate(begins[u * pair : (u + 1) * pair], axis=1) for u in range(units)]
    ends = [jnp.concatenate(ends[u * pair : (u + 1) * pair], axis=1) for u in range(units)]

    ratio = key_tile // edge_tile
    tiles = 2 * spans * shard_rows // edge_tile
    lo = jnp.clip((jnp.maximum(low_least, begin_first) - base) // edge_tile, 0, tiles)
    hi = jnp.clip(
        (jnp.minimum(high_most, last_row + 1) - base + edge_tile - 1) // edge_tile, lo, tiles
    )
    full_lo = (jnp.maximum(low_most, begin_last) - base + key_tile - 1) // key_tile
    full_hi = (jnp.minimum(high_least, first_row + 1) - base) // key_tile
    full_lo = jnp.clip(full_lo, 0, tiles // ratio)
    full_hi = jnp.minimum(full_hi, tiles // ratio)
    some = full_hi > full_lo
    inner_lo = jnp.where(some, full_lo * ratio, lo)
    inner_hi = jnp.where(some, full_hi * ratio, lo)

    def reset():
        if resume:
            acc[...] = states[0][...].reshape(acc.shape)
            peak[...] = states[1][...].reshape(peak.shape)
            total[...] = states[2][...].reshape(total.shape)
        else:
            acc[...] = jnp.zeros_like(acc)
            peak[...] = jnp.full_like(peak, FLOOR_SCORE)
            total[...] = jnp.zeros_like(total)

    reset()
    factor = math.log2(math.e) / math.sqrt(width)

    def wait():
        for copy in copies:
            copy.wait()

    if suspend:
        pl.when(pl.program_id(0) == 0)(wait)
    else:
        wait()

    def sweep(count, tile_of, size, masked, fixed):
        per_shard = shard_rows // size

        def keys_of(tile):
            offset = pl.multiple_of((tile % per_shard) * size, size)
            return key_all[tile // per_shard, pl.ds(offset, size), :]

        def values_of(tile):
            offset = pl.multiple_of((tile % per_shard) * size, size)
            values = value_all[tile // per_shard, :, pl.ds(offset, size)]
            return jnp.concatenate([values, jnp.ones((16, size), jnp.bfloat16)], axis=0)

        def scores_of(keys, unit):
            return lax.dot_general(
                keys,
                q_ref[unit * pair : (unit + 1) * pair].reshape(cols, width),
                (((1,), (1,)), ((), ())),
                preferred_element_type=jnp.float32,
            )

        def gather(values, unit, weights, rescale):
            product = lax.dot_general(
                values, weights, (((1,), (0,)), ((), ())), preferred_element_type=jnp.float32
            )
            if fixed:
                total[unit] += product[width : width + 1]
                acc[unit] += product[:width]
            else:
                total[unit] = total[unit] * rescale + product[width : width + 1]
                acc[unit] = acc[unit] * rescale + product[:width]

        def step(turn, carried):
            tile = tile_of(turn)
            keys, values = keys_of(tile), values_of(tile)
            key_pos = (
                base + tile * size + lax.broadcasted_iota(jnp.int32, (size, 1), 0)
                if masked
                else None
            )
            scores = s_buf[:size]
            waiting = None
            for unit in range(units):
                if unit + 1 < units:
                    ahead = scores_of(keys, unit + 1)
                else:
                    ahead = scores_of(keys_of(tile_of(jnp.minimum(turn + 1, count - 1))), 0)
                if masked:
                    visible = (key_pos >= begins[unit]) & (key_pos <= ends[unit])
                    scores = jnp.where(visible, scores, FLOOR_SCORE)
                before = peak[unit]
                if fixed:
                    now, rescale = before, None
                else:
                    now = jnp.maximum(before, jnp.max(scores, axis=0, keepdims=True) * factor)
                    peak[unit] = now
                    rescale = jnp.exp2(before - now)
                weights = jnp.exp2(scores * factor - now).astype(jnp.bfloat16)
                if waiting is not None:
                    gather(values, unit - 1, *waiting)
                else:
                    earlier = values_of(tile_of(jnp.maximum(turn - 1, 0)))
                    gather(earlier, units - 1, p_buf[:size], rescale_buf[...])
                waiting = weights, rescale
                scores = ahead
            s_buf[:size] = scores
            p_buf[:size] = waiting[0]
            if not fixed:
                rescale_buf[...] = waiting[1]
            return carried

        def whole():
            p_buf[:size] = jnp.zeros((size, cols), jnp.bfloat16)
            rescale_buf[...] = jnp.ones_like(rescale_buf)
            s_buf[:size] = scores_of(keys_of(tile_of(0)), 0)
            lax.fori_loop(0, count, step, 0)
            gather(values_of(tile_of(count - 1)), units - 1, p_buf[:size], rescale_buf[...])

        pl.when(count > 0)(whole)

    sweep(
        (inner_hi - inner_lo) // ratio,
        lambda turn: inner_lo // ratio + turn,
        key_tile,
        False,
        resume,
    )
    left = inner_lo - lo
    sweep(
        left + hi - inner_hi,
        lambda turn: jnp.where(turn < left, lo + turn, inner_hi + turn - left),
        edge_tile,
        True,
        resume,
    )
    if resume:
        in_range = jnp.min(jnp.where(total[...] < SAFE_TOTAL, 1.0, 0.0))

        @pl.when(in_range < 0.5)
        def again():
            reset()
            sweep(hi - lo, lambda turn: lo + turn, edge_tile, True, False)

    if suspend:
        outs[0][...] = acc[...].reshape(outs[0].shape)
        outs[1][...] = peak[...].reshape(outs[1].shape)
        outs[2][...] = total[...].reshape(outs[2].shape)
        return
    for unit in range(units):
        done = (acc[unit] / total[unit]).T.astype(jnp.bfloat16)
        for member in range(pair):
            head = unit * pair + member
            outs[0][:, head * width : (head + 1) * width] = done[member * rows : (member + 1) * rows]


def attend(place, lengths, tasks, queries, kvs, chunk, rows, q_block, states=None, suspend=False):
    heads, tok_dev, width = queries.shape
    shard_rows = kvs[0][0].shape[0]
    slots = len(kvs)
    pair = max(1, min(heads, 512 // rows))
    key_tile = min(KEY_TILE, shard_rows)
    edge_tile = min(EDGE_TILE, key_tile)
    units, cols = heads // pair, pair * rows
    state_shapes = [(units, width, cols), (units, 1, cols), (units, 1, cols)]

    def at_chunk(shape):
        return pl.BlockSpec((1,) + shape, lambda i, *_: (chunk + i, 0, 0, 0))

    in_specs = [pl.BlockSpec((heads, rows, width), lambda i, *_: (0, chunk + i, 0))]
    in_specs += [pl.BlockSpec(memory_space=pl.ANY)] * (2 * slots)
    if states is not None:
        in_specs += [at_chunk(shape) for shape in state_shapes]
    steps = tok_dev // rows if suspend else 1
    if suspend:
        out_specs = [at_chunk(shape) for shape in state_shapes]
        out_shape = [jax.ShapeDtypeStruct((steps,) + shape, jnp.float32) for shape in state_shapes]
    else:
        out_specs = pl.BlockSpec((rows, heads * width), lambda i, *_: (0, 0))
        out_shape = jax.ShapeDtypeStruct((rows, heads * width), jnp.bfloat16)
    return pl.pallas_call(
        partial(
            attend_kernel,
            spans=slots // 2,
            shard_rows=shard_rows,
            q_block=q_block,
            key_tile=key_tile,
            edge_tile=edge_tile,
            pair=pair,
            resume=states is not None,
            suspend=suspend,
        ),
        grid_spec=pltpu.PrefetchScalarGridSpec(
            num_scalar_prefetch=3,
            grid=(steps,),
            in_specs=in_specs,
            out_specs=out_specs,
            scratch_shapes=[
                pltpu.VMEM((slots, shard_rows, width), jnp.bfloat16),
                pltpu.VMEM((slots, width, shard_rows), jnp.bfloat16),
                pltpu.VMEM((units, width, cols), jnp.float32),
                pltpu.VMEM((units, 1, cols), jnp.float32),
                pltpu.VMEM((units, 1, cols), jnp.float32),
                pltpu.VMEM((key_tile, cols), jnp.float32),
                pltpu.VMEM((key_tile, cols), jnp.bfloat16),
                pltpu.VMEM((1, cols), jnp.float32),
                pltpu.SemaphoreType.DMA((2 * slots,)),
            ],
        ),
        out_shape=out_shape,
        compiler_params=pltpu.CompilerParams(vmem_limit_bytes=48 * 2**20),
        cost_estimate=pl.CostEstimate(
            flops=heads * rows * 4096 * width * 4,
            bytes_accessed=8 * 2**20,
            transcendentals=heads * rows * 4096,
        ),
    )(place, lengths, tasks, queries, *[k for k, _ in kvs], *[v for _, v in kvs], *(states or ()))


def local(queries, keys, values, doc_lengths, tasks, w_out):
    heads, tok_dev, width = queries.shape
    n_tok = lax.axis_size("tok")
    n_head = lax.axis_size("head")
    me = lax.axis_index("tok")
    tokens = n_tok * tok_dev
    q_block = tokens * heads // tasks.shape[0]
    chips = n_tok // 2
    doc_most = tokens * 4 // doc_lengths.shape[0]
    back = min(chips - 1, -(-(doc_most - 1) // (2 * tok_dev)))

    own = keys[0], values[0].T
    spans = []
    for hop in range(back, 0, -1):
        pairs = [(i, i + 2 * hop) for i in range(n_tok - 2 * hop)]
        spans.append(tuple(lax.ppermute(part, "tok", pairs) for part in own))
    swap = [(i, i ^ 1) for i in range(n_tok)]
    beside = [own, tuple(lax.ppermute(part, "tok", swap) for part in own)]

    z = lax.axis_index("head")
    out_cols = w_out.shape[1] // n_head
    flat_tasks = tasks.reshape(-1)
    rows = tok_dev // CHUNKS
    base = (me // 2 - back) * 2 * tok_dev

    def column(block):
        return lax.dynamic_slice_in_dim(w_out, block * out_cols, out_cols, 1)

    w_send = jnp.concatenate([column((z ^ 1) ^ 2), column(z ^ 1)], axis=1)
    w_keep = jnp.concatenate([column(z ^ 2), column(z)], axis=1)
    near = [(i, i ^ 1) for i in range(n_head)]
    far = [(i, i ^ 2) for i in range(n_head)]
    w_send, w_keep, flat_tasks, beside = lax.optimization_barrier(
        (w_send, w_keep, flat_tasks, beside)
    )
    chip_start = (me // 2) * 2 * tok_dev
    place = jnp.stack([me % 2, me * tok_dev, chip_start]).astype(jnp.int32)
    states = attend(
        place, doc_lengths, flat_tasks, queries, beside, 0, rows, q_block, suspend=True
    )
    spans, states = lax.optimization_barrier((spans, states))
    kvs = []
    for mine in spans:
        kvs += [mine, tuple(lax.ppermute(part, "tok", swap) for part in mine)]

    def project(attended):
        sent = jnp.dot(attended, w_send, preferred_element_type=jnp.float32)
        return sent.astype(jnp.bfloat16)

    def hop(attended, arrived):
        kept = jnp.dot(attended, w_keep, preferred_element_type=jnp.float32)
        summed = kept + arrived.astype(jnp.float32)
        return summed[:, :out_cols].astype(jnp.bfloat16), summed[:, out_cols:]

    halves = []
    attended = sent = summed = None
    for chunk in range(CHUNKS):
        place = jnp.stack([me % 2, me * tok_dev + chunk * rows, base]).astype(jnp.int32)
        place, sent, summed = lax.optimization_barrier((place, sent, summed))
        arrived = None if sent is None else lax.ppermute(sent, "head", near)
        crossed = None if summed is None else lax.ppermute(summed[0], "head", far)
        ready = attend(place, doc_lengths, flat_tasks, queries, kvs, chunk, rows, q_block, states)
        sent, arrived, crossed = lax.optimization_barrier((project(ready), arrived, crossed))
        if crossed is not None:
            halves.append((summed[1], crossed))
        summed = None if arrived is None else hop(attended, arrived)
        attended = ready
    arrived = lax.ppermute(sent, "head", near)
    if summed is not None:
        halves.append((summed[1], lax.ppermute(summed[0], "head", far)))
    summed = hop(attended, arrived)
    halves.append((summed[1], lax.ppermute(summed[0], "head", far)))
    outs = [(held + crossed.astype(jnp.float32)).astype(jnp.bfloat16) for held, crossed in halves]
    return jnp.concatenate(outs, axis=0)


def solution(mesh):
    placed = (
        P("head", "tok", None),
        P("head", "tok", None),
        P("head", "tok", None),
        P(),
        P(),
        P("head", None),
    )
    return jax.shard_map(
        local, mesh=mesh, in_specs=placed, out_specs=P("tok", "head"), check_vma=False
    )
```

time: 137 us -> 148 us (1.080)
  Pallas kernels: 56.5 us -> 73.2 us
  waiting for transfers between devices: 51.2 us -> 39 us
  starting transfers between devices: 13.6 us -> 19.5 us
  other arithmetic: 4.18 us -> 6.48 us
    ppermute x5 -> x10, waiting for transfers between devices: 19.8 us -> 1.63 us  [the longest x4 1.61 us: local(): kvs += [mine, tuple((lax.ppermute(part, 'tok', swap) for part in mine))]]
    pallas_call x4 -> x5, Pallas kernels: 56.5 us -> 73.2 us  [attend(): pl.pallas_call(partial(attend_kernel, spans=slots // 2, shard_rows=shard_...]
    ppermute x3, waiting for transfers between devices: 4.28 us -> 9.31 us  [local(): arrived = None if sent is None else lax.ppermute(sent, 'head', near)]
    ppermute x5 -> x10, starting transfers between devices: 5.42 us -> 9.8 us  [the longest x4 7.61 us: local(): spans.append(tuple((lax.ppermute(part, 'tok', pairs) for part in own)))]
    ppermute x2, waiting for transfers between devices: 2.55 us -> 0.01 us  [local(): crossed = None if summed is None else lax.ppermute(summed[0], 'head', far)]
    concatenate x1, other arithmetic: 2.6 us -> 4.91 us  [local(): w_send = jnp.concatenate([column(z ^ 1 ^ 2), column(z ^ 1)], axis=1)]
    ppermute x1, waiting for transfers between devices: 12.3 us -> 14.6 us  [local(): arrived = lax.ppermute(sent, 'head', near)]
    dynamic_slice x1, local copies, waits for them, and re-layouts: 2.48 us -> 4.31 us  [column(): return lax.dynamic_slice_in_dim(w_out, block * out_cols, out_cols, 1)]
  transfers between devices with their start and end apart: 13 -> 18, of which waited for: 8 -> 9; matrix products, arithmetic and copies ran while one was open for 7% -> 9% of each run, Pallas kernels for 29% -> 42%
where the time goes in v1:
time: 148 us; the launch traced here: 150 us
  Pallas kernels  73.2 us (49%)
  waiting for transfers between devices  39 us (26%)
  starting transfers between devices  19.5 us (13%)
  other arithmetic  6.48 us (4%)
  local copies, waits for them, and re-layouts  5.9 us (4%)
  matrix products  5.78 us (4%)
    pallas_call x5, Pallas kernels, attend(): pl.pallas_call(partial(attend_kernel, spans=slots // 2, shard_rows=shard_...  73.2 us
    ppermute x1, waiting for transfers between devices, local(): arrived = lax.ppermute(sent, 'head', near)  14.6 us
    ppermute x2, waiting for transfers between devices, local(): halves.append((summed[1], lax.ppermute(summed[0], 'head', far)))  13.4 us
    ppermute x3, waiting for transfers between devices, local(): arrived = None if sent is None else lax.ppermute(sent, 'head', near)  9.31 us
    ppermute x4, starting transfers between devices, local(): spans.append(tuple((lax.ppermute(part, 'tok', pairs) for part in own)))  7.61 us
    concatenate x1, other arithmetic, local(): w_send = jnp.concatenate([column(z ^ 1 ^ 2), column(z ^ 1)], axis=1)  4.91 us
    dynamic_slice x1, local copies, waits for them, and re-layouts, column(): return lax.dynamic_slice_in_dim(w_out, block * out_cols, out_cols, 1)  4.31 us
    ppermute x2, starting transfers between devices, local(): crossed = None if summed is None else lax.ppermute(summed[0], 'head', far)  3.82 us
  transfers between devices with their start and end apart: 18, of which 9 were waited for; matrix products, arithmetic and copies ran while one was open for 9% of the time, Pallas kernels for 42%

profile of v1, /device:TPU:5, one launch (start us, length us, event | category | flops | bytes accessed | tf_op | source)
XLA Modules:
  0.0 150.2 jit_solution(3434189232997957597)
XLA Ops:
  0.0 1.1 copy.9
  1.1 3.1 %collective-permute-start.5 = (bf16[128,1024]{1,0:T(8,128)(2,1)S(1)}, bf16[128,1024]{1,0:T(8,128)(2,1)S(1)}, u32[]{:S(2)}, u32[]{:S(2)}) collective-permute-start(bf16[128,1024]{1,0:T(8,128)(2,1)S(1)} %bitcast.27), channel_id=1, source_target_pairs={{0,8},{4,12},{8,16},{12,20},{16,24},{20,28},{1,9},{5,13},{9,17},{1... | collective-permute-start | bytes 786440 | tf_op jit(solution)/shard_map/ppermute | solution.py:304
  4.2 1.3 collective-permute-start.3
  5.5 1.0 collective-permute-start.1
  6.5 1.9 %collective-permute-start.4 = (bf16[1024,128]{1,0:T(8,128)(2,1)}, bf16[1024,128]{1,0:T(8,128)(2,1)S(1)}, u32[]{:S(2)}, u32[]{:S(2)}) collective-permute-start(bf16[1024,128]{1,0:T(8,128)(2,1)} %bitcast.31), channel_id=1, source_target_pairs={{0,8},{4,12},{8,16},{12,20},{16,24},{20,28},{1,9},{5,13},{9,17},{1... | collective-permute-start | bytes 786440 | tf_op jit(solution)/shard_map/ppermute | solution.py:304
  8.5 0.1 collective-permute-start
  8.6 4.3 %constant_dynamic-slice_fusion.1 = (bf16[1024,512]{1,0:T(8,128)(2,1)}, bf16[1024,512]{1,0:T(8,128)(2,1)}, bf16[1024,512]{1,0:T(8,128)(2,1)}, bf16[1024,512]{1,0:T(8,128)(2,1)}) fusion(bf16[1024,2048]{1,0:T(8,128)(2,1)} %param.11, s32[]{:T(128)S(6)} %select_n.36, s32[]{:T(128)S(6)} %select_n.35, s32[]{:T(128)S(6)} %select_n.34, s32[]{:T(128)S(6)} %select_n.37), kind=kLoop, calls=%fused_computation.22 | loop fusion | bytes 8388624 | tf_op jit(solution)/shard_map/dynamic_slice | solution.py:315
  12.9 0.1 pad_add_fusion.1
  13.0 0.1 copy.8
  13.1 0.2 reshape.3.tasks
  13.3 4.9 %pad_maximum_fusion = (bf16[1024,1024]{1,0:T(8,128)(2,1)}, bf16[1024,1024]{1,0:T(8,128)(2,1)}) fusion(bf16[1024,512]{1,0:T(8,128)(2,1)} %get-tuple-element.76, bf16[1024,512]{1,0:T(8,128)(2,1)} %get-tuple-element.77, bf16[1024,512]{1,0:T(8,128)(2,1)} %get-tuple-element.78, bf16[1024,512]{1,0:T(8,128)(2,1)} %get-tuple-element.75), kind=kLoop, calls=%fused_computation | loop fusion | flops 8388608 | bytes 8388608 | tf_op jit(solution)/shard_map/concatenate | solution.py:317
  18.3 1.3 collective-permute-start.2
  19.6 31.1 %shard_map.64 = (f32[4,4,128,512]{3,2,1,0:T(8,128)}, f32[4,4,1,512]{3,2,1,0:T(1,128)S(1)}, f32[4,4,1,512]{3,2,1,0:T(1,128)S(1)}) custom-call(s32[3]{0:T(128)S(1)} %get-tuple-element.81.place, s32[8]{0:T(128)S(1)} %copy-done.2, s32[640]{0:T(1024)S(1)} %reshape.3.tasks, bf16[8,1024,128]{2,1,0:T(8,128)(2,1)S(1)} %copy-done, bf16[1024,128]{1,0:T(8,128)(2,1)S(1)} %bitcast.34, ...), custom_call_target="tpu_custom_call" | custom-call | flops 4294967296 | bytes 8388608 | tf_op jit(solution)/shard_map/pallas_call | solution.py:250
  50.9 0.5 collective-permute-start.7
  51.4 0.1 collective-permute-start.8
  51.4 0.4 collective-permute-start.9
  51.9 0.1 pad_add_fusion.2.place
  51.9 0.1 add_add_fusion
  52.0 0.6 collective-permute-done.6.refs_1_
  52.6 0.2 collective-permute-done.7.refs_3_
  52.8 0.5 collective-permute-done.8.refs_5_
  53.3 0.4 collective-permute-done.9.refs_7_
  53.6 10.0 %shard_map.65 = bf16[256,1024]{1,0:T(8,128)(2,1)S(1)} custom-call(s32[3]{0:T(128)S(1)} %pad_add_fusion.2.place, s32[8]{0:T(128)S(1)} %copy-done.2, s32[640]{0:T(1024)S(1)} %reshape.3.tasks, bf16[8,1024,128]{2,1,0:T(8,128)(2,1)S(1)} %copy-done, bf16[1024,128]{1,0:T(8,128)(2,1)} %collective-permute-done.2.refs_0_, ...), custom_call_target="tpu_custom_call" | custom-call | flops 4294967296 | bytes 8388608 | tf_op jit(solution)/shard_map/pallas_call | solution.py:250
  63.6 0.7 convolution_convert_fusion.3
  64.4 1.4 collective-permute-start.10
  65.7 10.1 %shard_map.66 = bf16[256,1024]{1,0:T(8,128)(2,1)S(1)} custom-call(s32[3]{0:T(128)S(1)} %get-tuple-element.56.place, s32[8]{0:T(128)S(1)} %copy-done.2, s32[640]{0:T(1024)S(1)} %reshape.3.tasks, bf16[8,1024,128]{2,1,0:T(8,128)(2,1)S(1)} %copy-done, bf16[1024,128]{1,0:T(8,128)(2,1)} %collective-permute-done.2.refs_0_, ...), custom_call_target="tpu_custom_call" | custom-call | flops 4294967296 | bytes 8388608 | tf_op jit(solution)/shard_map/pallas_call | solution.py:250
  75.9 0.7 convolution_convert_fusion.2
  76.6 1.2 collective-permute-done.10
  77.8 0.7 convolution_add_fusion.3
  78.6 2.4 %collective-permute-start.12 = (bf16[256,512]{1,0:T(8,128)(2,1)S(1)}, bf16[256,512]{1,0:T(8,128)(2,1)S(1)}, u32[]{:S(2)}, u32[]{:S(2)}) collective-permute-start(bf16[256,512]{1,0:T(8,128)(2,1)S(1)} %slice.57), channel_id=1, source_target_pairs={{0,2},{1,3},{2,0},{3,1},{4,6},{5,7},{6,4},{7,5},{8,10},{9,11},{10,... | collective-permute-start | bytes 786440 | tf_op jit(solution)/shard_map/ppermute | solution.py:349
  81.0 1.3 collective-permute-start.11
  82.2 10.0 %shard_map.67 = bf16[256,1024]{1,0:T(8,128)(2,1)S(1)} custom-call(s32[3]{0:T(128)S(1)} %get-tuple-element.62.place, s32[8]{0:T(128)S(1)} %copy-done.2, s32[640]{0:T(1024)S(1)} %reshape.3.tasks, bf16[8,1024,128]{2,1,0:T(8,128)(2,1)S(1)} %copy-done, bf16[1024,128]{1,0:T(8,128)(2,1)} %collective-permute-done.2.refs_0_, ...), custom_call_target="tpu_custom_call" | custom-call | flops 4294967296 | bytes 8388608 | tf_op jit(solution)/shard_map/pallas_call | solution.py:250
  92.2 0.7 convolution_convert_fusion.1
  93.0 4.7 %collective-permute-done.11 = bf16[256,1024]{1,0:T(8,128)(2,1)S(1)} collective-permute-done((bf16[256,1024]{1,0:T(8,128)(2,1)S(1)}, bf16[256,1024]{1,0:T(8,128)(2,1)S(1)}, u32[]{:S(2)}, u32[]{:S(2)}) %collective-permute-start.11) | collective-permute-done | bytes 524320 | tf_op jit(solution)/shard_map/ppermute | solution.py:348
  97.7 0.7 convolution_add_fusion.2
  98.5 1.4 collective-permute-start.14
  99.9 1.2 collective-permute-start.13
  101.1 11.9 %shard_map.68 = bf16[256,1024]{1,0:T(8,128)(2,1)S(1)} custom-call(s32[3]{0:T(128)S(1)} %get-tuple-element.69.place, s32[8]{0:T(128)S(1)} %copy-done.2, s32[640]{0:T(1024)S(1)} %reshape.3.tasks, bf16[8,1024,128]{2,1,0:T(8,128)(2,1)S(1)} %copy-done, bf16[1024,128]{1,0:T(8,128)(2,1)} %collective-permute-done.2.refs_0_, ...), custom_call_target="tpu_custom_call" | custom-call | flops 4294967296 | bytes 8388608 | tf_op jit(solution)/shard_map/pallas_call | solution.py:250
  113.0 0.7 convolution_convert_fusion
  113.7 3.4 %collective-permute-done.13 = bf16[256,1024]{1,0:T(8,128)(2,1)S(1)} collective-permute-done((bf16[256,1024]{1,0:T(8,128)(2,1)S(1)}, bf16[256,1024]{1,0:T(8,128)(2,1)S(1)}, u32[]{:S(2)}, u32[]{:S(2)}) %collective-permute-start.13) | collective-permute-done | bytes 524320 | tf_op jit(solution)/shard_map/ppermute | solution.py:348
  117.2 0.1 add_convert_fusion.1
  117.3 0.7 convolution_add_fusion.1
  118.1 2.0 %collective-permute-start.15 = (bf16[256,512]{1,0:T(8,128)(2,1)S(1)}, bf16[256,512]{1,0:T(8,128)(2,1)S(1)}, u32[]{:S(2)}, u32[]{:S(2)}) collective-permute-start(bf16[256,512]{1,0:T(8,128)(2,1)S(1)} %slice.55), channel_id=1, source_target_pairs={{0,2},{1,3},{2,0},{3,1},{4,6},{5,7},{6,4},{7,5},{8,10},{9,11},{10,... | collective-permute-start | bytes 786440 | tf_op jit(solution)/shard_map/ppermute | solution.py:358
  120.1 14.6 %collective-permute-done.16 = bf16[256,1024]{1,0:T(8,128)(2,1)S(1)} collective-permute-done((bf16[256,1024]{1,0:T(8,128)(2,1)S(1)}, bf16[256,1024]{1,0:T(8,128)(2,1)S(1)}, u32[]{:S(2)}, u32[]{:S(2)}) %collective-permute-start.16) | collective-permute-done | bytes 524320 | tf_op jit(solution)/shard_map/ppermute | solution.py:356
  134.6 0.7 convolution_add_fusion
  135.5 0.1 add_convert_fusion
  135.7 13.4 %collective-permute-done.17 = bf16[256,512]{1,0:T(8,128)(2,1)S(1)} collective-permute-done((bf16[256,512]{1,0:T(8,128)(2,1)S(1)}, bf16[256,512]{1,0:T(8,128)(2,1)S(1)}, u32[]{:S(2)}, u32[]{:S(2)}) %collective-permute-start.17) | collective-permute-done | bytes 262176 | tf_op jit(solution)/shard_map/ppermute | solution.py:360
  149.2 1.0 pad_maximum_fusion.2
  (38 shorter events, 0.6 us)
Async XLA Ops:
  1.1 49.6 %collective-permute-start.5 = (bf16[128,1024]{1,0:T(8,128)(2,1)S(1)}, bf16[128,1024]{1,0:T(8,128)(2,1)S(1)}, u32[]{:S(2)}, u32[]{:S(2)}) collective-permute-start(bf16[128,1024]{1,0:T(8,128)(2,1)S(1)} %bitcast.27), channel_id=1, source_target_pairs={{0,8},{4,12},{8,16},{12,20},{16,24},{20,28},{1,9},{5,13},{9,17},{1... | collective-permute-start | bytes 786440 | tf_op jit(solution)/shard_map/ppermute | solution.py:304
  4.2 46.5 %collective-permute-start.3 = (bf16[128,1024]{1,0:T(8,128)(2,1)S(1)}, bf16[128,1024]{1,0:T(8,128)(2,1)S(1)}, u32[]{:S(2)}, u32[]{:S(2)}) collective-permute-start(bf16[128,1024]{1,0:T(8,128)(2,1)S(1)} %bitcast.28), channel_id=1, source_target_pairs={{0,16},{4,20},{8,24},{12,28},{1,17},{5,21},{9,25},{13,29},{2,18},{... | collective-permute-start | bytes 786440 | tf_op jit(solution)/shard_map/ppermute | solution.py:304
  5.5 12.7 %collective-permute-start.1 = (bf16[128,1024]{1,0:T(8,128)(2,1)S(1)}, bf16[128,1024]{1,0:T(8,128)(2,1)S(1)}, u32[]{:S(2)}, u32[]{:S(2)}) collective-permute-start(bf16[128,1024]{1,0:T(8,128)(2,1)S(1)} %bitcast.29), channel_id=1, source_target_pairs={{0,4},{4,0},{8,12},{12,8},{16,20},{20,16},{24,28},{28,24},{1,5},{5... | collective-permute-start | bytes 786440 | tf_op jit(solution)/shard_map/ppermute | solution.py:306
  6.5 44.2 %collective-permute-start.4 = (bf16[1024,128]{1,0:T(8,128)(2,1)}, bf16[1024,128]{1,0:T(8,128)(2,1)S(1)}, u32[]{:S(2)}, u32[]{:S(2)}) collective-permute-start(bf16[1024,128]{1,0:T(8,128)(2,1)} %bitcast.31), channel_id=1, source_target_pairs={{0,8},{4,12},{8,16},{12,20},{16,24},{20,28},{1,9},{5,13},{9,17},{1... | collective-permute-start | bytes 786440 | tf_op jit(solution)/shard_map/ppermute | solution.py:304
  8.5 11.1 %collective-permute-start = (bf16[1024,128]{1,0:T(8,128)(2,1)}, bf16[1024,128]{1,0:T(8,128)(2,1)}, u32[]{:S(2)}, u32[]{:S(2)}) collective-permute-start(bf16[1024,128]{1,0:T(8,128)(2,1)} %bitcast.32), channel_id=1, source_target_pairs={{0,4},{4,0},{8,12},{12,8},{16,20},{20,16},{24,28},{28,24},{1,5},{5... | collective-permute-start | bytes 786440 | tf_op jit(solution)/shard_map/ppermute | solution.py:306
  8.6 4.4 %copy-start.7 = (s32[128,5]{0,1:T(8,128)S(1)}, s32[128,5]{0,1:T(8,128)}, u32[]{:S(2)}) copy-start(s32[128,5]{0,1:T(8,128)} %param.10) | copy-start | bytes 7684
  13.3 5.0 %copy-start.1 = (bf16[1,1024,128]{2,1,0:T(8,128)(2,1)S(1)}, bf16[1,1024,128]{2,1,0:T(8,128)(2,1)}, u32[]{:S(2)}) copy-start(bf16[1,1024,128]{2,1,0:T(8,128)(2,1)} %param.7) | copy-start | bytes 786436
  13.3 6.2 %copy-start = (bf16[8,1024,128]{2,1,0:T(8,128)(2,1)S(1)}, bf16[8,1024,128]{2,1,0:T(8,128)(2,1)}, u32[]{:S(2)}) copy-start(bf16[8,1024,128]{2,1,0:T(8,128)(2,1)} %q_ref.9) | copy-start | bytes 6291460
  13.3 6.2 %copy-start.2 = (s32[8]{0:T(128)S(1)}, s32[8]{0:T(128)}, u32[]{:S(2)}) copy-start(s32[8]{0:T(128)} %lengths.9) | copy-start | bytes 100
  18.3 32.5 %collective-permute-start.2 = (bf16[1024,128]{1,0:T(8,128)(2,1)S(1)}, bf16[1024,128]{1,0:T(8,128)(2,1)}, u32[]{:S(2)}, u32[]{:S(2)}) collective-permute-start(bf16[1024,128]{1,0:T(8,128)(2,1)S(1)} %bitcast.33), channel_id=1, source_target_pairs={{0,16},{4,20},{8,24},{12,28},{1,17},{5,21},{9,25},{13,29},{2,18},{... | collective-permute-start | bytes 786440 | tf_op jit(solution)/shard_map/ppermute | solution.py:304
  50.8 1.8 %collective-permute-start.6 = (bf16[1024,128]{1,0:T(8,128)(2,1)}, bf16[1024,128]{1,0:T(8,128)(2,1)S(1)}, u32[]{:S(2)}, u32[]{:S(2)}) collective-permute-start(bf16[1024,128]{1,0:T(8,128)(2,1)} %collective-permute-done.2.refs_0_), channel_id=1, source_target_pairs={{0,4},{4,0},{8,12},{12,8},{16,20},{20,16},{24,28},{28,24},{1,5},{5... | collective-permute-start | bytes 786440 | tf_op jit(solution)/shard_map/ppermute | solution.py:332
  50.9 1.9 %collective-permute-start.7 = (bf16[1024,128]{1,0:T(8,128)(2,1)S(1)}, bf16[1024,128]{1,0:T(8,128)(2,1)S(1)}, u32[]{:S(2)}, u32[]{:S(2)}) collective-permute-start(bf16[1024,128]{1,0:T(8,128)(2,1)S(1)} %collective-permute-done.4.refs_2_), channel_id=1, source_target_pairs={{0,4},{4,0},{8,12},{12,8},{16,20},{20,16},{24,28},{28,24},{1,5},{5... | collective-permute-start | bytes 786440 | tf_op jit(solution)/shard_map/ppermute | solution.py:332
  51.4 1.9 %collective-permute-start.8 = (bf16[128,1024]{1,0:T(8,128)(2,1)S(1)}, bf16[128,1024]{1,0:T(8,128)(2,1)}, u32[]{:S(2)}, u32[]{:S(2)}) collective-permute-start(bf16[128,1024]{1,0:T(8,128)(2,1)S(1)} %collective-permute-done.3.refs_4_), channel_id=1, source_target_pairs={{0,4},{4,0},{8,12},{12,8},{16,20},{20,16},{24,28},{28,24},{1,5},{5... | collective-permute-start | bytes 786440 | tf_op jit(solution)/shard_map/ppermute | solution.py:332
  51.4 2.2 %collective-permute-start.9 = (bf16[128,1024]{1,0:T(8,128)(2,1)S(1)}, bf16[128,1024]{1,0:T(8,128)(2,1)}, u32[]{:S(2)}, u32[]{:S(2)}) collective-permute-start(bf16[128,1024]{1,0:T(8,128)(2,1)S(1)} %collective-permute-done.5.refs_6_), channel_id=1, source_target_pairs={{0,4},{4,0},{8,12},{12,8},{16,20},{20,16},{24,28},{28,24},{1,5},{5... | collective-permute-start | bytes 786440 | tf_op jit(solution)/shard_map/ppermute | solution.py:332
  52.0 11.6 %copy-start.6 = (bf16[1024,1024]{1,0:T(8,128)(2,1)S(1)}, bf16[1024,1024]{1,0:T(8,128)(2,1)}, u32[]{:S(2)}) copy-start(bf16[1024,1024]{1,0:T(8,128)(2,1)} %get-tuple-element.55) | copy-start | bytes 6291460
  64.4 13.5 %collective-permute-start.10 = (bf16[256,1024]{1,0:T(8,128)(2,1)S(1)}, bf16[256,1024]{1,0:T(8,128)(2,1)S(1)}, u32[]{:S(2)}, u32[]{:S(2)}) collective-permute-start(bf16[256,1024]{1,0:T(8,128)(2,1)S(1)} %convolution_convert_fusion.3), channel_id=1, source_target_pairs={{0,1},{1,0},{2,3},{3,2},{4,5},{5,4},{6,7},{7,6},{8,9},{9,8},{10,11... | collective-permute-start | bytes 1572872 | tf_op jit(solution)/shard_map/ppermute | solution.py:348
  75.9 1.9 %copy-start.3 = (bf16[1024,1024]{1,0:T(8,128)(2,1)S(1)}, bf16[1024,1024]{1,0:T(8,128)(2,1)}, u32[]{:S(2)}) copy-start(bf16[1024,1024]{1,0:T(8,128)(2,1)} %get-tuple-element.59) | copy-start | bytes 6291460
  78.6 13.7 %copy-start.4 = (f32[256,1024]{1,0:T(8,128)}, f32[256,1024]{1,0:T(8,128)S(1)}, u32[]{:S(2)}) copy-start(f32[256,1024]{1,0:T(8,128)S(1)} %convolution_add_fusion.3) | copy-start | bytes 3145732
  78.6 14.4 %collective-permute-start.12 = (bf16[256,512]{1,0:T(8,128)(2,1)S(1)}, bf16[256,512]{1,0:T(8,128)(2,1)S(1)}, u32[]{:S(2)}, u32[]{:S(2)}) collective-permute-start(bf16[256,512]{1,0:T(8,128)(2,1)S(1)} %slice.57), channel_id=1, source_target_pairs={{0,2},{1,3},{2,0},{3,1},{4,6},{5,7},{6,4},{7,5},{8,10},{9,11},{10,... | collective-permute-start | bytes 786440 | tf_op jit(solution)/shard_map/ppermute | solution.py:349
  81.0 16.7 %collective-permute-start.11 = (bf16[256,1024]{1,0:T(8,128)(2,1)S(1)}, bf16[256,1024]{1,0:T(8,128)(2,1)S(1)}, u32[]{:S(2)}, u32[]{:S(2)}) collective-permute-start(bf16[256,1024]{1,0:T(8,128)(2,1)S(1)} %convolution_convert_fusion.2), channel_id=1, source_target_pairs={{0,1},{1,0},{2,3},{3,2},{4,5},{5,4},{6,7},{7,6},{8,9},{9,8},{10,11... | collective-permute-start | bytes 1572872 | tf_op jit(solution)/shard_map/ppermute | solution.py:348
  98.4 14.6 %copy-start.5 = (f32[256,1024]{1,0:T(8,128)}, f32[256,1024]{1,0:T(8,128)S(1)}, u32[]{:S(2)}) copy-start(f32[256,1024]{1,0:T(8,128)S(1)} %convolution_add_fusion.2) | copy-start | bytes 3145732
  98.5 15.3 %collective-permute-start.14 = (bf16[256,512]{1,0:T(8,128)(2,1)S(1)}, bf16[256,512]{1,0:T(8,128)(2,1)S(1)}, u32[]{:S(2)}, u32[]{:S(2)}) collective-permute-start(bf16[256,512]{1,0:T(8,128)(2,1)S(1)} %slice.56), channel_id=1, source_target_pairs={{0,2},{1,3},{2,0},{3,1},{4,6},{5,7},{6,4},{7,5},{8,10},{9,11},{10,... | collective-permute-start | bytes 786440 | tf_op jit(solution)/shard_map/ppermute | solution.py:349
  99.9 17.2 %collective-permute-start.13 = (bf16[256,1024]{1,0:T(8,128)(2,1)S(1)}, bf16[256,1024]{1,0:T(8,128)(2,1)S(1)}, u32[]{:S(2)}, u32[]{:S(2)}) collective-permute-start(bf16[256,1024]{1,0:T(8,128)(2,1)S(1)} %convolution_convert_fusion.1), channel_id=1, source_target_pairs={{0,1},{1,0},{2,3},{3,2},{4,5},{5,4},{6,7},{7,6},{8,9},{9,8},{10,11... | collective-permute-start | bytes 1572872 | tf_op jit(solution)/shard_map/ppermute | solution.py:348
  113.0 4.2 %slice-start = ((f32[256,1024]{1,0:T(8,128)}), f32[256,512]{1,0:T(8,128)S(1)}, s32[]{:S(2)}) async-start(f32[256,1024]{1,0:T(8,128)} %copy-done.4), calls=%async_computation | async-start | bytes 1048576 | tf_op jit(solution)/shard_map/slice | solution.py:341
  117.2 17.5 %collective-permute-start.16 = (bf16[256,1024]{1,0:T(8,128)(2,1)S(1)}, bf16[256,1024]{1,0:T(8,128)(2,1)S(1)}, u32[]{:S(2)}, u32[]{:S(2)}) collective-permute-start(bf16[256,1024]{1,0:T(8,128)(2,1)S(1)} %convolution_convert_fusion), channel_id=1, source_target_pairs={{0,1},{1,0},{2,3},{3,2},{4,5},{5,4},{6,7},{7,6},{8,9},{9,8},{10,11... | collective-permute-start | bytes 1572872 | tf_op jit(solution)/shard_map/ppermute | solution.py:356
  118.1 17.4 %slice-start.1 = ((f32[256,1024]{1,0:T(8,128)}), f32[256,512]{1,0:T(8,128)S(1)}, s32[]{:S(2)}) async-start(f32[256,1024]{1,0:T(8,128)} %copy-done.5), calls=%async_computation.1 | async-start | bytes 1048576 | tf_op jit(solution)/shard_map/slice | solution.py:341
  118.1 17.5 %collective-permute-start.15 = (bf16[256,512]{1,0:T(8,128)(2,1)S(1)}, bf16[256,512]{1,0:T(8,128)(2,1)S(1)}, u32[]{:S(2)}, u32[]{:S(2)}) collective-permute-start(bf16[256,512]{1,0:T(8,128)(2,1)S(1)} %slice.55), channel_id=1, source_target_pairs={{0,2},{1,3},{2,0},{3,1},{4,6},{5,7},{6,4},{7,5},{8,10},{9,11},{10,... | collective-permute-start | bytes 786440 | tf_op jit(solution)/shard_map/ppermute | solution.py:358
  135.4 13.7 %collective-permute-start.17 = (bf16[256,512]{1,0:T(8,128)(2,1)S(1)}, bf16[256,512]{1,0:T(8,128)(2,1)S(1)}, u32[]{:S(2)}, u32[]{:S(2)}) collective-permute-start(bf16[256,512]{1,0:T(8,128)(2,1)S(1)} %slice.54), channel_id=1, source_target_pairs={{0,2},{1,3},{2,0},{3,1},{4,6},{5,7},{6,4},{7,5},{8,10},{9,11},{10,... | collective-permute-start | bytes 786440 | tf_op jit(solution)/shard_map/ppermute | solution.py:360

commit v2 on v1

v2 whole, which is shorter than its diff:
```python
from functools import partial
import math

import jax
import jax.numpy as jnp
from jax import lax
from jax.experimental import pallas as pl
from jax.experimental.pallas import tpu as pltpu
from jax.sharding import PartitionSpec as P

FLOOR_SCORE = -1e30
SAFE_TOTAL = 2.0**100
KEY_TILE = 512
EDGE_TILE = 256
SUB = 128
PAIR = 4
FIRST_PARTS = 4
PARTS = (1, 2, 2, 2, 1)


def attend_kernel(
    place, lengths, tasks, q_ref, *refs, slots, subs, q_block, key_tile, edge_tile, resume
):
    key_refs, value_refs, refs = refs[:slots], refs[slots : 2 * slots], refs[2 * slots :]
    if resume:
        states, w_ref, refs = refs[:3], refs[3], refs[4:]
        sent_ref, kept_ref, q_buf, key_all, value_all, acc, peak, total = refs[:8]
        s_buf, p_buf, rescale_buf, sems, w_buf, attended, w_sems = refs[8:]
    else:
        outs, refs = refs[:3], refs[3:]
        q_buf, key_all, value_all, acc, peak, total, s_buf, p_buf, rescale_buf, sems = refs
    heads, _, width = q_ref.shape
    shard_rows = key_refs[0].shape[0]
    groups = heads // PAIR
    units = subs * groups
    cols = PAIR * SUB
    rows = subs * SUB
    step_id = pl.program_id(0)
    parity = place[0]
    first_row = place[1] + step_id * rows
    base = place[2]
    limit = place[3]
    local_row = place[4] + step_id * rows

    q_copy = pltpu.make_async_copy(
        q_ref.at[:, pl.ds(pl.multiple_of(local_row, SUB), rows), :], q_buf, sems.at[2 * slots]
    )
    q_copy.start()
    copies = []
    for at in range(slots):
        slot = at if at == slots - 1 else at // 2 * 2 + (parity if at % 2 == 0 else 1 - parity)
        copies.append(pltpu.make_async_copy(key_refs[at], key_all.at[slot], sems.at[2 * at]))
        copies.append(
            pltpu.make_async_copy(value_refs[at], value_all.at[slot], sems.at[2 * at + 1])
        )

    def fetch():
        for copy in copies:
            copy.start()

    def wait():
        for copy in copies:
            copy.wait()

    if resume:
        fetch()
        sub_row = local_row // SUB
        state_copies = [
            pltpu.make_async_copy(
                state.at[pl.ds(sub_row, subs)], ref, sems.at[2 * slots + 1 + at]
            )
            for at, (state, ref) in enumerate(zip(states, (acc, peak, total)))
        ]
        for copy in state_copies:
            copy.start()
        out_cols = w_buf.shape[2]
        w_copies = []
        for at in range(4):
            column = pl.multiple_of(place[5 + at] * out_cols, out_cols)
            w_copies.append(
                pltpu.make_async_copy(
                    w_ref.at[:, pl.ds(column, out_cols)], w_buf.at[at], w_sems.at[at]
                )
            )
        for copy in w_copies:
            copy.start()
    else:
        pl.when(step_id == 0)(fetch)

    last_row = first_row + rows - 1
    one_head = [
        first_row + sub * SUB + lax.broadcasted_iota(jnp.int32, (1, SUB), 1) for sub in range(subs)
    ]
    begin = [jnp.zeros((1, SUB), jnp.int32)] * subs
    begin_first = jnp.int32(0)
    begin_last = jnp.int32(0)
    start = jnp.int32(0)
    for doc in range(lengths.shape[0]):
        begin = [
            jnp.where(one >= start, jnp.maximum(old, start), old)
            for one, old in zip(one_head, begin)
        ]
        begin_first = jnp.where(first_row >= start, jnp.maximum(begin_first, start), begin_first)
        begin_last = jnp.where(last_row >= start, jnp.maximum(begin_last, start), begin_last)
        start = start + lengths[doc]

    task = (first_row // q_block) * heads
    lows = [tasks[(task + head) * 5 + 2] * q_block for head in range(heads)]
    highs = [tasks[(task + head) * 5 + 3] * q_block for head in range(heads)]
    low_least, low_most, high_least, high_most = lows[0], lows[0], highs[0], highs[0]
    for low, high in zip(lows[1:], highs[1:]):
        low_least, low_most = jnp.minimum(low_least, low), jnp.maximum(low_most, low)
        high_least, high_most = jnp.minimum(high_least, high), jnp.maximum(high_most, high)
    begins, ends = [], []
    for sub in range(subs):
        for group in range(groups):
            members = range(group * PAIR, (group + 1) * PAIR)
            begins.append(
                jnp.concatenate([jnp.maximum(begin[sub], lows[m]) for m in members], axis=1)
            )
            ends.append(
                jnp.concatenate([jnp.minimum(one_head[sub], highs[m] - 1) for m in members], axis=1)
            )

    ratio = key_tile // edge_tile
    tiles = limit // edge_tile
    lo = jnp.clip((jnp.maximum(low_least, begin_first) - base) // edge_tile, 0, tiles)
    hi = jnp.clip(
        (jnp.minimum(high_most, last_row + 1) - base + edge_tile - 1) // edge_tile, lo, tiles
    )
    full_lo = (jnp.maximum(low_most, begin_last) - base + key_tile - 1) // key_tile
    full_hi = (jnp.minimum(high_least, first_row + 1) - base) // key_tile
    full_lo = jnp.maximum(full_lo, 0)
    full_hi = jnp.minimum(full_hi, tiles // ratio)
    some = full_hi > full_lo
    inner_lo = jnp.where(some, full_lo * ratio, lo)
    inner_hi = jnp.where(some, full_hi * ratio, lo)
    factor = math.log2(math.e) / math.sqrt(width)

    if resume:
        for copy in state_copies:
            copy.wait()
        wait()
    else:
        acc[...] = jnp.zeros_like(acc)
        peak[...] = jnp.full_like(peak, FLOOR_SCORE)
        total[...] = jnp.zeros_like(total)
        pl.when(step_id == 0)(wait)
    q_copy.wait()

    def sweep(count, tile_of, size, masked, fixed):
        per_shard = shard_rows // size

        def keys_of(tile):
            offset = pl.multiple_of((tile % per_shard) * size, size)
            return key_all[tile // per_shard, pl.ds(offset, size), :]

        def values_of(tile):
            offset = pl.multiple_of((tile % per_shard) * size, size)
            values = value_all[tile // per_shard, :, pl.ds(offset, size)]
            return jnp.concatenate([values, jnp.ones((16, size), jnp.bfloat16)], axis=0)

        def scores_of(keys, unit):
            sub, group = divmod(unit, groups)
            asked = q_buf[group * PAIR : (group + 1) * PAIR, sub * SUB : (sub + 1) * SUB, :]
            return lax.dot_general(
                keys,
                asked.reshape(cols, width),
                (((1,), (1,)), ((), ())),
                preferred_element_type=jnp.float32,
            )

        def gather(values, unit, weights, rescale):
            at = divmod(unit, groups)
            product = lax.dot_general(
                values, weights, (((1,), (0,)), ((), ())), preferred_element_type=jnp.float32
            )
            if fixed:
                total[at] += product[width : width + 1]
                acc[at] += product[:width]
            else:
                total[at] = total[at] * rescale + product[width : width + 1]
                acc[at] = acc[at] * rescale + product[:width]

        def step(turn, carried):
            tile = tile_of(turn)
            keys, values = keys_of(tile), values_of(tile)
            key_pos = (
                base + tile * size + lax.broadcasted_iota(jnp.int32, (size, 1), 0)
                if masked
                else None
            )
            scores = s_buf[:size]
            waiting = None
            for unit in range(units):
                at = divmod(unit, groups)
                if unit + 1 < units:
                    ahead = scores_of(keys, unit + 1)
                else:
                    ahead = scores_of(keys_of(tile_of(jnp.minimum(turn + 1, count - 1))), 0)
                if masked:
                    visible = (key_pos >= begins[unit]) & (key_pos <= ends[unit])
                    scores = jnp.where(visible, scores, FLOOR_SCORE)
                before = peak[at]
                if fixed:
                    now, rescale = before, None
                else:
                    now = jnp.maximum(before, jnp.max(scores, axis=0, keepdims=True) * factor)
                    peak[at] = now
                    rescale = jnp.exp2(before - now)
                weights = jnp.exp2(scores * factor - now).astype(jnp.bfloat16)
                if waiting is not None:
                    gather(values, unit - 1, *waiting)
                else:
                    earlier = values_of(tile_of(jnp.maximum(turn - 1, 0)))
                    gather(earlier, units - 1, p_buf[:size], rescale_buf[...])
                waiting = weights, rescale
                scores = ahead
            s_buf[:size] = scores
            p_buf[:size] = waiting[0]
            if not fixed:
                rescale_buf[...] = waiting[1]
            return carried

        def whole():
            p_buf[:size] = jnp.zeros((size, cols), jnp.bfloat16)
            rescale_buf[...] = jnp.ones_like(rescale_buf)
            s_buf[:size] = scores_of(keys_of(tile_of(0)), 0)
            lax.fori_loop(0, count, step, 0)
            gather(values_of(tile_of(count - 1)), units - 1, p_buf[:size], rescale_buf[...])

        pl.when(count > 0)(whole)

    sweep(
        (inner_hi - inner_lo) // ratio,
        lambda turn: inner_lo // ratio + turn,
        key_tile,
        False,
        resume,
    )
    left = inner_lo - lo
    sweep(
        left + hi - inner_hi,
        lambda turn: jnp.where(turn < left, lo + turn, inner_hi + turn - left),
        edge_tile,
        True,
        resume,
    )
    if not resume:
        outs[0][...] = acc[...]
        outs[1][...] = peak[...]
        outs[2][...] = total[...]
        return
    in_range = jnp.min(jnp.where(total[...] < SAFE_TOTAL, 1.0, 0.0))

    @pl.when(in_range < 0.5)
    def again():
        for copy in state_copies:
            copy.start()
        for copy in state_copies:
            copy.wait()
        sweep(hi - lo, lambda turn: lo + turn, edge_tile, True, False)

    for sub in range(subs):
        for group in range(groups):
            done = (acc[sub, group] / total[sub, group]).T.astype(jnp.bfloat16)
            for member in range(PAIR):
                head = group * PAIR + member
                attended[sub * SUB : (sub + 1) * SUB, head * width : (head + 1) * width] = done[
                    member * SUB : (member + 1) * SUB
                ]
    for at in range(4):
        w_copies[at].wait()
        product = jnp.dot(attended[...], w_buf[at], preferred_element_type=jnp.float32)
        ref = sent_ref if at < 2 else kept_ref
        column = (at % 2) * out_cols
        ref[:, column : column + out_cols] = product.astype(ref.dtype)


def attend(place, lengths, tasks, queries, kvs, subs, q_block, states=None, w_out=None, out_cols=0):
    heads, tok_dev, width = queries.shape
    shard_rows = kvs[0][0].shape[0]
    slots = len(kvs)
    key_tile = min(KEY_TILE, shard_rows)
    edge_tile = min(EDGE_TILE, key_tile)
    resume = states is not None
    groups, cols, rows = heads // PAIR, PAIR * SUB, subs * SUB
    state_shapes = [(groups, width, cols), (groups, 1, cols), (groups, 1, cols)]
    hbm = pl.BlockSpec(memory_space=pl.ANY)
    scratch = [
        pltpu.VMEM((heads, rows, width), jnp.bfloat16),
        pltpu.VMEM((slots, shard_rows, width), jnp.bfloat16),
        pltpu.VMEM((slots, width, shard_rows), jnp.bfloat16),
        *[pltpu.VMEM((subs,) + shape, jnp.float32) for shape in state_shapes],
        pltpu.VMEM((key_tile, cols), jnp.float32),
        pltpu.VMEM((key_tile, cols), jnp.bfloat16),
        pltpu.VMEM((1, cols), jnp.float32),
        pltpu.SemaphoreType.DMA((2 * slots + 4,)),
    ]
    if resume:
        extra = [*states, w_out]
        out_specs = [pl.BlockSpec((rows, 2 * out_cols), lambda i, *_: (0, 0))] * 2
        out_shape = [
            jax.ShapeDtypeStruct((rows, 2 * out_cols), jnp.bfloat16),
            jax.ShapeDtypeStruct((rows, 2 * out_cols), jnp.float32),
        ]
        scratch += [
            pltpu.VMEM((4, heads * width, out_cols), jnp.bfloat16),
            pltpu.VMEM((rows, heads * width), jnp.bfloat16),
            pltpu.SemaphoreType.DMA((4,)),
        ]
    else:
        extra = []
        out_specs = [
            pl.BlockSpec((subs,) + shape, lambda i, *_: (i, 0, 0, 0)) for shape in state_shapes
        ]
        out_shape = [
            jax.ShapeDtypeStruct((tok_dev // SUB,) + shape, jnp.float32) for shape in state_shapes
        ]
    return pl.pallas_call(
        partial(
            attend_kernel,
            slots=slots,
            subs=subs,
            q_block=q_block,
            key_tile=key_tile,
            edge_tile=edge_tile,
            resume=resume,
        ),
        grid_spec=pltpu.PrefetchScalarGridSpec(
            num_scalar_prefetch=3,
            grid=(1 if resume else tok_dev // rows,),
            in_specs=[hbm] * (1 + 2 * slots + len(extra)),
            out_specs=out_specs,
            scratch_shapes=scratch,
        ),
        out_shape=out_shape,
        compiler_params=pltpu.CompilerParams(vmem_limit_bytes=40 * 2**20),
        cost_estimate=pl.CostEstimate(
            flops=heads * rows * 4096 * width * 4,
            bytes_accessed=8 * 2**20,
            transcendentals=heads * rows * 4096,
        ),
    )(place, lengths, tasks, queries, *[k for k, _ in kvs], *[v for _, v in kvs], *extra)


def local(queries, keys, values, doc_lengths, tasks, w_out):
    heads, tok_dev, width = queries.shape
    n_tok = lax.axis_size("tok")
    n_head = lax.axis_size("head")
    me = lax.axis_index("tok")
    z = lax.axis_index("head")
    tokens = n_tok * tok_dev
    q_block = tokens * heads // tasks.shape[0]
    chips = n_tok // 2
    doc_most = tokens * 4 // doc_lengths.shape[0]
    back = min(chips - 1, -(-(doc_most - 1) // (2 * tok_dev)))
    out_cols = w_out.shape[1] // n_head
    flat_tasks = tasks.reshape(-1)

    own = keys[0], values[0].T
    spans = []
    for hop in range(back, 0, -1):
        pairs = [(i, i + 2 * hop) for i in range(n_tok - 2 * hop)]
        spans.append(tuple(lax.ppermute(part, "tok", pairs) for part in own))
    swap = [(i, i ^ 1) for i in range(n_tok)]

    columns = [(z ^ 1) ^ 2, z ^ 1, z ^ 2, z]

    def placed(base, limit, row):
        numbers = [me % 2, me * tok_dev + row, base, limit, row, *columns]
        return jnp.stack([jnp.asarray(n, jnp.int32) for n in numbers])

    states = attend(
        placed(me * tok_dev, tok_dev, 0),
        doc_lengths,
        flat_tasks,
        queries,
        [own],
        tok_dev // SUB // FIRST_PARTS,
        q_block,
    )
    spans, states = lax.optimization_barrier((spans, states))
    kvs = []
    for mine in spans:
        kvs += [mine, tuple(lax.ppermute(part, "tok", swap) for part in mine)]
    kvs.append(tuple(lax.ppermute(part, "tok", swap) for part in own))
    base = (me // 2 - back) * 2 * tok_dev

    near = [(i, i ^ 1) for i in range(n_head)]
    far = [(i, i ^ 2) for i in range(n_head)]

    def hop(kept, arrived):
        summed = kept + arrived.astype(jnp.float32)
        return summed[:, :out_cols].astype(jnp.bfloat16), summed[:, out_cols:]

    halves = []
    kept = sent = summed = None
    row = 0
    for part in PARTS:
        subs = tok_dev // SUB * part // sum(PARTS)
        place = placed(base, me * tok_dev - base, row)
        row += subs * SUB
        place, sent, summed = lax.optimization_barrier((place, sent, summed))
        arrived = None if sent is None else lax.ppermute(sent, "head", near)
        crossed = None if summed is None else lax.ppermute(summed[0], "head", far)
        sent, kept_now = attend(
            place, doc_lengths, flat_tasks, queries, kvs, subs, q_block, states, w_out, out_cols
        )
        sent, arrived, crossed = lax.optimization_barrier((sent, arrived, crossed))
        if crossed is not None:
            halves.append((summed[1], crossed))
        summed = None if arrived is None else hop(kept, arrived)
        kept = kept_now
    arrived = lax.ppermute(sent, "head", near)
    if summed is not None:
        halves.append((summed[1], lax.ppermute(summed[0], "head", far)))
    summed = hop(kept, arrived)
    halves.append((summed[1], lax.ppermute(summed[0], "head", far)))
    outs = [(held + crossed.astype(jnp.float32)).astype(jnp.bfloat16) for held, crossed in halves]
    return jnp.concatenate(outs, axis=0)


def solution(mesh):
    placed = (
        P("head", "tok", None),
        P("head", "tok", None),
        P("head", "tok", None),
        P(),
        P(),
        P("head", None),
    )
    return jax.shard_map(
        local, mesh=mesh, in_specs=placed, out_specs=P("tok", "head"), check_vma=False
    )
```

time: 148 us -> 140 us (0.946)
  the two profiles are of different devices: /device:TPU:5 before, /device:TPU:0 now
where the time goes in v2:
time: 140 us; the launch traced here: 139 us
  waiting for transfers between devices  41.3 us (30%)
  Pallas kernels  36 us (26%)
  starting transfers between devices  35.8 us (26%)
  local copies, waits for them, and re-layouts  21.5 us (15%)
  other arithmetic  3.69 us (3%)
    pallas_call x6, Pallas kernels, attend(): pl.pallas_call(partial(attend_kernel, slots=slots, subs=subs, q_block=q_b...  36 us
    ppermute x3, waiting for transfers between devices, local(): crossed = None if summed is None else lax.ppermute(summed[0], 'head', far)  20.7 us
    unnamed x40, local copies, waits for them, and re-layouts  19.3 us
    ppermute x4, starting transfers between devices, local(): spans.append(tuple((lax.ppermute(part, 'tok', pairs) for part in own)))  11.5 us
    ppermute x4, starting transfers between devices, local(): arrived = None if sent is None else lax.ppermute(sent, 'head', near)  10 us
    ppermute x1, waiting for transfers between devices, local(): arrived = lax.ppermute(sent, 'head', near)  8.78 us
    ppermute x2, waiting for transfers between devices, local(): halves.append((summed[1], lax.ppermute(summed[0], 'head', far)))  8.5 us
    ppermute x3, starting transfers between devices, local(): crossed = None if summed is None else lax.ppermute(summed[0], 'head', far)  8.18 us
  transfers between devices with their start and end apart: 20, of which 15 were waited for; matrix products, arithmetic and copies ran while one was open for 1% of the time, Pallas kernels for 23%

profile of v2, /device:TPU:0, one launch (start us, length us, event | category | flops | bytes accessed | tf_op | source)
XLA Modules:
  0.0 138.7 jit_solution(12687005610799826572)
XLA Ops:
  0.0 1.8 %copy.9 = bf16[1,1024,128]{1,2,0:T(8,128)(2,1)} copy(bf16[1,1024,128]{2,1,0:T(8,128)(2,1)} %param.8) | data formatting | bytes 524288 | tf_op args[2]
  1.8 4.9 %collective-permute-start.1 = (bf16[128,1024]{1,0:T(8,128)(2,1)}, bf16[128,1024]{1,0:T(8,128)(2,1)S(1)}, u32[]{:S(2)}, u32[]{:S(2)}) collective-permute-start(bf16[128,1024]{1,0:T(8,128)(2,1)} %bitcast.12.refs_1_), channel_id=1, source_target_pairs={{0,16},{4,20},{8,24},{12,28},{1,17},{5,21},{9,25},{13,29},{2,18},{... | collective-permute-start | bytes 786440 | tf_op jit(solution)/shard_map/ppermute | solution.py:365
  6.7 3.4 %collective-permute-start.3 = (bf16[128,1024]{1,0:T(8,128)(2,1)}, bf16[128,1024]{1,0:T(8,128)(2,1)S(1)}, u32[]{:S(2)}, u32[]{:S(2)}) collective-permute-start(bf16[128,1024]{1,0:T(8,128)(2,1)} %bitcast.12.refs_1_), channel_id=1, source_target_pairs={{0,8},{4,12},{8,16},{12,20},{16,24},{20,28},{1,9},{5,13},{9,17},{1... | collective-permute-start | bytes 786440 | tf_op jit(solution)/shard_map/ppermute | solution.py:365
  10.1 1.3 collective-permute-start
  11.4 1.9 %collective-permute-start.2 = (bf16[1024,128]{1,0:T(8,128)(2,1)}, bf16[1024,128]{1,0:T(8,128)(2,1)S(1)}, u32[]{:S(2)}, u32[]{:S(2)}) collective-permute-start(bf16[1024,128]{1,0:T(8,128)(2,1)} %bitcast.10.refs_0_), channel_id=1, source_target_pairs={{0,8},{4,12},{8,16},{12,20},{16,24},{20,28},{1,9},{5,13},{9,17},{1... | collective-permute-start | bytes 786440 | tf_op jit(solution)/shard_map/ppermute | solution.py:365
  13.4 0.8 copy.8
  14.5 1.6 %copy-done.6 = bf16[8,1024,128]{2,1,0:T(8,128)(2,1)S(1)} copy-done((bf16[8,1024,128]{2,1,0:T(8,128)(2,1)S(1)}, bf16[8,1024,128]{2,1,0:T(8,128)(2,1)}, u32[]{:S(2)}) %copy-start.6) | copy-done | bytes 2097176
  16.1 0.7 copy-done.12
  16.8 15.0 %shard_map.64 = (f32[8,2,128,512]{3,2,1,0:T(8,128)S(1)}, f32[8,2,1,512]{3,2,1,0:T(1,128)S(1)}, f32[8,2,1,512]{3,2,1,0:T(1,128)S(1)}) custom-call(s32[9]{0:T(128)S(1)} %stack.49.place, s32[8]{0:T(128)S(1)} %copy-done.12, s32[640]{0:T(1024)S(1)} %reshape.3.tasks, bf16[8,1024,128]{2,1,0:T(8,128)(2,1)S(1)} %copy-done.6, bf16[1024,128]{1,0:T(8,128)(2,1)} %bitcast.10.refs_0_, ...), custom_call_target="tpu_custom_call" | custom-call | flops 4294967296 | bytes 8388608 | tf_op jit(solution)/shard_map/pallas_call | solution.py:320
  31.8 2.0 %copy-done.2 = f32[8,2,128,512]{3,2,1,0:T(8,128)} copy-done((f32[8,2,128,512]{3,2,1,0:T(8,128)}, f32[8,2,128,512]{3,2,1,0:T(8,128)S(1)}, u32[]{:S(2)}) %copy-start.2) | copy-done | bytes 4194328
  33.8 0.5 collective-permute-start.6
  34.3 0.5 collective-permute-start.5
  37.1 2.2 %copy-done = bf16[1024,2048]{1,0:T(8,128)(2,1)S(1)} copy-done((bf16[1024,2048]{1,0:T(8,128)(2,1)S(1)}, bf16[1024,2048]{1,0:T(8,128)(2,1)}, u32[]{:S(2)}) %copy-start) | copy-done | bytes 4194328
  39.3 2.2 %copy-done.3 = f32[8,2,128,512]{3,2,1,0:T(8,128)S(1)} copy-done((f32[8,2,128,512]{3,2,1,0:T(8,128)S(1)}, f32[8,2,128,512]{3,2,1,0:T(8,128)}, u32[]{:S(2)}) %copy-start.3) | copy-done | bytes 4194328
  41.5 3.6 %shard_map.65 = (bf16[128,1024]{1,0:T(8,128)(2,1)S(1)}, f32[128,1024]{1,0:T(8,128)S(1)}) custom-call(s32[9]{0:T(128)S(1)} %stack.48.place, s32[8]{0:T(128)S(1)} %copy-done.13, s32[640]{0:T(1024)S(1)} %reshape.3.tasks, bf16[8,1024,128]{2,1,0:T(8,128)(2,1)S(1)} %copy-done.7, bf16[1024,128]{1,0:T(8,128)(2,1)S(1)} %collective-permute-done.refs_0_, ...), custom_call_target="tpu_custom_call" | custom-call | flops 2147483648 | bytes 8388608 | tf_op jit(solution)/shard_map/pallas_call | solution.py:320
  45.1 1.6 %collective-permute-start.10 = (bf16[128,1024]{1,0:T(8,128)(2,1)S(1)}, bf16[128,1024]{1,0:T(8,128)(2,1)S(1)}, u32[]{:S(2)}, u32[]{:S(2)}) collective-permute-start(bf16[128,1024]{1,0:T(8,128)(2,1)S(1)} %get-tuple-element.63), channel_id=1, source_target_pairs={{0,1},{1,0},{2,3},{3,2},{4,5},{5,4},{6,7},{7,6},{8,9},{9,8},{10,11... | collective-permute-start | bytes 786440 | tf_op jit(solution)/shard_map/ppermute | solution.py:405
  46.8 4.7 %shard_map.66 = (bf16[256,1024]{1,0:T(8,128)(2,1)}, f32[256,1024]{1,0:T(8,128)S(1)}) custom-call(s32[9]{0:T(128)S(1)} %stack.46.place, s32[8]{0:T(128)S(1)} %copy-done.13, s32[640]{0:T(1024)S(1)} %reshape.3.tasks, bf16[8,1024,128]{2,1,0:T(8,128)(2,1)S(1)} %copy-done.7, bf16[1024,128]{1,0:T(8,128)(2,1)S(1)} %collective-permute-done.refs_0_, ...), custom_call_target="tpu_custom_call" | custom-call | flops 4294967296 | bytes 8388608 | tf_op jit(solution)/shard_map/pallas_call | solution.py:320
  51.5 1.0 copy-done.10
  52.5 0.8 collective-permute-done.10
  53.3 0.8 copy-done.15
  54.1 0.7 slice.74
  54.8 1.6 %collective-permute-start.11 = (bf16[256,1024]{1,0:T(8,128)(2,1)}, bf16[256,1024]{1,0:T(8,128)(2,1)}, u32[]{:S(2)}, u32[]{:S(2)}) collective-permute-start(bf16[256,1024]{1,0:T(8,128)(2,1)} %get-tuple-element.70), channel_id=1, source_target_pairs={{0,1},{1,0},{2,3},{3,2},{4,5},{5,4},{6,7},{7,6},{8,9},{9,8},{10,11... | collective-permute-start | bytes 1572872 | tf_op jit(solution)/shard_map/ppermute | solution.py:405
  56.5 2.6 %collective-permute-start.12 = (bf16[128,512]{1,0:T(8,128)(2,1)}, bf16[128,512]{1,0:T(8,128)(2,1)S(1)}, u32[]{:S(2)}, u32[]{:S(2)}) collective-permute-start(bf16[128,512]{1,0:T(8,128)(2,1)} %slice.74), channel_id=1, source_target_pairs={{0,2},{1,3},{2,0},{3,1},{4,6},{5,7},{6,4},{7,5},{8,10},{9,11},{10,... | collective-permute-start | bytes 393224 | tf_op jit(solution)/shard_map/ppermute | solution.py:406
  59.1 2.2 %copy-done.4 = f32[8,2,128,512]{3,2,1,0:T(8,128)S(1)} copy-done((f32[8,2,128,512]{3,2,1,0:T(8,128)S(1)}, f32[8,2,128,512]{3,2,1,0:T(8,128)}, u32[]{:S(2)}) %copy-start.4) | copy-done | bytes 4194328
  61.2 4.6 %shard_map.67 = (bf16[256,1024]{1,0:T(8,128)(2,1)}, f32[256,1024]{1,0:T(8,128)S(1)}) custom-call(s32[9]{0:T(128)S(1)} %stack.44.place, s32[8]{0:T(128)S(1)} %copy-done.13, s32[640]{0:T(1024)S(1)} %reshape.3.tasks, bf16[8,1024,128]{2,1,0:T(8,128)(2,1)S(1)} %copy-done.7, bf16[1024,128]{1,0:T(8,128)(2,1)S(1)} %collective-permute-done.refs_0_, ...), custom_call_target="tpu_custom_call" | custom-call | flops 4294967296 | bytes 8388608 | tf_op jit(solution)/shard_map/pallas_call | solution.py:320
  65.9 1.0 copy-done.8
  66.9 3.0 %collective-permute-done.12 = bf16[128,512]{1,0:T(8,128)(2,1)S(1)} collective-permute-done((bf16[128,512]{1,0:T(8,128)(2,1)}, bf16[128,512]{1,0:T(8,128)(2,1)S(1)}, u32[]{:S(2)}, u32[]{:S(2)}) %collective-permute-start.12) | collective-permute-done | bytes 131104 | tf_op jit(solution)/shard_map/ppermute | solution.py:406
  70.0 1.2 convert_add_fusion.2
  71.2 1.0 copy-done.14
  72.2 0.7 slice.72
  72.9 2.2 %collective-permute-start.13 = (bf16[256,1024]{1,0:T(8,128)(2,1)}, bf16[256,1024]{1,0:T(8,128)(2,1)}, u32[]{:S(2)}, u32[]{:S(2)}) collective-permute-start(bf16[256,1024]{1,0:T(8,128)(2,1)} %get-tuple-element.79), channel_id=1, source_target_pairs={{0,1},{1,0},{2,3},{3,2},{4,5},{5,4},{6,7},{7,6},{8,9},{9,8},{10,11... | collective-permute-start | bytes 1572872 | tf_op jit(solution)/shard_map/ppermute | solution.py:405
  75.2 3.1 %collective-permute-start.14 = (bf16[256,512]{1,0:T(8,128)(2,1)}, bf16[256,512]{1,0:T(8,128)(2,1)S(1)}, u32[]{:S(2)}, u32[]{:S(2)}) collective-permute-start(bf16[256,512]{1,0:T(8,128)(2,1)} %slice.72), channel_id=1, source_target_pairs={{0,2},{1,3},{2,0},{3,1},{4,6},{5,7},{6,4},{7,5},{8,10},{9,11},{10,... | collective-permute-start | bytes 786440 | tf_op jit(solution)/shard_map/ppermute | solution.py:406
  78.3 2.2 %copy-done.5 = f32[8,2,128,512]{3,2,1,0:T(8,128)S(1)} copy-done((f32[8,2,128,512]{3,2,1,0:T(8,128)S(1)}, f32[8,2,128,512]{3,2,1,0:T(8,128)}, u32[]{:S(2)}) %copy-start.5) | copy-done | bytes 4194328
  80.5 4.4 %shard_map.68 = (bf16[256,1024]{1,0:T(8,128)(2,1)S(1)}, f32[256,1024]{1,0:T(8,128)S(1)}) custom-call(s32[9]{0:T(128)S(1)} %stack.51.place, s32[8]{0:T(128)S(1)} %copy-done.13, s32[640]{0:T(1024)S(1)} %reshape.3.tasks, bf16[8,1024,128]{2,1,0:T(8,128)(2,1)S(1)} %copy-done.7, bf16[1024,128]{1,0:T(8,128)(2,1)S(1)} %collective-permute-done.refs_0_, ...), custom_call_target="tpu_custom_call" | custom-call | flops 4294967296 | bytes 8388608 | tf_op jit(solution)/shard_map/pallas_call | solution.py:320
  84.9 6.5 %collective-permute-done.14 = bf16[256,512]{1,0:T(8,128)(2,1)S(1)} collective-permute-done((bf16[256,512]{1,0:T(8,128)(2,1)}, bf16[256,512]{1,0:T(8,128)(2,1)S(1)}, u32[]{:S(2)}, u32[]{:S(2)}) %collective-permute-start.14) | collective-permute-done | bytes 262176 | tf_op jit(solution)/shard_map/ppermute | solution.py:406
  91.6 1.2 convert_add_fusion.1
  92.9 4.6 %collective-permute-start.15 = (bf16[256,1024]{1,0:T(8,128)(2,1)S(1)}, bf16[256,1024]{1,0:T(8,128)(2,1)S(1)}, u32[]{:S(2)}, u32[]{:S(2)}) collective-permute-start(bf16[256,1024]{1,0:T(8,128)(2,1)S(1)} %get-tuple-element.88), channel_id=1, source_target_pairs={{0,1},{1,0},{2,3},{3,2},{4,5},{5,4},{6,7},{7,6},{8,9},{9,8},{10,11... | collective-permute-start | bytes 1572872 | tf_op jit(solution)/shard_map/ppermute | solution.py:405
  97.6 2.5 %collective-permute-start.16 = (bf16[256,512]{1,0:T(8,128)(2,1)S(1)}, bf16[256,512]{1,0:T(8,128)(2,1)S(1)}, u32[]{:S(2)}, u32[]{:S(2)}) collective-permute-start(bf16[256,512]{1,0:T(8,128)(2,1)S(1)} %slice.71), channel_id=1, source_target_pairs={{0,2},{1,3},{2,0},{3,1},{4,6},{5,7},{6,4},{7,5},{8,10},{9,11},{10,... | collective-permute-start | bytes 786440 | tf_op jit(solution)/shard_map/ppermute | solution.py:406
  100.1 3.6 %shard_map.69 = (bf16[128,1024]{1,0:T(8,128)(2,1)S(1)}, f32[128,1024]{1,0:T(8,128)S(1)}) custom-call(s32[9]{0:T(128)S(1)} %stack.106.place, s32[8]{0:T(128)S(1)} %copy-done.13, s32[640]{0:T(1024)S(1)} %reshape.3.tasks, bf16[8,1024,128]{2,1,0:T(8,128)(2,1)S(1)} %copy-done.7, bf16[1024,128]{1,0:T(8,128)(2,1)S(1)} %collective-permute-done.refs_0_, ...), custom_call_target="tpu_custom_call" | custom-call | flops 2147483648 | bytes 8388608 | tf_op jit(solution)/shard_map/pallas_call | solution.py:320
  103.8 11.2 %collective-permute-done.16 = bf16[256,512]{1,0:T(8,128)(2,1)S(1)} collective-permute-done((bf16[256,512]{1,0:T(8,128)(2,1)S(1)}, bf16[256,512]{1,0:T(8,128)(2,1)S(1)}, u32[]{:S(2)}, u32[]{:S(2)}) %collective-permute-start.16) | collective-permute-done | bytes 262176 | tf_op jit(solution)/shard_map/ppermute | solution.py:406
  115.0 0.7 collective-permute-done.15
  115.8 2.1 %collective-permute-start.18 = (bf16[128,1024]{1,0:T(8,128)(2,1)S(1)}, bf16[128,1024]{1,0:T(8,128)(2,1)S(1)}, u32[]{:S(2)}, u32[]{:S(2)}) collective-permute-start(bf16[128,1024]{1,0:T(8,128)(2,1)S(1)} %get-tuple-element.94), channel_id=1, source_target_pairs={{0,1},{1,0},{2,3},{3,2},{4,5},{5,4},{6,7},{7,6},{8,9},{9,8},{10,11... | collective-permute-start | bytes 786440 | tf_op jit(solution)/shard_map/ppermute | solution.py:415
  118.1 1.8 %collective-permute-start.17 = (bf16[256,512]{1,0:T(8,128)(2,1)S(1)}, bf16[256,512]{1,0:T(8,128)(2,1)S(1)}, u32[]{:S(2)}, u32[]{:S(2)}) collective-permute-start(bf16[256,512]{1,0:T(8,128)(2,1)S(1)} %slice.70), channel_id=1, source_target_pairs={{0,2},{1,3},{2,0},{3,1},{4,6},{5,7},{6,4},{7,5},{8,10},{9,11},{10,... | collective-permute-start | bytes 786440 | tf_op jit(solution)/shard_map/ppermute | solution.py:417
  120.0 8.8 %collective-permute-done.18 = bf16[128,1024]{1,0:T(8,128)(2,1)S(1)} collective-permute-done((bf16[128,1024]{1,0:T(8,128)(2,1)S(1)}, bf16[128,1024]{1,0:T(8,128)(2,1)S(1)}, u32[]{:S(2)}, u32[]{:S(2)}) %collective-permute-start.18) | collective-permute-done | bytes 262176 | tf_op jit(solution)/shard_map/ppermute | solution.py:415
  128.9 0.5 collective-permute-start.19
  129.4 6.6 %collective-permute-done.17 = bf16[256,512]{1,0:T(8,128)(2,1)S(1)} collective-permute-done((bf16[256,512]{1,0:T(8,128)(2,1)S(1)}, bf16[256,512]{1,0:T(8,128)(2,1)S(1)}, u32[]{:S(2)}, u32[]{:S(2)}) %collective-permute-start.17) | collective-permute-done | bytes 262176 | tf_op jit(solution)/shard_map/ppermute | solution.py:417
  136.1 1.9 %collective-permute-done.19 = bf16[128,512]{1,0:T(8,128)(2,1)S(1)} collective-permute-done((bf16[128,512]{1,0:T(8,128)(2,1)S(1)}, bf16[128,512]{1,0:T(8,128)(2,1)S(1)}, u32[]{:S(2)}, u32[]{:S(2)}) %collective-permute-start.19) | collective-permute-done | bytes 131104 | tf_op jit(solution)/shard_map/ppermute | solution.py:419
  138.0 0.7 fusion.6
  (65 shorter events, 3.9 us)
Async XLA Ops:
  1.8 32.0 %collective-permute-start.1 = (bf16[128,1024]{1,0:T(8,128)(2,1)}, bf16[128,1024]{1,0:T(8,128)(2,1)S(1)}, u32[]{:S(2)}, u32[]{:S(2)}) collective-permute-start(bf16[128,1024]{1,0:T(8,128)(2,1)} %bitcast.12.refs_1_), channel_id=1, source_target_pairs={{0,16},{4,20},{8,24},{12,28},{1,17},{5,21},{9,25},{13,29},{2,18},{... | collective-permute-start | bytes 786440 | tf_op jit(solution)/shard_map/ppermute | solution.py:365
  6.7 27.6 %collective-permute-start.3 = (bf16[128,1024]{1,0:T(8,128)(2,1)}, bf16[128,1024]{1,0:T(8,128)(2,1)S(1)}, u32[]{:S(2)}, u32[]{:S(2)}) collective-permute-start(bf16[128,1024]{1,0:T(8,128)(2,1)} %bitcast.12.refs_1_), channel_id=1, source_target_pairs={{0,8},{4,12},{8,16},{12,20},{16,24},{20,28},{1,9},{5,13},{9,17},{1... | collective-permute-start | bytes 786440 | tf_op jit(solution)/shard_map/ppermute | solution.py:365
  10.1 24.2 %collective-permute-start = (bf16[1024,128]{1,0:T(8,128)(2,1)}, bf16[1024,128]{1,0:T(8,128)(2,1)S(1)}, u32[]{:S(2)}, u32[]{:S(2)}) collective-permute-start(bf16[1024,128]{1,0:T(8,128)(2,1)} %bitcast.10.refs_0_), channel_id=1, source_target_pairs={{0,16},{4,20},{8,24},{12,28},{1,17},{5,21},{9,25},{13,29},{2,18},{... | collective-permute-start | bytes 786440 | tf_op jit(solution)/shard_map/ppermute | solution.py:365
  11.4 22.8 %collective-permute-start.2 = (bf16[1024,128]{1,0:T(8,128)(2,1)}, bf16[1024,128]{1,0:T(8,128)(2,1)S(1)}, u32[]{:S(2)}, u32[]{:S(2)}) collective-permute-start(bf16[1024,128]{1,0:T(8,128)(2,1)} %bitcast.10.refs_0_), channel_id=1, source_target_pairs={{0,8},{4,12},{8,16},{12,20},{16,24},{20,28},{1,9},{5,13},{9,17},{1... | collective-permute-start | bytes 786440 | tf_op jit(solution)/shard_map/ppermute | solution.py:365
  13.3 21.6 %collective-permute-start.9 = (bf16[128,1024]{1,0:T(8,128)(2,1)}, bf16[128,1024]{1,0:T(8,128)(2,1)S(1)}, u32[]{:S(2)}, u32[]{:S(2)}) collective-permute-start(bf16[128,1024]{1,0:T(8,128)(2,1)} %bitcast.12.refs_1_), channel_id=1, source_target_pairs={{0,4},{4,0},{8,12},{12,8},{16,20},{20,16},{24,28},{28,24},{1,5},{5... | collective-permute-start | bytes 786440 | tf_op jit(solution)/shard_map/ppermute | solution.py:387
  14.5 1.6 %copy-start.6 = (bf16[8,1024,128]{2,1,0:T(8,128)(2,1)S(1)}, bf16[8,1024,128]{2,1,0:T(8,128)(2,1)}, u32[]{:S(2)}) copy-start(bf16[8,1024,128]{2,1,0:T(8,128)(2,1)} %q_ref.11) | copy-start | bytes 6291460
  16.1 0.7 copy-start.12
  16.8 20.3 %copy-start.7 = (bf16[8,1024,128]{2,1,0:T(8,128)(2,1)S(1)}, bf16[8,1024,128]{2,1,0:T(8,128)(2,1)}, u32[]{:S(2)}) copy-start(bf16[8,1024,128]{2,1,0:T(8,128)(2,1)} %q_ref.11) | copy-start | bytes 6291460
  16.8 20.3 %copy-start.13 = (s32[8]{0:T(128)S(1)}, s32[8]{0:T(128)}, u32[]{:S(2)}) copy-start(s32[8]{0:T(128)} %lengths.11) | copy-start | bytes 100
  31.8 2.0 %copy-start.2 = (f32[8,2,128,512]{3,2,1,0:T(8,128)}, f32[8,2,128,512]{3,2,1,0:T(8,128)S(1)}, u32[]{:S(2)}) copy-start(f32[8,2,128,512]{3,2,1,0:T(8,128)S(1)} %get-tuple-element.57.refs_10_) | copy-start | bytes 12582916
  33.8 2.0 %collective-permute-start.6 = (bf16[1024,128]{1,0:T(8,128)(2,1)}, bf16[1024,128]{1,0:T(8,128)(2,1)}, u32[]{:S(2)}, u32[]{:S(2)}) collective-permute-start(bf16[1024,128]{1,0:T(8,128)(2,1)} %bitcast.10.refs_0_), channel_id=1, source_target_pairs={{0,4},{4,0},{8,12},{12,8},{16,20},{20,16},{24,28},{28,24},{1,5},{5... | collective-permute-start | bytes 786440 | tf_op jit(solution)/shard_map/ppermute | solution.py:387
  34.2 1.7 %collective-permute-start.4 = (bf16[1024,128]{1,0:T(8,128)(2,1)S(1)}, bf16[1024,128]{1,0:T(8,128)(2,1)}, u32[]{:S(2)}, u32[]{:S(2)}) collective-permute-start(bf16[1024,128]{1,0:T(8,128)(2,1)S(1)} %collective-permute-done.refs_0_), channel_id=1, source_target_pairs={{0,4},{4,0},{8,12},{12,8},{16,20},{20,16},{24,28},{28,24},{1,5},{5... | collective-permute-start | bytes 786440 | tf_op jit(solution)/shard_map/ppermute | solution.py:386
  34.3 2.0 %collective-permute-start.5 = (bf16[1024,128]{1,0:T(8,128)(2,1)S(1)}, bf16[1024,128]{1,0:T(8,128)(2,1)}, u32[]{:S(2)}, u32[]{:S(2)}) collective-permute-start(bf16[1024,128]{1,0:T(8,128)(2,1)S(1)} %collective-permute-done.2.refs_2_), channel_id=1, source_target_pairs={{0,4},{4,0},{8,12},{12,8},{16,20},{20,16},{24,28},{28,24},{1,5},{5... | collective-permute-start | bytes 786440 | tf_op jit(solution)/shard_map/ppermute | solution.py:386
  34.8 1.9 %collective-permute-start.7 = (bf16[128,1024]{1,0:T(8,128)(2,1)S(1)}, bf16[128,1024]{1,0:T(8,128)(2,1)}, u32[]{:S(2)}, u32[]{:S(2)}) collective-permute-start(bf16[128,1024]{1,0:T(8,128)(2,1)S(1)} %collective-permute-done.1.refs_5_), channel_id=1, source_target_pairs={{0,4},{4,0},{8,12},{12,8},{16,20},{20,16},{24,28},{28,24},{1,5},{5... | collective-permute-start | bytes 786440 | tf_op jit(solution)/shard_map/ppermute | solution.py:386
  34.9 2.2 %collective-permute-start.8 = (bf16[128,1024]{1,0:T(8,128)(2,1)S(1)}, bf16[128,1024]{1,0:T(8,128)(2,1)}, u32[]{:S(2)}, u32[]{:S(2)}) collective-permute-start(bf16[128,1024]{1,0:T(8,128)(2,1)S(1)} %collective-permute-done.3.refs_7_), channel_id=1, source_target_pairs={{0,4},{4,0},{8,12},{12,8},{16,20},{20,16},{24,28},{28,24},{1,5},{5... | collective-permute-start | bytes 786440 | tf_op jit(solution)/shard_map/ppermute | solution.py:386
  37.1 2.2 %copy-start = (bf16[1024,2048]{1,0:T(8,128)(2,1)S(1)}, bf16[1024,2048]{1,0:T(8,128)(2,1)}, u32[]{:S(2)}) copy-start(bf16[1024,2048]{1,0:T(8,128)(2,1)} %refs_13_.9) | copy-start | bytes 12582916
  39.3 2.2 %copy-start.3 = (f32[8,2,128,512]{3,2,1,0:T(8,128)S(1)}, f32[8,2,128,512]{3,2,1,0:T(8,128)}, u32[]{:S(2)}) copy-start(f32[8,2,128,512]{3,2,1,0:T(8,128)} %copy-done.2) | copy-start | bytes 12582916
  45.1 8.1 %collective-permute-start.10 = (bf16[128,1024]{1,0:T(8,128)(2,1)S(1)}, bf16[128,1024]{1,0:T(8,128)(2,1)S(1)}, u32[]{:S(2)}, u32[]{:S(2)}) collective-permute-start(bf16[128,1024]{1,0:T(8,128)(2,1)S(1)} %get-tuple-element.63), channel_id=1, source_target_pairs={{0,1},{1,0},{2,3},{3,2},{4,5},{5,4},{6,7},{7,6},{8,9},{9,8},{10,11... | collective-permute-start | bytes 786440 | tf_op jit(solution)/shard_map/ppermute | solution.py:405
  51.5 1.0 copy-start.10
  53.3 0.8 copy-start.15
  54.8 15.2 %collective-permute-start.11 = (bf16[256,1024]{1,0:T(8,128)(2,1)}, bf16[256,1024]{1,0:T(8,128)(2,1)}, u32[]{:S(2)}, u32[]{:S(2)}) collective-permute-start(bf16[256,1024]{1,0:T(8,128)(2,1)} %get-tuple-element.70), channel_id=1, source_target_pairs={{0,1},{1,0},{2,3},{3,2},{4,5},{5,4},{6,7},{7,6},{8,9},{9,8},{10,11... | collective-permute-start | bytes 1572872 | tf_op jit(solution)/shard_map/ppermute | solution.py:405
  56.5 13.4 %collective-permute-start.12 = (bf16[128,512]{1,0:T(8,128)(2,1)}, bf16[128,512]{1,0:T(8,128)(2,1)S(1)}, u32[]{:S(2)}, u32[]{:S(2)}) collective-permute-start(bf16[128,512]{1,0:T(8,128)(2,1)} %slice.74), channel_id=1, source_target_pairs={{0,2},{1,3},{2,0},{3,1},{4,6},{5,7},{6,4},{7,5},{8,10},{9,11},{10,... | collective-permute-start | bytes 393224 | tf_op jit(solution)/shard_map/ppermute | solution.py:406
  59.1 2.2 %copy-start.4 = (f32[8,2,128,512]{3,2,1,0:T(8,128)S(1)}, f32[8,2,128,512]{3,2,1,0:T(8,128)}, u32[]{:S(2)}) copy-start(f32[8,2,128,512]{3,2,1,0:T(8,128)} %copy-done.2) | copy-start | bytes 12582916
  61.2 8.7 %copy-start.11 = (f32[256,1024]{1,0:T(8,128)S(1)}, f32[256,1024]{1,0:T(8,128)}, u32[]{:S(2)}) copy-start(f32[256,1024]{1,0:T(8,128)} %copy-done.10) | copy-start | bytes 3145732
  65.9 1.0 copy-start.8
  69.9 3.0 %copy-start.16 = (bf16[128,512]{1,0:T(8,128)(2,1)}, bf16[128,512]{1,0:T(8,128)(2,1)S(1)}, u32[]{:S(2)}) copy-start(bf16[128,512]{1,0:T(8,128)(2,1)S(1)} %collective-permute-done.12) | copy-start | bytes 393220
  71.2 1.0 copy-start.14
  72.9 18.7 %collective-permute-start.13 = (bf16[256,1024]{1,0:T(8,128)(2,1)}, bf16[256,1024]{1,0:T(8,128)(2,1)}, u32[]{:S(2)}, u32[]{:S(2)}) collective-permute-start(bf16[256,1024]{1,0:T(8,128)(2,1)} %get-tuple-element.79), channel_id=1, source_target_pairs={{0,1},{1,0},{2,3},{3,2},{4,5},{5,4},{6,7},{7,6},{8,9},{9,8},{10,11... | collective-permute-start | bytes 1572872 | tf_op jit(solution)/shard_map/ppermute | solution.py:405
  75.2 16.2 %collective-permute-start.14 = (bf16[256,512]{1,0:T(8,128)(2,1)}, bf16[256,512]{1,0:T(8,128)(2,1)S(1)}, u32[]{:S(2)}, u32[]{:S(2)}) collective-permute-start(bf16[256,512]{1,0:T(8,128)(2,1)} %slice.72), channel_id=1, source_target_pairs={{0,2},{1,3},{2,0},{3,1},{4,6},{5,7},{6,4},{7,5},{8,10},{9,11},{10,... | collective-permute-start | bytes 786440 | tf_op jit(solution)/shard_map/ppermute | solution.py:406
  78.3 2.2 %copy-start.5 = (f32[8,2,128,512]{3,2,1,0:T(8,128)S(1)}, f32[8,2,128,512]{3,2,1,0:T(8,128)}, u32[]{:S(2)}) copy-start(f32[8,2,128,512]{3,2,1,0:T(8,128)} %copy-done.2) | copy-start | bytes 12582916
  80.5 11.1 %copy-start.9 = (f32[256,1024]{1,0:T(8,128)S(1)}, f32[256,1024]{1,0:T(8,128)}, u32[]{:S(2)}) copy-start(f32[256,1024]{1,0:T(8,128)} %copy-done.8) | copy-start | bytes 3145732
  80.5 17.0 %slice-start.1 = ((f32[128,1024]{1,0:T(8,128)}), f32[128,512]{1,0:T(8,128)S(1)}, s32[]{:S(2)}) async-start(f32[128,1024]{1,0:T(8,128)} %copy-done.15), calls=%async_computation.1 | async-start | bytes 524288 | tf_op jit(solution)/shard_map/slice | solution.py:395
  80.5 17.0 %copy-start.17 = (bf16[128,512]{1,0:T(8,128)(2,1)S(1)}, bf16[128,512]{1,0:T(8,128)(2,1)}, u32[]{:S(2)}) copy-start(bf16[128,512]{1,0:T(8,128)(2,1)} %copy-done.16) | copy-start | bytes 393220
  84.9 15.2 %copy-start.1 = (bf16[1024,2048]{1,0:T(8,128)(2,1)S(1)}, bf16[1024,2048]{1,0:T(8,128)(2,1)}, u32[]{:S(2)}) copy-start(bf16[1024,2048]{1,0:T(8,128)(2,1)} %refs_13_.9) | copy-start | bytes 12582916
  92.9 22.8 %collective-permute-start.15 = (bf16[256,1024]{1,0:T(8,128)(2,1)S(1)}, bf16[256,1024]{1,0:T(8,128)(2,1)S(1)}, u32[]{:S(2)}, u32[]{:S(2)}) collective-permute-start(bf16[256,1024]{1,0:T(8,128)(2,1)S(1)} %get-tuple-element.88), channel_id=1, source_target_pairs={{0,1},{1,0},{2,3},{3,2},{4,5},{5,4},{6,7},{7,6},{8,9},{9,8},{10,11... | collective-permute-start | bytes 1572872 | tf_op jit(solution)/shard_map/ppermute | solution.py:405
  97.6 6.2 %slice-start = ((f32[256,1024]{1,0:T(8,128)}), f32[256,512]{1,0:T(8,128)S(1)}, s32[]{:S(2)}) async-start(f32[256,1024]{1,0:T(8,128)} %copy-done.14), calls=%async_computation | async-start | bytes 1048576 | tf_op jit(solution)/shard_map/slice | solution.py:395
  97.6 17.4 %collective-permute-start.16 = (bf16[256,512]{1,0:T(8,128)(2,1)S(1)}, bf16[256,512]{1,0:T(8,128)(2,1)S(1)}, u32[]{:S(2)}, u32[]{:S(2)}) collective-permute-start(bf16[256,512]{1,0:T(8,128)(2,1)S(1)} %slice.71), channel_id=1, source_target_pairs={{0,2},{1,3},{2,0},{3,1},{4,6},{5,7},{6,4},{7,5},{8,10},{9,11},{10,... | collective-permute-start | bytes 786440 | tf_op jit(solution)/shard_map/ppermute | solution.py:406
  115.8 13.0 %collective-permute-start.18 = (bf16[128,1024]{1,0:T(8,128)(2,1)S(1)}, bf16[128,1024]{1,0:T(8,128)(2,1)S(1)}, u32[]{:S(2)}, u32[]{:S(2)}) collective-permute-start(bf16[128,1024]{1,0:T(8,128)(2,1)S(1)} %get-tuple-element.94), channel_id=1, source_target_pairs={{0,1},{1,0},{2,3},{3,2},{4,5},{5,4},{6,7},{7,6},{8,9},{9,8},{10,11... | collective-permute-start | bytes 786440 | tf_op jit(solution)/shard_map/ppermute | solution.py:415
  118.1 17.9 %collective-permute-start.17 = (bf16[256,512]{1,0:T(8,128)(2,1)S(1)}, bf16[256,512]{1,0:T(8,128)(2,1)S(1)}, u32[]{:S(2)}, u32[]{:S(2)}) collective-permute-start(bf16[256,512]{1,0:T(8,128)(2,1)S(1)} %slice.70), channel_id=1, source_target_pairs={{0,2},{1,3},{2,0},{3,1},{4,6},{5,7},{6,4},{7,5},{8,10},{9,11},{10,... | collective-permute-start | bytes 786440 | tf_op jit(solution)/shard_map/ppermute | solution.py:417
  128.9 9.1 %collective-permute-start.19 = (bf16[128,512]{1,0:T(8,128)(2,1)S(1)}, bf16[128,512]{1,0:T(8,128)(2,1)S(1)}, u32[]{:S(2)}, u32[]{:S(2)}) collective-permute-start(bf16[128,512]{1,0:T(8,128)(2,1)S(1)} %slice.73), channel_id=1, source_target_pairs={{0,2},{1,3},{2,0},{3,1},{4,6},{5,7},{6,4},{7,5},{8,10},{9,11},{10,... | collective-permute-start | bytes 393224 | tf_op jit(solution)/shard_map/ppermute | solution.py:419
  136.1 1.9 %copy-start.18 = (bf16[1024,512]{1,0:T(8,128)(2,1)}, bf16[1024,512]{1,0:T(8,128)(2,1)S(1)}, u32[]{:S(2)}) copy-start(bf16[1024,512]{1,0:T(8,128)(2,1)S(1)} %fusion.3) | copy-start | bytes 3145732

commit v3 on v2

--- a/solution.py
+++ b/solution.py
@@ -12,25 +12,26 @@
 SAFE_TOTAL = 2.0**100
 KEY_TILE = 512
 EDGE_TILE = 256
+VMEM_BYTES = 60 * 2**20
 SUB = 128
 PAIR = 4
 FIRST_PARTS = 4
-PARTS = (1, 2, 2, 2, 1)
+PARTS = (2, 2, 2, 2)
 
 
 def attend_kernel(
     place, lengths, tasks, q_ref, *refs, slots, subs, q_block, key_tile, edge_tile, resume
 ):
-    key_refs, value_refs, refs = refs[:slots], refs[slots : 2 * slots], refs[2 * slots :]
+    kv_refs, refs = refs[:slots], refs[slots:]
     if resume:
         states, w_ref, refs = refs[:3], refs[3], refs[4:]
-        sent_ref, kept_ref, q_buf, key_all, value_all, acc, peak, total = refs[:8]
-        s_buf, p_buf, rescale_buf, sems, w_buf, attended, w_sems = refs[8:]
+        sent_ref, pass_ref, keep_ref, q_buf, kv_all, acc, peak, total = refs[:8]
+        s_buf, p_buf, v_buf, rescale_buf, sems, w_buf, attended, w_sems = refs[8:]
     else:
         outs, refs = refs[:3], refs[3:]
-        q_buf, key_all, value_all, acc, peak, total, s_buf, p_buf, rescale_buf, sems = refs
+        q_buf, kv_all, acc, peak, total, s_buf, p_buf, v_buf, rescale_buf, sems = refs
     heads, _, width = q_ref.shape
-    shard_rows = key_refs[0].shape[0]
+    shard_rows = kv_refs[0].shape[1]
     groups = heads // PAIR
     units = subs * groups
     cols = PAIR * SUB
@@ -43,16 +44,13 @@
     local_row = place[4] + step_id * rows
 
     q_copy = pltpu.make_async_copy(
-        q_ref.at[:, pl.ds(pl.multiple_of(local_row, SUB), rows), :], q_buf, sems.at[2 * slots]
+        q_ref.at[:, pl.ds(pl.multiple_of(local_row, SUB), rows), :], q_buf, sems.at[slots]
     )
     q_copy.start()
     copies = []
     for at in range(slots):
         slot = at if at == slots - 1 else at // 2 * 2 + (parity if at % 2 == 0 else 1 - parity)
-        copies.append(pltpu.make_async_copy(key_refs[at], key_all.at[slot], sems.at[2 * at]))
-        copies.append(
-            pltpu.make_async_copy(value_refs[at], value_all.at[slot], sems.at[2 * at + 1])
-        )
+        copies.append(pltpu.make_async_copy(kv_refs[at], kv_all.at[slot], sems.at[at]))
 
     def fetch():
         for copy in copies:
@@ -67,7 +65,7 @@
         sub_row = local_row // SUB
         state_copies = [
             pltpu.make_async_copy(
-                state.at[pl.ds(sub_row, subs)], ref, sems.at[2 * slots + 1 + at]
+                state.at[pl.ds(sub_row, subs)], ref, sems.at[slots + 1 + at]
             )
             for at, (state, ref) in enumerate(zip(states, (acc, peak, total)))
         ]
@@ -82,8 +80,6 @@
                     w_ref.at[:, pl.ds(column, out_cols)], w_buf.at[at], w_sems.at[at]
                 )
             )
-        for copy in w_copies:
-            copy.start()
     else:
         pl.when(step_id == 0)(fetch)
 
@@ -141,6 +137,8 @@
         for copy in state_copies:
             copy.wait()
         wait()
+        for copy in w_copies:
+            copy.start()
     else:
         acc[...] = jnp.zeros_like(acc)
         peak[...] = jnp.full_like(peak, FLOOR_SCORE)
@@ -153,11 +151,11 @@
 
         def keys_of(tile):
             offset = pl.multiple_of((tile % per_shard) * size, size)
-            return key_all[tile // per_shard, pl.ds(offset, size), :]
+            return kv_all[tile // per_shard, 0, pl.ds(offset, size), :]
 
         def values_of(tile):
             offset = pl.multiple_of((tile % per_shard) * size, size)
-            values = value_all[tile // per_shard, :, pl.ds(offset, size)]
+            values = kv_all[tile // per_shard, 1, pl.ds(offset, size), :].T
             return jnp.concatenate([values, jnp.ones((16, size), jnp.bfloat16)], axis=0)
 
         def scores_of(keys, unit):
@@ -212,11 +210,11 @@
                 if waiting is not None:
                     gather(values, unit - 1, *waiting)
                 else:
-                    earlier = values_of(tile_of(jnp.maximum(turn - 1, 0)))
-                    gather(earlier, units - 1, p_buf[:size], rescale_buf[...])
+                    gather(v_buf[:, :size], units - 1, p_buf[:size], rescale_buf[...])
                 waiting = weights, rescale
                 scores = ahead
             s_buf[:size] = scores
+            v_buf[:, :size] = values
             p_buf[:size] = waiting[0]
             if not fixed:
                 rescale_buf[...] = waiting[1]
@@ -225,9 +223,10 @@
         def whole():
             p_buf[:size] = jnp.zeros((size, cols), jnp.bfloat16)
             rescale_buf[...] = jnp.ones_like(rescale_buf)
+            v_buf[:, :size] = jnp.zeros((width + 16, size), jnp.bfloat16)
             s_buf[:size] = scores_of(keys_of(tile_of(0)), 0)
             lax.fori_loop(0, count, step, 0)
-            gather(values_of(tile_of(count - 1)), units - 1, p_buf[:size], rescale_buf[...])
+            gather(v_buf[:, :size], units - 1, p_buf[:size], rescale_buf[...])
 
         pl.when(count > 0)(whole)
 
@@ -272,37 +271,41 @@
     for at in range(4):
         w_copies[at].wait()
         product = jnp.dot(attended[...], w_buf[at], preferred_element_type=jnp.float32)
-        ref = sent_ref if at < 2 else kept_ref
-        column = (at % 2) * out_cols
-        ref[:, column : column + out_cols] = product.astype(ref.dtype)
+        if at < 2:
+            sent_ref[:, at * out_cols : (at + 1) * out_cols] = product.astype(jnp.bfloat16)
+        elif at == 2:
+            pass_ref[...] = product
+        else:
+            keep_ref[...] = product
 
 
 def attend(place, lengths, tasks, queries, kvs, subs, q_block, states=None, w_out=None, out_cols=0):
     heads, tok_dev, width = queries.shape
-    shard_rows = kvs[0][0].shape[0]
+    shard_rows = kvs[0].shape[1]
     slots = len(kvs)
     key_tile = min(KEY_TILE, shard_rows)
     edge_tile = min(EDGE_TILE, key_tile)
     resume = states is not None
     groups, cols, rows = heads // PAIR, PAIR * SUB, subs * SUB
     state_shapes = [(groups, width, cols), (groups, 1, cols), (groups, 1, cols)]
-    hbm = pl.BlockSpec(memory_space=pl.ANY)
+    hbm = pl.BlockSpec(memory_space=pltpu.HBM)
     scratch = [
         pltpu.VMEM((heads, rows, width), jnp.bfloat16),
-        pltpu.VMEM((slots, shard_rows, width), jnp.bfloat16),
-        pltpu.VMEM((slots, width, shard_rows), jnp.bfloat16),
+        pltpu.VMEM((slots, 2, shard_rows, width), jnp.bfloat16),
         *[pltpu.VMEM((subs,) + shape, jnp.float32) for shape in state_shapes],
         pltpu.VMEM((key_tile, cols), jnp.float32),
         pltpu.VMEM((key_tile, cols), jnp.bfloat16),
+        pltpu.VMEM((width + 16, key_tile), jnp.bfloat16),
         pltpu.VMEM((1, cols), jnp.float32),
-        pltpu.SemaphoreType.DMA((2 * slots + 4,)),
+        pltpu.SemaphoreType.DMA((slots + 4,)),
     ]
     if resume:
         extra = [*states, w_out]
-        out_specs = [pl.BlockSpec((rows, 2 * out_cols), lambda i, *_: (0, 0))] * 2
+        out_specs = [pl.BlockSpec((rows, n * out_cols), lambda i, *_: (0, 0)) for n in (2, 1, 1)]
         out_shape = [
             jax.ShapeDtypeStruct((rows, 2 * out_cols), jnp.bfloat16),
-            jax.ShapeDtypeStruct((rows, 2 * out_cols), jnp.float32),
+            jax.ShapeDtypeStruct((rows, out_cols), jnp.float32),
+            jax.ShapeDtypeStruct((rows, out_cols), jnp.float32),
         ]
         scratch += [
             pltpu.VMEM((4, heads * width, out_cols), jnp.bfloat16),
@@ -330,18 +333,18 @@
         grid_spec=pltpu.PrefetchScalarGridSpec(
             num_scalar_prefetch=3,
             grid=(1 if resume else tok_dev // rows,),
-            in_specs=[hbm] * (1 + 2 * slots + len(extra)),
+            in_specs=[hbm] * (1 + slots + len(extra)),
             out_specs=out_specs,
             scratch_shapes=scratch,
         ),
         out_shape=out_shape,
-        compiler_params=pltpu.CompilerParams(vmem_limit_bytes=40 * 2**20),
+        compiler_params=pltpu.CompilerParams(vmem_limit_bytes=VMEM_BYTES),
         cost_estimate=pl.CostEstimate(
             flops=heads * rows * 4096 * width * 4,
             bytes_accessed=8 * 2**20,
             transcendentals=heads * rows * 4096,
         ),
-    )(place, lengths, tasks, queries, *[k for k, _ in kvs], *[v for _, v in kvs], *extra)
+    )(place, lengths, tasks, queries, *kvs, *extra)
 
 
 def local(queries, keys, values, doc_lengths, tasks, w_out):
@@ -358,11 +361,11 @@
     out_cols = w_out.shape[1] // n_head
     flat_tasks = tasks.reshape(-1)
 
-    own = keys[0], values[0].T
+    own = jnp.concatenate([keys, values], axis=0)
     spans = []
     for hop in range(back, 0, -1):
         pairs = [(i, i + 2 * hop) for i in range(n_tok - 2 * hop)]
-        spans.append(tuple(lax.ppermute(part, "tok", pairs) for part in own))
+        spans.append(lax.ppermute(own, "tok", pairs))
     swap = [(i, i ^ 1) for i in range(n_tok)]
 
     columns = [(z ^ 1) ^ 2, z ^ 1, z ^ 2, z]
@@ -383,41 +386,45 @@
     spans, states = lax.optimization_barrier((spans, states))
     kvs = []
     for mine in spans:
-        kvs += [mine, tuple(lax.ppermute(part, "tok", swap) for part in mine)]
-    kvs.append(tuple(lax.ppermute(part, "tok", swap) for part in own))
+        kvs += [mine, lax.ppermute(mine, "tok", swap)]
+    kvs.append(lax.ppermute(own, "tok", swap))
     base = (me // 2 - back) * 2 * tok_dev
 
     near = [(i, i ^ 1) for i in range(n_head)]
     far = [(i, i ^ 2) for i in range(n_head)]
 
-    def hop(kept, arrived):
-        summed = kept + arrived.astype(jnp.float32)
-        return summed[:, :out_cols].astype(jnp.bfloat16), summed[:, out_cols:]
-
-    halves = []
-    kept = sent = summed = None
+    def onward(passed, arrived):
+        return (passed + arrived[:, :out_cols].astype(jnp.float32)).astype(jnp.bfloat16)
+
+    terms = []
+    sent = passed = kept = other = held = None
     row = 0
     for part in PARTS:
         subs = tok_dev // SUB * part // sum(PARTS)
         place = placed(base, me * tok_dev - base, row)
         row += subs * SUB
-        place, sent, summed = lax.optimization_barrier((place, sent, summed))
+        place, sent, other = lax.optimization_barrier((place, sent, other))
         arrived = None if sent is None else lax.ppermute(sent, "head", near)
-        crossed = None if summed is None else lax.ppermute(summed[0], "head", far)
-        sent, kept_now = attend(
+        crossed = None if other is None else lax.ppermute(other, "head", far)
+        sent, passed_now, kept_now = attend(
             place, doc_lengths, flat_tasks, queries, kvs, subs, q_block, states, w_out, out_cols
         )
         sent, arrived, crossed = lax.optimization_barrier((sent, arrived, crossed))
         if crossed is not None:
-            halves.append((summed[1], crossed))
-        summed = None if arrived is None else hop(kept, arrived)
-        kept = kept_now
+            terms.append((*held, crossed))
+        if arrived is not None:
+            other, held = onward(passed, arrived), (kept, arrived)
+        passed, kept = passed_now, kept_now
     arrived = lax.ppermute(sent, "head", near)
-    if summed is not None:
-        halves.append((summed[1], lax.ppermute(summed[0], "head", far)))
-    summed = hop(kept, arrived)
-    halves.append((summed[1], lax.ppermute(summed[0], "head", far)))
-    outs = [(held + crossed.astype(jnp.float32)).astype(jnp.bfloat16) for held, crossed in halves]
+    if other is not None:
+        terms.append((*held, lax.ppermute(other, "head", far)))
+    terms.append((kept, arrived, lax.ppermute(onward(passed, arrived), "head", far)))
+    outs = [
+        (kept + arrived[:, out_cols:].astype(jnp.float32) + crossed.astype(jnp.float32)).astype(
+            jnp.bfloat16
+        )
+        for kept, arrived, crossed in terms
+    ]
     return jnp.concatenate(outs, axis=0)
 
 

time: 140 us -> 135 us (0.964)
  the two profiles are of different devices: /device:TPU:0 before, /device:TPU:5 now
where the time goes in v3:
time: 135 us; the launch traced here: 134 us
  Pallas kernels  75.5 us (56%)
  waiting for transfers between devices  35.9 us (27%)
  starting transfers between devices  11.5 us (9%)
  local copies, waits for them, and re-layouts  7.58 us (6%)
  other arithmetic  2.83 us (2%)
    pallas_call x5, Pallas kernels, attend(): pl.pallas_call(partial(attend_kernel, slots=slots, subs=subs, q_block=q_b...  75.5 us
    ppermute x1, waiting for transfers between devices, local(): arrived = lax.ppermute(sent, 'head', near)  13 us
    ppermute x1, waiting for transfers between devices, local(): lax.ppermute(onward(passed, arrived), 'head', far)  11.7 us
    ppermute x2, starting transfers between devices, local(): spans.append(lax.ppermute(own, 'tok', pairs))  4.41 us
    ppermute x2, waiting for transfers between devices, local(): crossed = None if other is None else lax.ppermute(other, 'head', far)  4.1 us
    ppermute x3, waiting for transfers between devices, local(): arrived = None if sent is None else lax.ppermute(sent, 'head', near)  3.55 us
    another operation x5, local copies, waits for them, and re-layouts, placed(): return jnp.stack([jnp.asarray(n, jnp.int32) for n in numbers])  3.15 us
    ppermute x3, starting transfers between devices, local(): arrived = None if sent is None else lax.ppermute(sent, 'head', near)  2.96 us
  transfers between devices with their start and end apart: 13, of which 7 were waited for; matrix products, arithmetic and copies ran while one was open for 5% of the time, Pallas kernels for 45%

profile of v3, /device:TPU:5, one launch (start us, length us, event | category | flops | bytes accessed | tf_op | source)
XLA Modules:
  0.0 133.6 jit_solution(2779225634837674663)
XLA Ops:
  0.0 1.0 constant_dynamic-update-slice_fusion.1
  1.0 1.0 constant_dynamic-update-slice_fusion.refs_0_
  2.0 0.0 copy-start.7
  2.0 3.1 %collective-permute-start.1 = (bf16[2,1024,128]{2,1,0:T(8,128)(2,1)S(1)}, bf16[2,1024,128]{2,1,0:T(8,128)(2,1)S(1)}, u32[]{:S(2)}, u32[]{:S(2)}) collective-permute-start(bf16[2,1024,128]{2,1,0:T(8,128)(2,1)S(1)} %constant_dynamic-update-slice_fusion.refs_0_), channel_id=1, source_target_pairs={{0,8},{4,12},{8,16},{12,20},{16,24},{20,28},{1,9},{5,13},{9,17},{1... | collective-permute-start | bytes 1572872 | tf_op jit(solution)/shard_map/ppermute | solution.py:368
  5.1 1.3 collective-permute-start
  6.4 1.0 collective-permute-start.4
  7.4 0.8 copy.7
  8.2 0.8 reshape.3.tasks
  9.0 0.6 stack.41.place
  9.6 17.7 %shard_map.64 = (f32[8,2,128,512]{3,2,1,0:T(8,128)}, f32[8,2,1,512]{3,2,1,0:T(1,128)}, f32[8,2,1,512]{3,2,1,0:T(1,128)}) custom-call(s32[9]{0:T(128)} %stack.41.place, s32[8]{0:T(128)} %lengths.9, s32[640]{0:T(1024)} %reshape.3.tasks, bf16[8,1024,128]{2,1,0:T(8,128)(2,1)} %q_ref.9, bf16[2,1024,128]{2,1,0:T(8,128)(2,1)} %copy-done.7), custom_call_target="tpu_custom_call" | custom-call | flops 4294967296 | bytes 8388608 | tf_op jit(solution)/shard_map/pallas_call | solution.py:323
  27.3 0.0 collective-permute-done.1.refs_2_
  27.3 2.5 %collective-permute-done.refs_0_ = bf16[2,1024,128]{2,1,0:T(8,128)(2,1)S(1)} collective-permute-done((bf16[2,1024,128]{2,1,0:T(8,128)(2,1)S(1)}, bf16[2,1024,128]{2,1,0:T(8,128)(2,1)S(1)}, u32[]{:S(2)}, u32[]{:S(2)}) %collective-permute-start) | collective-permute-done | bytes 524320 | tf_op jit(solution)/shard_map/ppermute | solution.py:368
  29.8 0.5 collective-permute-start.2
  30.3 0.0 collective-permute-start.3
  30.4 0.7 stack.40.place
  31.0 0.6 stack.43.place
  31.6 0.0 collective-permute-done.4.refs_4_
  31.6 0.3 collective-permute-done.2.refs_1_
  31.9 0.7 collective-permute-done.3.refs_3_
  32.6 0.1 copy-done.11
  32.7 0.8 copy-done.12
  33.5 15.8 %shard_map.65 = (bf16[256,1024]{1,0:T(8,128)(2,1)}, f32[256,512]{1,0:T(8,128)}, f32[256,512]{1,0:T(8,128)}) custom-call(s32[9]{0:T(128)} %stack.40.place, s32[8]{0:T(128)} %lengths.9, s32[640]{0:T(1024)} %reshape.3.tasks, bf16[8,1024,128]{2,1,0:T(8,128)(2,1)} %q_ref.9, bf16[2,1024,128]{2,1,0:T(8,128)(2,1)} %copy-done.9, bf16[2,1024,128]{2,1,0:T(8,128)(2,1)} %copy-done.11, ...), custom_call_target="tpu_custom_call" | custom-call | flops 4294967296 | bytes 8388608 | tf_op jit(solution)/shard_map/pallas_call | solution.py:323
  49.3 1.4 %collective-permute-start.5 = (bf16[256,1024]{1,0:T(8,128)(2,1)}, bf16[256,1024]{1,0:T(8,128)(2,1)S(1)}, u32[]{:S(2)}, u32[]{:S(2)}) collective-permute-start(bf16[256,1024]{1,0:T(8,128)(2,1)} %get-tuple-element.53), channel_id=1, source_target_pairs={{0,1},{1,0},{2,3},{3,2},{4,5},{5,4},{6,7},{7,6},{8,9},{9,8},{10,11... | collective-permute-start | bytes 1572872 | tf_op jit(solution)/shard_map/ppermute | solution.py:407
  50.7 0.7 stack.89.place
  51.3 16.1 %shard_map.66 = (bf16[256,1024]{1,0:T(8,128)(2,1)}, f32[256,512]{1,0:T(8,128)}, f32[256,512]{1,0:T(8,128)}) custom-call(s32[9]{0:T(128)} %stack.43.place, s32[8]{0:T(128)} %lengths.9, s32[640]{0:T(1024)} %reshape.3.tasks, bf16[8,1024,128]{2,1,0:T(8,128)(2,1)} %q_ref.9, bf16[2,1024,128]{2,1,0:T(8,128)(2,1)} %copy-done.9, bf16[2,1024,128]{2,1,0:T(8,128)(2,1)} %copy-done.11, ...), custom_call_target="tpu_custom_call" | custom-call | flops 4294967296 | bytes 8388608 | tf_op jit(solution)/shard_map/pallas_call | solution.py:323
  67.4 0.0 collective-permute-done.5
  67.5 0.1 add_convert_fusion.7
  67.5 0.2 collective-permute-start.6
  67.8 0.6 stack.91.place
  68.4 2.3 %collective-permute-start.7 = (bf16[256,512]{1,0:T(8,128)(2,1)S(1)}, bf16[256,512]{1,0:T(8,128)(2,1)S(1)}, u32[]{:S(2)}, u32[]{:S(2)}) collective-permute-start(bf16[256,512]{1,0:T(8,128)(2,1)S(1)} %add_convert_fusion.7), channel_id=1, source_target_pairs={{0,2},{1,3},{2,0},{3,1},{4,6},{5,7},{6,4},{7,5},{8,10},{9,11},{10,... | collective-permute-start | bytes 786440 | tf_op jit(solution)/shard_map/ppermute | solution.py:408
  70.7 19.1 %shard_map.67 = (bf16[256,1024]{1,0:T(8,128)(2,1)}, f32[256,512]{1,0:T(8,128)}, f32[256,512]{1,0:T(8,128)}) custom-call(s32[9]{0:T(128)} %stack.89.place, s32[8]{0:T(128)} %lengths.9, s32[640]{0:T(1024)} %reshape.3.tasks, bf16[8,1024,128]{2,1,0:T(8,128)(2,1)} %q_ref.9, bf16[2,1024,128]{2,1,0:T(8,128)(2,1)} %copy-done.9, bf16[2,1024,128]{2,1,0:T(8,128)(2,1)} %copy-done.11, ...), custom_call_target="tpu_custom_call" | custom-call | flops 4294967296 | bytes 8388608 | tf_op jit(solution)/shard_map/pallas_call | solution.py:323
  89.8 0.0 collective-permute-done.7
  89.9 0.1 add_convert_fusion.5
  90.0 1.4 %collective-permute-start.8 = (bf16[256,1024]{1,0:T(8,128)(2,1)}, bf16[256,1024]{1,0:T(8,128)(2,1)S(1)}, u32[]{:S(2)}, u32[]{:S(2)}) collective-permute-start(bf16[256,1024]{1,0:T(8,128)(2,1)} %get-tuple-element.68), channel_id=1, source_target_pairs={{0,1},{1,0},{2,3},{3,2},{4,5},{5,4},{6,7},{7,6},{8,9},{9,8},{10,11... | collective-permute-start | bytes 1572872 | tf_op jit(solution)/shard_map/ppermute | solution.py:407
  91.3 0.2 collective-permute-start.9
  91.5 6.8 %shard_map.68 = (bf16[256,1024]{1,0:T(8,128)(2,1)}, f32[256,512]{1,0:T(8,128)}, f32[256,512]{1,0:T(8,128)}) custom-call(s32[9]{0:T(128)} %stack.91.place, s32[8]{0:T(128)} %lengths.9, s32[640]{0:T(1024)} %reshape.3.tasks, bf16[8,1024,128]{2,1,0:T(8,128)(2,1)} %q_ref.9, bf16[2,1024,128]{2,1,0:T(8,128)(2,1)} %copy-done.9, bf16[2,1024,128]{2,1,0:T(8,128)(2,1)} %copy-done.11, ...), custom_call_target="tpu_custom_call" | custom-call | flops 4294967296 | bytes 8388608 | tf_op jit(solution)/shard_map/pallas_call | solution.py:323
  98.4 4.1 %collective-permute-done.9 = bf16[256,512]{1,0:T(8,128)(2,1)S(1)} collective-permute-done((bf16[256,512]{1,0:T(8,128)(2,1)S(1)}, bf16[256,512]{1,0:T(8,128)(2,1)S(1)}, u32[]{:S(2)}, u32[]{:S(2)}) %collective-permute-start.9) | collective-permute-done | bytes 262176 | tf_op jit(solution)/shard_map/ppermute | solution.py:408
  102.5 3.5 %collective-permute-done.8 = bf16[256,1024]{1,0:T(8,128)(2,1)S(1)} collective-permute-done((bf16[256,1024]{1,0:T(8,128)(2,1)}, bf16[256,1024]{1,0:T(8,128)(2,1)S(1)}, u32[]{:S(2)}, u32[]{:S(2)}) %collective-permute-start.8) | collective-permute-done | bytes 524320 | tf_op jit(solution)/shard_map/ppermute | solution.py:407
  106.0 0.1 add_convert_fusion.3
  106.1 0.1 collective-permute-start.10
  106.2 13.0 %collective-permute-done.11 = bf16[256,1024]{1,0:T(8,128)(2,1)S(1)} collective-permute-done((bf16[256,1024]{1,0:T(8,128)(2,1)}, bf16[256,1024]{1,0:T(8,128)(2,1)S(1)}, u32[]{:S(2)}, u32[]{:S(2)}) %collective-permute-start.11) | collective-permute-done | bytes 524320 | tf_op jit(solution)/shard_map/ppermute | solution.py:418
  119.2 1.1 add_convert_fusion.1
  120.4 0.1 collective-permute-start.12
  120.5 0.2 add_convert_fusion.4
  120.7 0.1 add_convert_fusion.2
  120.8 11.7 %collective-permute-done.12 = bf16[256,512]{1,0:T(8,128)(2,1)S(1)} collective-permute-done((bf16[256,512]{1,0:T(8,128)(2,1)S(1)}, bf16[256,512]{1,0:T(8,128)(2,1)S(1)}, u32[]{:S(2)}, u32[]{:S(2)}) %collective-permute-start.12) | collective-permute-done | bytes 262176 | tf_op jit(solution)/shard_map/ppermute | solution.py:421
  132.5 0.1 add_convert_fusion
  132.6 1.0 pad_maximum_fusion
  (26 shorter events, 0.1 us)
Async XLA Ops:
  2.0 7.6 %copy-start.7 = (bf16[2,1024,128]{2,1,0:T(8,128)(2,1)}, bf16[2,1024,128]{2,1,0:T(8,128)(2,1)S(1)}, u32[]{:S(2)}) copy-start(bf16[2,1024,128]{2,1,0:T(8,128)(2,1)S(1)} %constant_dynamic-update-slice_fusion.refs_0_) | copy-start | bytes 1572868
  2.0 25.3 %collective-permute-start.1 = (bf16[2,1024,128]{2,1,0:T(8,128)(2,1)S(1)}, bf16[2,1024,128]{2,1,0:T(8,128)(2,1)S(1)}, u32[]{:S(2)}, u32[]{:S(2)}) collective-permute-start(bf16[2,1024,128]{2,1,0:T(8,128)(2,1)S(1)} %constant_dynamic-update-slice_fusion.refs_0_), channel_id=1, source_target_pairs={{0,8},{4,12},{8,16},{12,20},{16,24},{20,28},{1,9},{5,13},{9,17},{1... | collective-permute-start | bytes 1572872 | tf_op jit(solution)/shard_map/ppermute | solution.py:368
  5.1 24.7 %collective-permute-start = (bf16[2,1024,128]{2,1,0:T(8,128)(2,1)S(1)}, bf16[2,1024,128]{2,1,0:T(8,128)(2,1)S(1)}, u32[]{:S(2)}, u32[]{:S(2)}) collective-permute-start(bf16[2,1024,128]{2,1,0:T(8,128)(2,1)S(1)} %constant_dynamic-update-slice_fusion.refs_0_), channel_id=1, source_target_pairs={{0,16},{4,20},{8,24},{12,28},{1,17},{5,21},{9,25},{13,29},{2,18},{... | collective-permute-start | bytes 1572872 | tf_op jit(solution)/shard_map/ppermute | solution.py:368
  6.4 25.2 %collective-permute-start.4 = (bf16[2,1024,128]{2,1,0:T(8,128)(2,1)S(1)}, bf16[2,1024,128]{2,1,0:T(8,128)(2,1)S(1)}, u32[]{:S(2)}, u32[]{:S(2)}) collective-permute-start(bf16[2,1024,128]{2,1,0:T(8,128)(2,1)S(1)} %constant_dynamic-update-slice_fusion.refs_0_), channel_id=1, source_target_pairs={{0,4},{4,0},{8,12},{12,8},{16,20},{20,16},{24,28},{28,24},{1,5},{5... | collective-permute-start | bytes 1572872 | tf_op jit(solution)/shard_map/ppermute | solution.py:390
  27.3 5.3 %copy-start.8 = (bf16[2,1024,128]{2,1,0:T(8,128)(2,1)}, bf16[2,1024,128]{2,1,0:T(8,128)(2,1)S(1)}, u32[]{:S(2)}) copy-start(bf16[2,1024,128]{2,1,0:T(8,128)(2,1)S(1)} %collective-permute-done.1.refs_2_) | copy-start | bytes 1572868
  29.8 2.8 %copy-start.9 = (bf16[2,1024,128]{2,1,0:T(8,128)(2,1)}, bf16[2,1024,128]{2,1,0:T(8,128)(2,1)S(1)}, u32[]{:S(2)}) copy-start(bf16[2,1024,128]{2,1,0:T(8,128)(2,1)S(1)} %collective-permute-done.refs_0_) | copy-start | bytes 1572868
  29.8 2.0 %collective-permute-start.2 = (bf16[2,1024,128]{2,1,0:T(8,128)(2,1)S(1)}, bf16[2,1024,128]{2,1,0:T(8,128)(2,1)S(1)}, u32[]{:S(2)}, u32[]{:S(2)}) collective-permute-start(bf16[2,1024,128]{2,1,0:T(8,128)(2,1)S(1)} %collective-permute-done.refs_0_), channel_id=1, source_target_pairs={{0,4},{4,0},{8,12},{12,8},{16,20},{20,16},{24,28},{28,24},{1,5},{5... | collective-permute-start | bytes 1572872 | tf_op jit(solution)/shard_map/ppermute | solution.py:389
  30.3 2.3 %collective-permute-start.3 = (bf16[2,1024,128]{2,1,0:T(8,128)(2,1)S(1)}, bf16[2,1024,128]{2,1,0:T(8,128)(2,1)S(1)}, u32[]{:S(2)}, u32[]{:S(2)}) collective-permute-start(bf16[2,1024,128]{2,1,0:T(8,128)(2,1)S(1)} %collective-permute-done.1.refs_2_), channel_id=1, source_target_pairs={{0,4},{4,0},{8,12},{12,8},{16,20},{20,16},{24,28},{28,24},{1,5},{5... | collective-permute-start | bytes 1572872 | tf_op jit(solution)/shard_map/ppermute | solution.py:389
  31.6 1.0 copy-start.10
  31.9 0.8 copy-start.11
  32.7 0.8 copy-start.12
  49.3 18.1 %collective-permute-start.5 = (bf16[256,1024]{1,0:T(8,128)(2,1)}, bf16[256,1024]{1,0:T(8,128)(2,1)S(1)}, u32[]{:S(2)}, u32[]{:S(2)}) collective-permute-start(bf16[256,1024]{1,0:T(8,128)(2,1)} %get-tuple-element.53), channel_id=1, source_target_pairs={{0,1},{1,0},{2,3},{3,2},{4,5},{5,4},{6,7},{7,6},{8,9},{9,8},{10,11... | collective-permute-start | bytes 1572872 | tf_op jit(solution)/shard_map/ppermute | solution.py:407
  51.3 16.1 %copy-start.6 = (f32[256,512]{1,0:T(8,128)S(1)}, f32[256,512]{1,0:T(8,128)}, u32[]{:S(2)}) copy-start(f32[256,512]{1,0:T(8,128)} %get-tuple-element.56) | copy-start | bytes 1572868
  67.5 22.3 %collective-permute-start.6 = (bf16[256,1024]{1,0:T(8,128)(2,1)}, bf16[256,1024]{1,0:T(8,128)(2,1)S(1)}, u32[]{:S(2)}, u32[]{:S(2)}) collective-permute-start(bf16[256,1024]{1,0:T(8,128)(2,1)} %get-tuple-element.59), channel_id=1, source_target_pairs={{0,1},{1,0},{2,3},{3,2},{4,5},{5,4},{6,7},{7,6},{8,9},{9,8},{10,11... | collective-permute-start | bytes 1572872 | tf_op jit(solution)/shard_map/ppermute | solution.py:407
  68.4 21.4 %copy-start.5 = (f32[256,512]{1,0:T(8,128)S(1)}, f32[256,512]{1,0:T(8,128)}, u32[]{:S(2)}) copy-start(f32[256,512]{1,0:T(8,128)} %get-tuple-element.65) | copy-start | bytes 1572868
  68.4 21.4 %collective-permute-start.7 = (bf16[256,512]{1,0:T(8,128)(2,1)S(1)}, bf16[256,512]{1,0:T(8,128)(2,1)S(1)}, u32[]{:S(2)}, u32[]{:S(2)}) collective-permute-start(bf16[256,512]{1,0:T(8,128)(2,1)S(1)} %add_convert_fusion.7), channel_id=1, source_target_pairs={{0,2},{1,3},{2,0},{3,1},{4,6},{5,7},{6,4},{7,5},{8,10},{9,11},{10,... | collective-permute-start | bytes 786440 | tf_op jit(solution)/shard_map/ppermute | solution.py:408
  90.0 16.1 %copy-start.4 = (f32[256,512]{1,0:T(8,128)S(1)}, f32[256,512]{1,0:T(8,128)}, u32[]{:S(2)}) copy-start(f32[256,512]{1,0:T(8,128)} %get-tuple-element.73) | copy-start | bytes 1572868
  90.0 16.1 %collective-permute-start.8 = (bf16[256,1024]{1,0:T(8,128)(2,1)}, bf16[256,1024]{1,0:T(8,128)(2,1)S(1)}, u32[]{:S(2)}, u32[]{:S(2)}) collective-permute-start(bf16[256,1024]{1,0:T(8,128)(2,1)} %get-tuple-element.68), channel_id=1, source_target_pairs={{0,1},{1,0},{2,3},{3,2},{4,5},{5,4},{6,7},{7,6},{8,9},{9,8},{10,11... | collective-permute-start | bytes 1572872 | tf_op jit(solution)/shard_map/ppermute | solution.py:407
  91.3 11.2 %collective-permute-start.9 = (bf16[256,512]{1,0:T(8,128)(2,1)S(1)}, bf16[256,512]{1,0:T(8,128)(2,1)S(1)}, u32[]{:S(2)}, u32[]{:S(2)}) collective-permute-start(bf16[256,512]{1,0:T(8,128)(2,1)S(1)} %add_convert_fusion.5), channel_id=1, source_target_pairs={{0,2},{1,3},{2,0},{3,1},{4,6},{5,7},{6,4},{7,5},{8,10},{9,11},{10,... | collective-permute-start | bytes 786440 | tf_op jit(solution)/shard_map/ppermute | solution.py:408
  98.4 22.1 %copy-start = (f32[256,512]{1,0:T(8,128)S(1)}, f32[256,512]{1,0:T(8,128)}, u32[]{:S(2)}) copy-start(f32[256,512]{1,0:T(8,128)} %get-tuple-element.49) | copy-start | bytes 1572868
  98.4 22.1 %copy-start.1 = (f32[256,512]{1,0:T(8,128)S(1)}, f32[256,512]{1,0:T(8,128)}, u32[]{:S(2)}) copy-start(f32[256,512]{1,0:T(8,128)} %get-tuple-element.62) | copy-start | bytes 1572868
  106.0 13.2 %collective-permute-start.11 = (bf16[256,1024]{1,0:T(8,128)(2,1)}, bf16[256,1024]{1,0:T(8,128)(2,1)S(1)}, u32[]{:S(2)}, u32[]{:S(2)}) collective-permute-start(bf16[256,1024]{1,0:T(8,128)(2,1)} %get-tuple-element.75), channel_id=1, source_target_pairs={{0,1},{1,0},{2,3},{3,2},{4,5},{5,4},{6,7},{7,6},{8,9},{9,8},{10,11... | collective-permute-start | bytes 1572872 | tf_op jit(solution)/shard_map/ppermute | solution.py:418
  106.1 14.6 %copy-start.2 = (f32[256,512]{1,0:T(8,128)S(1)}, f32[256,512]{1,0:T(8,128)}, u32[]{:S(2)}) copy-start(f32[256,512]{1,0:T(8,128)} %get-tuple-element.71) | copy-start | bytes 1572868
  106.1 14.6 %collective-permute-start.10 = (bf16[256,512]{1,0:T(8,128)(2,1)S(1)}, bf16[256,512]{1,0:T(8,128)(2,1)S(1)}, u32[]{:S(2)}, u32[]{:S(2)}) collective-permute-start(bf16[256,512]{1,0:T(8,128)(2,1)S(1)} %add_convert_fusion.3), channel_id=1, source_target_pairs={{0,2},{1,3},{2,0},{3,1},{4,6},{5,7},{6,4},{7,5},{8,10},{9,11},{10,... | collective-permute-start | bytes 786440 | tf_op jit(solution)/shard_map/ppermute | solution.py:420
  120.4 12.1 %copy-start.3 = (f32[256,512]{1,0:T(8,128)S(1)}, f32[256,512]{1,0:T(8,128)}, u32[]{:S(2)}) copy-start(f32[256,512]{1,0:T(8,128)} %get-tuple-element.74) | copy-start | bytes 1572868
  120.4 12.1 %collective-permute-start.12 = (bf16[256,512]{1,0:T(8,128)(2,1)S(1)}, bf16[256,512]{1,0:T(8,128)(2,1)S(1)}, u32[]{:S(2)}, u32[]{:S(2)}) collective-permute-start(bf16[256,512]{1,0:T(8,128)(2,1)S(1)} %add_convert_fusion.1), channel_id=1, source_target_pairs={{0,2},{1,3},{2,0},{3,1},{4,6},{5,7},{6,4},{7,5},{8,10},{9,11},{10,... | collective-permute-start | bytes 786440 | tf_op jit(solution)/shard_map/ppermute | solution.py:421

commit v4 on v2

v4 whole, which is shorter than its diff:
```python
from functools import partial
import math

import jax
import jax.numpy as jnp
from jax import lax
from jax.experimental import pallas as pl
from jax.experimental.pallas import tpu as pltpu
from jax.sharding import PartitionSpec as P

FLOOR_SCORE = -1e30
SAFE_TOTAL = 2.0**100
KEY_TILE = 512
EDGE_TILE = 256
VMEM_BYTES = 40 * 2**20
SUB = 128
LAG = 2
PAIR = 4
PARTS = (1, 2, 2, 2, 1)


def attend_kernel(place, lengths, tasks, q_ref, *refs, slots, subs, q_block, key_tile, edge_tile):
    kv_refs, refs = refs[:slots], refs[slots:]
    out_ref, q_buf, kv_all, acc, peak, total, s_buf, p_buf, rescale_buf, sems = refs
    heads, _, width = q_ref.shape
    shard_rows = kv_refs[0].shape[1]
    groups = heads // PAIR
    units = subs * groups
    cols = PAIR * SUB
    rows = subs * SUB
    parity = place[0]
    first_row = place[1]
    base = place[2]
    q_copy = pltpu.make_async_copy(
        q_ref.at[:, pl.ds(pl.multiple_of(place[3], SUB), rows), :], q_buf, sems.at[slots]
    )
    q_copy.start()

    last_row = first_row + rows - 1
    one_head = [
        first_row + sub * SUB + lax.broadcasted_iota(jnp.int32, (1, SUB), 1) for sub in range(subs)
    ]
    begin = [jnp.zeros((1, SUB), jnp.int32)] * subs
    begin_first = jnp.int32(0)
    begin_last = jnp.int32(0)
    start = jnp.int32(0)
    for doc in range(lengths.shape[0]):
        begin = [
            jnp.where(one >= start, jnp.maximum(old, start), old)
            for one, old in zip(one_head, begin)
        ]
        begin_first = jnp.where(first_row >= start, jnp.maximum(begin_first, start), begin_first)
        begin_last = jnp.where(last_row >= start, jnp.maximum(begin_last, start), begin_last)
        start = start + lengths[doc]

    begins, ends, lows, highs = [], [], [], []
    for sub in range(subs):
        task = ((first_row + sub * SUB) // q_block) * heads
        low = [tasks[(task + head) * 5 + 2] * q_block for head in range(heads)]
        high = [tasks[(task + head) * 5 + 3] * q_block for head in range(heads)]
        for group in range(groups):
            members = range(group * PAIR, (group + 1) * PAIR)
            begins.append(
                jnp.concatenate([jnp.maximum(begin[sub], low[m]) for m in members], axis=1)
            )
            ends.append(
                jnp.concatenate([jnp.minimum(one_head[sub], high[m] - 1) for m in members], axis=1)
            )
        lows += low
        highs += high
    low_least, low_most, high_least, high_most = lows[0], lows[0], highs[0], highs[0]
    for low, high in zip(lows[1:], highs[1:]):
        low_least, low_most = jnp.minimum(low_least, low), jnp.maximum(low_most, low)
        high_least, high_most = jnp.minimum(high_least, high), jnp.maximum(high_most, high)

    ratio = key_tile // edge_tile
    tiles = slots * shard_rows // edge_tile
    lo = jnp.clip((jnp.maximum(low_least, begin_first) - base) // edge_tile, 0, tiles)
    hi = jnp.clip(
        (jnp.minimum(high_most, last_row + 1) - base + edge_tile - 1) // edge_tile, lo, tiles
    )
    full_lo = (jnp.maximum(low_most, begin_last) - base + key_tile - 1) // key_tile
    full_hi = (jnp.minimum(high_least, first_row + 1) - base) // key_tile
    full_lo = jnp.maximum(full_lo, 0)
    full_hi = jnp.minimum(full_hi, tiles // ratio)
    some = full_hi > full_lo
    inner_lo = jnp.where(some, full_lo * ratio, lo)
    inner_hi = jnp.where(some, full_hi * ratio, lo)
    factor = math.log2(math.e) / math.sqrt(width)

    def reset():
        acc[...] = jnp.zeros_like(acc)
        peak[...] = jnp.full_like(peak, FLOOR_SCORE)
        total[...] = jnp.zeros_like(total)

    per_slot = shard_rows // edge_tile
    early, late = [], []
    for at in range(slots):
        slot = at // 2 * 2 + (parity if at % 2 == 0 else 1 - parity)
        copy = pltpu.make_async_copy(kv_refs[at], kv_all.at[slot], sems.at[at])
        first, last = slot * per_slot, (slot + 1) * per_slot
        below = (lo < inner_lo) & (lo < last) & (inner_lo > first)
        above = (inner_hi < hi) & (inner_hi < last) & (hi > first)
        used = (lo < last) & (hi > first)
        early.append((below | above, copy))
        late.append((used & jnp.logical_not(below | above), copy))
    for needed, copy in early + late:
        pl.when(needed)(copy.start)

    def wait(copies):
        for needed, copy in copies:
            pl.when(needed)(copy.wait)

    reset()
    q_copy.wait()
    wait(early)

    def sweep(count, tile_of, size, masked, fixed):
        per_shard = shard_rows // size

        def keys_of(tile):
            offset = pl.multiple_of((tile % per_shard) * size, size)
            return kv_all[tile // per_shard, 0, pl.ds(offset, size), :]

        def values_of(tile):
            offset = pl.multiple_of((tile % per_shard) * size, size)
            values = kv_all[tile // per_shard, 1, pl.ds(offset, size), :]
            values = [values[at : at + width] for at in range(0, size, width)]
            values = jnp.concatenate(values, axis=1)
            return jnp.concatenate([values, jnp.ones((16, size), jnp.bfloat16)], axis=0)

        def scores_of(keys, unit):
            sub, group = divmod(unit, groups)
            asked = q_buf[group * PAIR : (group + 1) * PAIR, sub * SUB : (sub + 1) * SUB, :]
            return lax.dot_general(
                keys,
                asked.reshape(cols, width),
                (((1,), (1,)), ((), ())),
                preferred_element_type=jnp.float32,
            )

        def gather(values, unit, weights, rescale):
            at = divmod(unit, groups)
            product = lax.dot_general(
                values, weights, (((1,), (0,)), ((), ())), preferred_element_type=jnp.float32
            )
            if fixed:
                total[at] += product[width : width + 1]
                acc[at] += product[:width]
            else:
                total[at] = total[at] * rescale + product[width : width + 1]
                acc[at] = acc[at] * rescale + product[:width]

        def step(turn, carried):
            tile = tile_of(turn)
            keys, values = keys_of(tile), values_of(tile)
            key_pos = (
                base + tile * size + lax.broadcasted_iota(jnp.int32, (size, 1), 0)
                if masked
                else None
            )
            scores = s_buf[:size]
            waiting = None
            for unit in range(units):
                at = divmod(unit, groups)
                if unit + 1 < units:
                    ahead = scores_of(keys, unit + 1)
                else:
                    ahead = scores_of(keys_of(tile_of(jnp.minimum(turn + 1, count - 1))), 0)
                if masked:
                    visible = (key_pos >= begins[unit]) & (key_pos <= ends[unit])
                    scores = jnp.where(visible, scores, FLOOR_SCORE)
                before = peak[at]
                if fixed:
                    now, rescale = before, None
                else:
                    now = jnp.maximum(before, jnp.max(scores, axis=0, keepdims=True) * factor)
                    peak[at] = now
                    rescale = jnp.exp2(before - now)
                weights = jnp.exp2(scores * factor - now).astype(jnp.bfloat16)
                if waiting is not None:
                    gather(values, unit - 1, *waiting)
                else:
                    earlier = values_of(tile_of(jnp.maximum(turn - 1, 0)))
                    gather(earlier, units - 1, p_buf[:size], rescale_buf[...])
                waiting = weights, rescale
                scores = ahead
            s_buf[:size] = scores
            p_buf[:size] = waiting[0]
            if not fixed:
                rescale_buf[...] = waiting[1]
            return carried

        def whole():
            p_buf[:size] = jnp.zeros((size, cols), jnp.bfloat16)
            rescale_buf[...] = jnp.ones_like(rescale_buf)
            s_buf[:size] = scores_of(keys_of(tile_of(0)), 0)
            lax.fori_loop(0, count, step, 0)
            gather(values_of(tile_of(count - 1)), units - 1, p_buf[:size], rescale_buf[...])

        pl.when(count > 0)(whole)

    left = inner_lo - lo
    sweep(
        left + hi - inner_hi,
        lambda turn: jnp.where(turn < left, lo + turn, inner_hi + turn - left),
        edge_tile,
        True,
        False,
    )
    wait(late)
    sweep(
        (inner_hi - inner_lo) // ratio,
        lambda turn: inner_lo // ratio + turn,
        key_tile,
        False,
        True,
    )
    in_range = jnp.min(jnp.where(total[...] < SAFE_TOTAL, 1.0, 0.0))

    @pl.when(in_range < 0.5)
    def again():
        reset()
        sweep(hi - lo, lambda turn: lo + turn, edge_tile, True, False)

    for sub in range(subs):
        for group in range(groups):
            done = (acc[sub, group] * (1.0 / total[sub, group])).astype(jnp.bfloat16).T
            for member in range(PAIR):
                head = group * PAIR + member
                out_ref[sub * SUB : (sub + 1) * SUB, head * width : (head + 1) * width] = done[
                    member * SUB : (member + 1) * SUB
                ]


def attend(place, lengths, tasks, queries, kvs, subs, q_block):
    heads, _, width = queries.shape
    shard_rows = kvs[0].shape[1]
    slots = len(kvs)
    key_tile = min(KEY_TILE, shard_rows)
    edge_tile = min(EDGE_TILE, key_tile)
    groups, cols, rows = heads // PAIR, PAIR * SUB, subs * SUB
    return pl.pallas_call(
        partial(
            attend_kernel,
            slots=slots,
            subs=subs,
            q_block=q_block,
            key_tile=key_tile,
            edge_tile=edge_tile,
        ),
        grid_spec=pltpu.PrefetchScalarGridSpec(
            num_scalar_prefetch=3,
            grid=(1,),
            in_specs=[pl.BlockSpec(memory_space=pl.ANY)] * (1 + slots),
            out_specs=pl.BlockSpec((rows, heads * width), lambda i, *_: (0, 0)),
            scratch_shapes=[
                pltpu.VMEM((heads, rows, width), jnp.bfloat16),
                pltpu.VMEM((slots, 2, shard_rows, width), jnp.bfloat16),
                pltpu.VMEM((subs, groups, width, cols), jnp.float32),
                pltpu.VMEM((subs, groups, 1, cols), jnp.float32),
                pltpu.VMEM((subs, groups, 1, cols), jnp.float32),
                pltpu.VMEM((key_tile, cols), jnp.float32),
                pltpu.VMEM((key_tile, cols), jnp.bfloat16),
                pltpu.VMEM((1, cols), jnp.float32),
                pltpu.SemaphoreType.DMA((slots + 1,)),
            ],
        ),
        out_shape=jax.ShapeDtypeStruct((rows, heads * width), jnp.bfloat16),
        compiler_params=pltpu.CompilerParams(vmem_limit_bytes=VMEM_BYTES),
        cost_estimate=pl.CostEstimate(flops=rows, bytes_accessed=rows, transcendentals=0),
    )(place, lengths, tasks, queries, *kvs)


def local(queries, keys, values, doc_lengths, tasks, w_out):
    heads, tok_dev, width = queries.shape
    n_tok = lax.axis_size("tok")
    n_head = lax.axis_size("head")
    me = lax.axis_index("tok")
    z = lax.axis_index("head")
    tokens = n_tok * tok_dev
    q_block = tokens * heads // tasks.shape[0]
    chips = n_tok // 2
    doc_most = tokens * 4 // doc_lengths.shape[0]
    back = min(chips - 1, -(-(doc_most - 1) // (2 * tok_dev)))
    out_cols = w_out.shape[1] // n_head
    flat_tasks = tasks.reshape(-1)

    turned = values.reshape(-1, width, width).transpose(0, 2, 1).reshape(values.shape)
    own = jnp.concatenate([keys, turned], axis=0)
    spans = []
    for reach in range(back, 0, -1):
        pairs = [(i, i + 2 * reach) for i in range(n_tok - 2 * reach)]
        spans.append(lax.ppermute(own, "tok", pairs))

    def column(block):
        return lax.dynamic_slice_in_dim(w_out, block * out_cols, out_cols, 1)

    w_send = jnp.concatenate([column((z ^ 1) ^ 2), column(z ^ 1)], axis=1)
    w_pass, w_keep = column(z ^ 2), column(z)
    base = (me // 2 - back) * 2 * tok_dev
    starts = [tok_dev // SUB * sum(PARTS[:at]) // sum(PARTS) for at in range(len(PARTS) + 1)]
    places = []
    for at in starts[:-1]:
        numbers = [me % 2, me * tok_dev + at * SUB, base, at * SUB]
        places.append(jnp.stack([jnp.asarray(n, jnp.int32) for n in numbers]))
    spans, w_send, w_pass, w_keep, flat_tasks, places = lax.optimization_barrier(
        (spans, w_send, w_pass, w_keep, flat_tasks, places)
    )
    swap = [(i, i ^ 1) for i in range(n_tok)]
    kvs = []
    for mine in [*spans, own]:
        kvs += [mine, lax.ppermute(mine, "tok", swap)]

    near = [(i, i ^ 1) for i in range(n_head)]
    far = [(i, i ^ 2) for i in range(n_head)]

    def project(attended):
        sent = jnp.dot(attended, w_send, preferred_element_type=jnp.float32)
        return sent.astype(jnp.bfloat16)

    def onward(attended, arrived):
        summed = jnp.dot(attended, w_pass, preferred_element_type=jnp.float32)
        summed = summed + arrived[:, :out_cols].astype(jnp.float32)
        return summed.astype(jnp.bfloat16)

    def finish(attended, arrived, crossed):
        summed = jnp.dot(attended, w_keep, preferred_element_type=jnp.float32)
        summed = summed + arrived[:, out_cols:].astype(jnp.float32)
        return (summed + crossed.astype(jnp.float32)).astype(jnp.bfloat16)

    attended, sent, arrived, other, crossed = {}, {}, {}, {}, {}
    count = len(PARTS)
    for chunk in range(count):
        place = places[chunk]
        if chunk >= 1:
            place, sent[chunk - 1] = lax.optimization_barrier((place, sent[chunk - 1]))
            arrived[chunk - 1] = lax.ppermute(sent[chunk - 1], "head", near)
        if chunk >= LAG + 1:
            late = chunk - LAG - 1
            place, other[late] = lax.optimization_barrier((place, other[late]))
            crossed[late] = lax.ppermute(other[late], "head", far)
        subs = starts[chunk + 1] - starts[chunk]
        attended[chunk] = attend(
            place, doc_lengths, flat_tasks, queries, kvs, subs, q_block
        )
        sent[chunk] = project(attended[chunk])
        due = [chunk - LAG] if chunk < count - 1 else range(chunk - LAG, chunk)
        for late in due:
            if late >= 0:
                sent[chunk], arrived[late] = lax.optimization_barrier((sent[chunk], arrived[late]))
                other[late] = onward(attended[late], arrived[late])
        if chunk >= LAG + 1:
            late = chunk - LAG - 1
            sent[chunk], crossed[late] = lax.optimization_barrier((sent[chunk], crossed[late]))
    arrived[count - 1] = lax.ppermute(sent[count - 1], "head", near)
    for chunk in range(count):
        if chunk not in other:
            other[chunk] = onward(attended[chunk], arrived[chunk])
        if chunk not in crossed:
            crossed[chunk] = lax.ppermute(other[chunk], "head", far)
    outs = [finish(attended[c], arrived[c], crossed[c]) for c in range(count)]
    return jnp.concatenate(outs, axis=0)


def solution(mesh):
    placed = (
        P("head", "tok", None),
        P("head", "tok", None),
        P("head", "tok", None),
        P(),
        P(),
        P("head", None),
    )
    return jax.shard_map(
        local, mesh=mesh, in_specs=placed, out_specs=P("tok", "head"), check_vma=False
    )
```

time: 140 us -> 132 us (0.943)
  the two profiles are of different devices: /device:TPU:0 before, /device:TPU:5 now
where the time goes in v4:
time: 132 us; the launch traced here: 130 us
  waiting for transfers between devices  55.8 us (42%)
  Pallas kernels  46.4 us (35%)
  starting transfers between devices  13.3 us (10%)
  matrix products  7.6 us (6%)
  local copies, waits for them, and re-layouts  4.6 us (3%)
  other arithmetic  1.55 us (1%)
    pallas_call x5, Pallas kernels, attend(): pl.pallas_call(partial(attend_kernel, slots=slots, subs=subs, q_block=q_b...  46.4 us
    ppermute x4, waiting for transfers between devices, local(): arrived[chunk - 1] = lax.ppermute(sent[chunk - 1], 'head', near)  21.9 us
    ppermute x2, waiting for transfers between devices, local(): spans.append(lax.ppermute(own, 'tok', pairs))  19.4 us
    ppermute x1, waiting for transfers between devices, local(): arrived[count - 1] = lax.ppermute(sent[count - 1], 'head', near)  6.65 us
    ppermute x3, waiting for transfers between devices, local(): crossed[chunk] = lax.ppermute(other[chunk], 'head', far)  5.64 us
    ppermute x2, starting transfers between devices, local(): spans.append(lax.ppermute(own, 'tok', pairs))  4.4 us
    ppermute x4, starting transfers between devices, local(): arrived[chunk - 1] = lax.ppermute(sent[chunk - 1], 'head', near)  3.14 us
    dot_general x5, matrix products, project(): sent = jnp.dot(attended, w_send, preferred_element_type=jnp.float32)  3.04 us
  transfers between devices with their start and end apart: 15, of which 9 were waited for; matrix products, arithmetic and copies ran while one was open for 8% of the time, Pallas kernels for 31%

profile of v4, /device:TPU:5, one launch (start us, length us, event | category | flops | bytes accessed | tf_op | source)
XLA Modules:
  0.0 129.6 jit_solution(17001862298928455807)
XLA Ops:
  0.0 1.1 copy.8
  1.1 1.0 pad_maximum_fusion.1.refs_4_
  2.1 0.7 collective-permute-start.4
  2.9 3.1 %collective-permute-start.1 = (bf16[2,1024,128]{2,1,0:T(8,128)(2,1)S(1)}, bf16[2,1024,128]{2,1,0:T(8,128)(2,1)S(1)}, u32[]{:S(2)}, u32[]{:S(2)}) collective-permute-start(bf16[2,1024,128]{2,1,0:T(8,128)(2,1)S(1)} %pad_maximum_fusion.1.refs_4_), channel_id=1, source_target_pairs={{0,8},{4,12},{8,16},{12,20},{16,24},{20,28},{1,9},{5,13},{9,17},{1... | collective-permute-start | bytes 1572872 | tf_op jit(solution)/shard_map/ppermute | solution.py:294
  6.0 1.3 collective-permute-start
  7.3 0.1 pad_add_fusion.2
  7.5 0.8 copy.9
  8.3 0.2 reshape.11.tasks
  8.5 0.1 pad_add_fusion
  8.6 2.5 %constant_dynamic-slice_fusion = (bf16[1024,512]{1,0:T(8,128)(2,1)S(1)}, bf16[1024,512]{1,0:T(8,128)(2,1)S(1)}, bf16[1024,512]{1,0:T(8,128)(2,1)S(1)}, bf16[1024,512]{1,0:T(8,128)(2,1)S(1)}) fusion(bf16[1024,2048]{1,0:T(8,128)(2,1)} %param.11, s32[]{:T(128)S(6)} %select_n.34, s32[]{:T(128)S(6)} %select_n.32, s32[]{:T(128)S(6)} %select_n.31, s32[]{:T(128)S(6)} %select_n.33), kind=kLoop, calls=%fused_computation.37 | loop fusion | bytes 8388624 | tf_op jit(solution)/shard_map/dynamic_slice | solution.py:297
  11.1 0.3 pad_maximum_fusion
  11.4 7.8 %collective-permute-done.1.refs_2_ = bf16[2,1024,128]{2,1,0:T(8,128)(2,1)S(1)} collective-permute-done((bf16[2,1024,128]{2,1,0:T(8,128)(2,1)S(1)}, bf16[2,1024,128]{2,1,0:T(8,128)(2,1)S(1)}, u32[]{:S(2)}, u32[]{:S(2)}) %collective-permute-start.1) | collective-permute-done | bytes 524320 | tf_op jit(solution)/shard_map/ppermute | solution.py:294
  19.2 11.5 %collective-permute-done.refs_0_ = bf16[2,1024,128]{2,1,0:T(8,128)(2,1)S(1)} collective-permute-done((bf16[2,1024,128]{2,1,0:T(8,128)(2,1)S(1)}, bf16[2,1024,128]{2,1,0:T(8,128)(2,1)S(1)}, u32[]{:S(2)}, u32[]{:S(2)}) %collective-permute-start) | collective-permute-done | bytes 524320 | tf_op jit(solution)/shard_map/ppermute | solution.py:294
  30.8 0.5 collective-permute-start.2
  31.3 1.5 %collective-permute-done.2.refs_1_ = bf16[2,1024,128]{2,1,0:T(8,128)(2,1)S(1)} collective-permute-done((bf16[2,1024,128]{2,1,0:T(8,128)(2,1)S(1)}, bf16[2,1024,128]{2,1,0:T(8,128)(2,1)S(1)}, u32[]{:S(2)}, u32[]{:S(2)}) %collective-permute-start.2) | collective-permute-done | bytes 524320 | tf_op jit(solution)/shard_map/ppermute | solution.py:313
  32.8 0.7 collective-permute-done.3.refs_3_
  33.5 5.9 %shard_map.64 = bf16[128,1024]{1,0:T(8,128)(2,1)S(1)} custom-call(s32[4]{0:T(128)S(1)} %get-tuple-element.40.place, s32[8]{0:T(128)S(1)} %copy-done.1, s32[640]{0:T(1024)S(1)} %reshape.11.tasks, bf16[8,1024,128]{2,1,0:T(8,128)(2,1)S(1)} %copy-done, bf16[2,1024,128]{2,1,0:T(8,128)(2,1)S(1)} %collective-permute-done.refs_0_, ...), custom_call_target="tpu_custom_call" | custom-call | flops 128 | bytes 128 | tf_op jit(solution)/shard_map/pallas_call | solution.py:243
  39.4 0.4 convolution_convert_fusion.4
  39.9 1.4 %collective-permute-start.5 = (bf16[128,1024]{1,0:T(8,128)(2,1)S(1)}, bf16[128,1024]{1,0:T(8,128)(2,1)S(1)}, u32[]{:S(2)}, u32[]{:S(2)}) collective-permute-start(bf16[128,1024]{1,0:T(8,128)(2,1)S(1)} %convolution_convert_fusion.4), channel_id=1, source_target_pairs={{0,1},{1,0},{2,3},{3,2},{4,5},{5,4},{6,7},{7,6},{8,9},{9,8},{10,11... | collective-permute-start | bytes 786440 | tf_op jit(solution)/shard_map/ppermute | solution.py:338
  41.3 10.2 %shard_map.65 = bf16[256,1024]{1,0:T(8,128)(2,1)S(1)} custom-call(s32[4]{0:T(128)S(1)} %get-tuple-element.48.place, s32[8]{0:T(128)S(1)} %copy-done.1, s32[640]{0:T(1024)S(1)} %reshape.11.tasks, bf16[8,1024,128]{2,1,0:T(8,128)(2,1)S(1)} %copy-done, bf16[2,1024,128]{2,1,0:T(8,128)(2,1)S(1)} %collective-permute-done.refs_0_, ...), custom_call_target="tpu_custom_call" | custom-call | flops 256 | bytes 256 | tf_op jit(solution)/shard_map/pallas_call | solution.py:243
  51.5 0.7 convolution_convert_fusion.2
  52.2 0.2 collective-permute-start.6
  52.5 11.5 %shard_map.66 = bf16[256,1024]{1,0:T(8,128)(2,1)S(1)} custom-call(s32[4]{0:T(128)S(1)} %get-tuple-element.49.place, s32[8]{0:T(128)S(1)} %copy-done.1, s32[640]{0:T(1024)S(1)} %reshape.11.tasks, bf16[8,1024,128]{2,1,0:T(8,128)(2,1)S(1)} %copy-done, bf16[2,1024,128]{2,1,0:T(8,128)(2,1)S(1)} %collective-permute-done.refs_0_, ...), custom_call_target="tpu_custom_call" | custom-call | flops 256 | bytes 256 | tf_op jit(solution)/shard_map/pallas_call | solution.py:243
  63.9 0.7 convolution_convert_fusion.1
  64.7 0.3 fusion.16
  65.0 2.4 %collective-permute-start.7 = (bf16[128,512]{1,0:T(8,128)(2,1)S(1)}, bf16[128,512]{1,0:T(8,128)(2,1)S(1)}, u32[]{:S(2)}, u32[]{:S(2)}) collective-permute-start(bf16[128,512]{1,0:T(8,128)(2,1)S(1)} %fusion.16), channel_id=1, source_target_pairs={{0,2},{1,3},{2,0},{3,1},{4,6},{5,7},{6,4},{7,5},{8,10},{9,11},{10,... | collective-permute-start | bytes 393224 | tf_op jit(solution)/shard_map/ppermute | solution.py:342
  67.4 11.4 %shard_map.67 = bf16[256,1024]{1,0:T(8,128)(2,1)S(1)} custom-call(s32[4]{0:T(128)S(1)} %get-tuple-element.56.place, s32[8]{0:T(128)S(1)} %copy-done.1, s32[640]{0:T(1024)S(1)} %reshape.11.tasks, bf16[8,1024,128]{2,1,0:T(8,128)(2,1)S(1)} %copy-done, bf16[2,1024,128]{2,1,0:T(8,128)(2,1)S(1)} %collective-permute-done.refs_0_, ...), custom_call_target="tpu_custom_call" | custom-call | flops 256 | bytes 256 | tf_op jit(solution)/shard_map/pallas_call | solution.py:243
  78.8 0.7 convolution_convert_fusion
  79.5 1.4 %collective-permute-start.8 = (bf16[256,1024]{1,0:T(8,128)(2,1)S(1)}, bf16[256,1024]{1,0:T(8,128)(2,1)S(1)}, u32[]{:S(2)}, u32[]{:S(2)}) collective-permute-start(bf16[256,1024]{1,0:T(8,128)(2,1)S(1)} %convolution_convert_fusion.1), channel_id=1, source_target_pairs={{0,1},{1,0},{2,3},{3,2},{4,5},{5,4},{6,7},{7,6},{8,9},{9,8},{10,11... | collective-permute-start | bytes 1572872 | tf_op jit(solution)/shard_map/ppermute | solution.py:338
  80.9 0.4 fusion.3
  81.3 0.1 collective-permute-start.10
  81.5 0.2 collective-permute-start.9
  81.6 7.3 %shard_map.68 = bf16[128,1024]{1,0:T(8,128)(2,1)S(1)} custom-call(s32[4]{0:T(128)S(1)} %pad_add_fusion.4.place, s32[8]{0:T(128)S(1)} %copy-done.1, s32[640]{0:T(1024)S(1)} %reshape.11.tasks, bf16[8,1024,128]{2,1,0:T(8,128)(2,1)S(1)} %copy-done, bf16[2,1024,128]{2,1,0:T(8,128)(2,1)S(1)} %collective-permute-done.refs_0_, ...), custom_call_target="tpu_custom_call" | custom-call | flops 128 | bytes 128 | tf_op jit(solution)/shard_map/pallas_call | solution.py:243
  89.0 0.4 convolution_convert_fusion.3
  89.4 0.3 fusion.15
  89.8 9.0 %collective-permute-done.8 = bf16[256,1024]{1,0:T(8,128)(2,1)S(1)} collective-permute-done((bf16[256,1024]{1,0:T(8,128)(2,1)S(1)}, bf16[256,1024]{1,0:T(8,128)(2,1)S(1)}, u32[]{:S(2)}, u32[]{:S(2)}) %collective-permute-start.8) | collective-permute-done | bytes 524320 | tf_op jit(solution)/shard_map/ppermute | solution.py:338
  98.7 0.4 fusion.4
  99.2 12.9 %collective-permute-done.9 = bf16[256,1024]{1,0:T(8,128)(2,1)S(1)} collective-permute-done((bf16[256,1024]{1,0:T(8,128)(2,1)S(1)}, bf16[256,1024]{1,0:T(8,128)(2,1)S(1)}, u32[]{:S(2)}, u32[]{:S(2)}) %collective-permute-start.9) | collective-permute-done | bytes 524320 | tf_op jit(solution)/shard_map/ppermute | solution.py:338
  112.2 0.4 fusion.5
  112.7 1.8 %collective-permute-start.13 = (bf16[128,1024]{1,0:T(8,128)(2,1)S(1)}, bf16[128,1024]{1,0:T(8,128)(2,1)S(1)}, u32[]{:S(2)}, u32[]{:S(2)}) collective-permute-start(bf16[128,1024]{1,0:T(8,128)(2,1)S(1)} %convolution_convert_fusion.3), channel_id=1, source_target_pairs={{0,1},{1,0},{2,3},{3,2},{4,5},{5,4},{6,7},{7,6},{8,9},{9,8},{10,11... | collective-permute-start | bytes 786440 | tf_op jit(solution)/shard_map/ppermute | solution.py:356
  114.5 0.4 fusion.11
  115.0 0.4 fusion.9
  115.4 6.6 %collective-permute-done.13 = bf16[128,1024]{1,0:T(8,128)(2,1)S(1)} collective-permute-done((bf16[128,1024]{1,0:T(8,128)(2,1)S(1)}, bf16[128,1024]{1,0:T(8,128)(2,1)S(1)}, u32[]{:S(2)}, u32[]{:S(2)}) %collective-permute-start.13) | collective-permute-done | bytes 262176 | tf_op jit(solution)/shard_map/ppermute | solution.py:356
  122.1 0.3 fusion.19
  122.5 1.3 %collective-permute-done.12 = bf16[256,512]{1,0:T(8,128)(2,1)S(1)} collective-permute-done((bf16[256,512]{1,0:T(8,128)(2,1)S(1)}, bf16[256,512]{1,0:T(8,128)(2,1)S(1)}, u32[]{:S(2)}, u32[]{:S(2)}) %collective-permute-start.12) | collective-permute-done | bytes 262176 | tf_op jit(solution)/shard_map/ppermute | solution.py:361
  123.8 0.4 fusion.7
  124.2 4.3 %collective-permute-done.14 = bf16[128,512]{1,0:T(8,128)(2,1)S(1)} collective-permute-done((bf16[128,512]{1,0:T(8,128)(2,1)S(1)}, bf16[128,512]{1,0:T(8,128)(2,1)S(1)}, u32[]{:S(2)}, u32[]{:S(2)}) %collective-permute-start.14) | collective-permute-done | bytes 131104 | tf_op jit(solution)/shard_map/ppermute | solution.py:361
  128.6 1.0 fusion.18
  (17 shorter events, 0.4 us)
Async XLA Ops:
  2.1 29.1 %collective-permute-start.4 = (bf16[2,1024,128]{2,1,0:T(8,128)(2,1)S(1)}, bf16[2,1024,128]{2,1,0:T(8,128)(2,1)S(1)}, u32[]{:S(2)}, u32[]{:S(2)}) collective-permute-start(bf16[2,1024,128]{2,1,0:T(8,128)(2,1)S(1)} %pad_maximum_fusion.1.refs_4_), channel_id=1, source_target_pairs={{0,4},{4,0},{8,12},{12,8},{16,20},{20,16},{24,28},{28,24},{1,5},{5... | collective-permute-start | bytes 1572872 | tf_op jit(solution)/shard_map/ppermute | solution.py:313
  2.9 16.4 %collective-permute-start.1 = (bf16[2,1024,128]{2,1,0:T(8,128)(2,1)S(1)}, bf16[2,1024,128]{2,1,0:T(8,128)(2,1)S(1)}, u32[]{:S(2)}, u32[]{:S(2)}) collective-permute-start(bf16[2,1024,128]{2,1,0:T(8,128)(2,1)S(1)} %pad_maximum_fusion.1.refs_4_), channel_id=1, source_target_pairs={{0,8},{4,12},{8,16},{12,20},{16,24},{20,28},{1,9},{5,13},{9,17},{1... | collective-permute-start | bytes 1572872 | tf_op jit(solution)/shard_map/ppermute | solution.py:294
  6.0 24.8 %collective-permute-start = (bf16[2,1024,128]{2,1,0:T(8,128)(2,1)S(1)}, bf16[2,1024,128]{2,1,0:T(8,128)(2,1)S(1)}, u32[]{:S(2)}, u32[]{:S(2)}) collective-permute-start(bf16[2,1024,128]{2,1,0:T(8,128)(2,1)S(1)} %pad_maximum_fusion.1.refs_4_), channel_id=1, source_target_pairs={{0,16},{4,20},{8,24},{12,28},{1,17},{5,21},{9,25},{13,29},{2,18},{... | collective-permute-start | bytes 1572872 | tf_op jit(solution)/shard_map/ppermute | solution.py:294
  11.0 22.5 %copy-start = (bf16[8,1024,128]{2,1,0:T(8,128)(2,1)S(1)}, bf16[8,1024,128]{2,1,0:T(8,128)(2,1)}, u32[]{:S(2)}) copy-start(bf16[8,1024,128]{2,1,0:T(8,128)(2,1)} %q_ref.9) | copy-start | bytes 6291460
  11.1 22.5 %copy-start.1 = (s32[8]{0:T(128)S(1)}, s32[8]{0:T(128)}, u32[]{:S(2)}) copy-start(s32[8]{0:T(128)} %lengths.9) | copy-start | bytes 100
  30.8 2.0 %collective-permute-start.2 = (bf16[2,1024,128]{2,1,0:T(8,128)(2,1)S(1)}, bf16[2,1024,128]{2,1,0:T(8,128)(2,1)S(1)}, u32[]{:S(2)}, u32[]{:S(2)}) collective-permute-start(bf16[2,1024,128]{2,1,0:T(8,128)(2,1)S(1)} %collective-permute-done.refs_0_), channel_id=1, source_target_pairs={{0,4},{4,0},{8,12},{12,8},{16,20},{20,16},{24,28},{28,24},{1,5},{5... | collective-permute-start | bytes 1572872 | tf_op jit(solution)/shard_map/ppermute | solution.py:313
  31.2 2.3 %collective-permute-start.3 = (bf16[2,1024,128]{2,1,0:T(8,128)(2,1)S(1)}, bf16[2,1024,128]{2,1,0:T(8,128)(2,1)S(1)}, u32[]{:S(2)}, u32[]{:S(2)}) collective-permute-start(bf16[2,1024,128]{2,1,0:T(8,128)(2,1)S(1)} %collective-permute-done.1.refs_2_), channel_id=1, source_target_pairs={{0,4},{4,0},{8,12},{12,8},{16,20},{20,16},{24,28},{28,24},{1,5},{5... | collective-permute-start | bytes 1572872 | tf_op jit(solution)/shard_map/ppermute | solution.py:313
  39.9 24.8 %collective-permute-start.5 = (bf16[128,1024]{1,0:T(8,128)(2,1)S(1)}, bf16[128,1024]{1,0:T(8,128)(2,1)S(1)}, u32[]{:S(2)}, u32[]{:S(2)}) collective-permute-start(bf16[128,1024]{1,0:T(8,128)(2,1)S(1)} %convolution_convert_fusion.4), channel_id=1, source_target_pairs={{0,1},{1,0},{2,3},{3,2},{4,5},{5,4},{6,7},{7,6},{8,9},{9,8},{10,11... | collective-permute-start | bytes 786440 | tf_op jit(solution)/shard_map/ppermute | solution.py:338
  52.2 28.6 %collective-permute-start.6 = (bf16[256,1024]{1,0:T(8,128)(2,1)S(1)}, bf16[256,1024]{1,0:T(8,128)(2,1)S(1)}, u32[]{:S(2)}, u32[]{:S(2)}) collective-permute-start(bf16[256,1024]{1,0:T(8,128)(2,1)S(1)} %convolution_convert_fusion.2), channel_id=1, source_target_pairs={{0,1},{1,0},{2,3},{3,2},{4,5},{5,4},{6,7},{7,6},{8,9},{9,8},{10,11... | collective-permute-start | bytes 1572872 | tf_op jit(solution)/shard_map/ppermute | solution.py:338
  65.0 15.9 %collective-permute-start.7 = (bf16[128,512]{1,0:T(8,128)(2,1)S(1)}, bf16[128,512]{1,0:T(8,128)(2,1)S(1)}, u32[]{:S(2)}, u32[]{:S(2)}) collective-permute-start(bf16[128,512]{1,0:T(8,128)(2,1)S(1)} %fusion.16), channel_id=1, source_target_pairs={{0,2},{1,3},{2,0},{3,1},{4,6},{5,7},{6,4},{7,5},{8,10},{9,11},{10,... | collective-permute-start | bytes 393224 | tf_op jit(solution)/shard_map/ppermute | solution.py:342
  79.5 19.2 %collective-permute-start.8 = (bf16[256,1024]{1,0:T(8,128)(2,1)S(1)}, bf16[256,1024]{1,0:T(8,128)(2,1)S(1)}, u32[]{:S(2)}, u32[]{:S(2)}) collective-permute-start(bf16[256,1024]{1,0:T(8,128)(2,1)S(1)} %convolution_convert_fusion.1), channel_id=1, source_target_pairs={{0,1},{1,0},{2,3},{3,2},{4,5},{5,4},{6,7},{7,6},{8,9},{9,8},{10,11... | collective-permute-start | bytes 1572872 | tf_op jit(solution)/shard_map/ppermute | solution.py:338
  81.3 30.8 %collective-permute-start.10 = (bf16[256,512]{1,0:T(8,128)(2,1)S(1)}, bf16[256,512]{1,0:T(8,128)(2,1)S(1)}, u32[]{:S(2)}, u32[]{:S(2)}) collective-permute-start(bf16[256,512]{1,0:T(8,128)(2,1)S(1)} %fusion.3), channel_id=1, source_target_pairs={{0,2},{1,3},{2,0},{3,1},{4,6},{5,7},{6,4},{7,5},{8,10},{9,11},{10,... | collective-permute-start | bytes 786440 | tf_op jit(solution)/shard_map/ppermute | solution.py:342
  81.5 30.7 %collective-permute-start.9 = (bf16[256,1024]{1,0:T(8,128)(2,1)S(1)}, bf16[256,1024]{1,0:T(8,128)(2,1)S(1)}, u32[]{:S(2)}, u32[]{:S(2)}) collective-permute-start(bf16[256,1024]{1,0:T(8,128)(2,1)S(1)} %convolution_convert_fusion), channel_id=1, source_target_pairs={{0,1},{1,0},{2,3},{3,2},{4,5},{5,4},{6,7},{7,6},{8,9},{9,8},{10,11... | collective-permute-start | bytes 1572872 | tf_op jit(solution)/shard_map/ppermute | solution.py:338
  99.1 15.8 %collective-permute-start.11 = (bf16[256,512]{1,0:T(8,128)(2,1)S(1)}, bf16[256,512]{1,0:T(8,128)(2,1)S(1)}, u32[]{:S(2)}, u32[]{:S(2)}) collective-permute-start(bf16[256,512]{1,0:T(8,128)(2,1)S(1)} %fusion.4), channel_id=1, source_target_pairs={{0,2},{1,3},{2,0},{3,1},{4,6},{5,7},{6,4},{7,5},{8,10},{9,11},{10,... | collective-permute-start | bytes 786440 | tf_op jit(solution)/shard_map/ppermute | solution.py:361
  112.6 11.2 %collective-permute-start.12 = (bf16[256,512]{1,0:T(8,128)(2,1)S(1)}, bf16[256,512]{1,0:T(8,128)(2,1)S(1)}, u32[]{:S(2)}, u32[]{:S(2)}) collective-permute-start(bf16[256,512]{1,0:T(8,128)(2,1)S(1)} %fusion.5), channel_id=1, source_target_pairs={{0,2},{1,3},{2,0},{3,1},{4,6},{5,7},{6,4},{7,5},{8,10},{9,11},{10,... | collective-permute-start | bytes 786440 | tf_op jit(solution)/shard_map/ppermute | solution.py:361
  112.7 9.4 %collective-permute-start.13 = (bf16[128,1024]{1,0:T(8,128)(2,1)S(1)}, bf16[128,1024]{1,0:T(8,128)(2,1)S(1)}, u32[]{:S(2)}, u32[]{:S(2)}) collective-permute-start(bf16[128,1024]{1,0:T(8,128)(2,1)S(1)} %convolution_convert_fusion.3), channel_id=1, source_target_pairs={{0,1},{1,0},{2,3},{3,2},{4,5},{5,4},{6,7},{7,6},{8,9},{9,8},{10,11... | collective-permute-start | bytes 786440 | tf_op jit(solution)/shard_map/ppermute | solution.py:356
  122.4 6.2 %collective-permute-start.14 = (bf16[128,512]{1,0:T(8,128)(2,1)S(1)}, bf16[128,512]{1,0:T(8,128)(2,1)S(1)}, u32[]{:S(2)}, u32[]{:S(2)}) collective-permute-start(bf16[128,512]{1,0:T(8,128)(2,1)S(1)} %fusion.19), channel_id=1, source_target_pairs={{0,2},{1,3},{2,0},{3,1},{4,6},{5,7},{6,4},{7,5},{8,10},{9,11},{10,... | collective-permute-start | bytes 393224 | tf_op jit(solution)/shard_map/ppermute | solution.py:361
  124.2 4.4 %copy-start.2 = (bf16[1024,512]{1,0:T(8,128)(2,1)}, bf16[1024,512]{1,0:T(8,128)(2,1)S(1)}, u32[]{:S(2)}) copy-start(bf16[1024,512]{1,0:T(8,128)(2,1)S(1)} %fusion.7) | copy-start | bytes 3145732

commit v5 on v4

--- a/solution.py
+++ b/solution.py
@@ -14,7 +14,7 @@
 EDGE_TILE = 256
 VMEM_BYTES = 40 * 2**20
 SUB = 128
-LAG = 2
+LAG = 1
 PAIR = 4
 PARTS = (1, 2, 2, 2, 1)
 
@@ -345,14 +345,14 @@
             place, doc_lengths, flat_tasks, queries, kvs, subs, q_block
         )
         sent[chunk] = project(attended[chunk])
-        due = [chunk - LAG] if chunk < count - 1 else range(chunk - LAG, chunk)
-        for late in due:
-            if late >= 0:
-                sent[chunk], arrived[late] = lax.optimization_barrier((sent[chunk], arrived[late]))
-                other[late] = onward(attended[late], arrived[late])
-        if chunk >= LAG + 1:
-            late = chunk - LAG - 1
-            sent[chunk], crossed[late] = lax.optimization_barrier((sent[chunk], crossed[late]))
+        if chunk >= LAG:
+            late = chunk - LAG
+            sent[chunk], arrived[late] = lax.optimization_barrier((sent[chunk], arrived[late]))
+            other[late] = onward(attended[late], arrived[late])
+            if late - 1 in crossed:
+                sent[chunk], crossed[late - 1] = lax.optimization_barrier(
+                    (sent[chunk], crossed[late - 1])
+                )
     arrived[count - 1] = lax.ppermute(sent[count - 1], "head", near)
     for chunk in range(count):
         if chunk not in other:

time: 132 us -> 127 us (0.962)
  waiting for transfers between devices: 55.8 us -> 47.2 us
  starting transfers between devices: 13.3 us -> 18.2 us
    ppermute x4, waiting for transfers between devices: 21.9 us -> 12.2 us  [local(): arrived[chunk - 1] = lax.ppermute(sent[chunk - 1], 'head', near)]
    ppermute x2, waiting for transfers between devices: 19.4 us -> 16.4 us  [local(): spans.append(lax.ppermute(own, 'tok', pairs))]
    ppermute x3 -> x2, waiting for transfers between devices: 5.64 us -> 8.11 us  [local(): crossed[chunk] = lax.ppermute(other[chunk], 'head', far)]
    ppermute x3 -> x2, starting transfers between devices: 0.21 us -> 2.58 us  [local(): crossed[chunk] = lax.ppermute(other[chunk], 'head', far)]
    ppermute x2 -> x3, starting transfers between devices: 2.5 us -> 4.24 us  [local(): crossed[late] = lax.ppermute(other[late], 'head', far)]
    ppermute x1, waiting for transfers between devices: 6.65 us -> 8.22 us  [local(): arrived[count - 1] = lax.ppermute(sent[count - 1], 'head', near)]
    ppermute x3, starting transfers between devices: 1.25 us -> 2.57 us  [local(): kvs += [mine, lax.ppermute(mine, 'tok', swap)]]
  transfers between devices with their start and end apart: 15 -> 15, of which waited for: 9 -> 8; matrix products, arithmetic and copies ran while one was open for 8% -> 8% of each run, Pallas kernels for 31% -> 32%
where the time goes in v5:
time: 127 us; the launch traced here: 126 us
  waiting for transfers between devices  47.2 us (37%)
  Pallas kernels  46.2 us (36%)
  starting transfers between devices  18.2 us (14%)
  matrix products  7.6 us (6%)
  local copies, waits for them, and re-layouts  4.6 us (4%)
  other arithmetic  1.55 us (1%)
    pallas_call x5, Pallas kernels, attend(): pl.pallas_call(partial(attend_kernel, slots=slots, subs=subs, q_block=q_b...  46.2 us
    ppermute x2, waiting for transfers between devices, local(): spans.append(lax.ppermute(own, 'tok', pairs))  16.4 us
    ppermute x4, waiting for transfers between devices, local(): arrived[chunk - 1] = lax.ppermute(sent[chunk - 1], 'head', near)  12.2 us
    ppermute x1, waiting for transfers between devices, local(): arrived[count - 1] = lax.ppermute(sent[count - 1], 'head', near)  8.22 us
    ppermute x2, waiting for transfers between devices, local(): crossed[chunk] = lax.ppermute(other[chunk], 'head', far)  8.11 us
    ppermute x2, starting transfers between devices, local(): spans.append(lax.ppermute(own, 'tok', pairs))  4.41 us
    ppermute x3, starting transfers between devices, local(): crossed[late] = lax.ppermute(other[late], 'head', far)  4.24 us
    dot_general x5, matrix products, project(): sent = jnp.dot(attended, w_send, preferred_element_type=jnp.float32)  3.04 us
  transfers between devices with their start and end apart: 15, of which 8 were waited for; matrix products, arithmetic and copies ran while one was open for 8% of the time, Pallas kernels for 32%

profile of v5, /device:TPU:5, one launch (start us, length us, event | category | flops | bytes accessed | tf_op | source)
XLA Modules:
  0.0 125.6 jit_solution(7492585092877171191)
XLA Ops:
  0.0 1.1 copy.8
  1.1 1.0 pad_maximum_fusion.1.refs_4_
  2.1 1.3 %collective-permute-start = (bf16[2,1024,128]{2,1,0:T(8,128)(2,1)S(1)}, bf16[2,1024,128]{2,1,0:T(8,128)(2,1)S(1)}, u32[]{:S(2)}, u32[]{:S(2)}) collective-permute-start(bf16[2,1024,128]{2,1,0:T(8,128)(2,1)S(1)} %pad_maximum_fusion.1.refs_4_), channel_id=1, source_target_pairs={{0,16},{4,20},{8,24},{12,28},{1,17},{5,21},{9,25},{13,29},{2,18},{... | collective-permute-start | bytes 1572872 | tf_op jit(solution)/shard_map/ppermute | solution.py:294
  3.4 3.1 %collective-permute-start.1 = (bf16[2,1024,128]{2,1,0:T(8,128)(2,1)S(1)}, bf16[2,1024,128]{2,1,0:T(8,128)(2,1)S(1)}, u32[]{:S(2)}, u32[]{:S(2)}) collective-permute-start(bf16[2,1024,128]{2,1,0:T(8,128)(2,1)S(1)} %pad_maximum_fusion.1.refs_4_), channel_id=1, source_target_pairs={{0,8},{4,12},{8,16},{12,20},{16,24},{20,28},{1,9},{5,13},{9,17},{1... | collective-permute-start | bytes 1572872 | tf_op jit(solution)/shard_map/ppermute | solution.py:294
  6.6 1.0 collective-permute-start.4
  7.6 0.1 pad_add_fusion.2
  7.7 0.8 copy.9
  8.5 0.2 reshape.11.tasks
  8.8 0.1 pad_add_fusion
  8.8 2.5 %constant_dynamic-slice_fusion = (bf16[1024,512]{1,0:T(8,128)(2,1)S(1)}, bf16[1024,512]{1,0:T(8,128)(2,1)S(1)}, bf16[1024,512]{1,0:T(8,128)(2,1)S(1)}, bf16[1024,512]{1,0:T(8,128)(2,1)S(1)}) fusion(bf16[1024,2048]{1,0:T(8,128)(2,1)} %param.11, s32[]{:T(128)S(6)} %select_n.34, s32[]{:T(128)S(6)} %select_n.32, s32[]{:T(128)S(6)} %select_n.31, s32[]{:T(128)S(6)} %select_n.33), kind=kLoop, calls=%fused_computation.37 | loop fusion | bytes 8388624 | tf_op jit(solution)/shard_map/dynamic_slice | solution.py:297
  11.3 0.3 pad_maximum_fusion
  11.6 16.4 %collective-permute-done.refs_0_ = bf16[2,1024,128]{2,1,0:T(8,128)(2,1)S(1)} collective-permute-done((bf16[2,1024,128]{2,1,0:T(8,128)(2,1)S(1)}, bf16[2,1024,128]{2,1,0:T(8,128)(2,1)S(1)}, u32[]{:S(2)}, u32[]{:S(2)}) %collective-permute-start) | collective-permute-done | bytes 524320 | tf_op jit(solution)/shard_map/ppermute | solution.py:294
  28.1 1.5 %collective-permute-start.2 = (bf16[2,1024,128]{2,1,0:T(8,128)(2,1)S(1)}, bf16[2,1024,128]{2,1,0:T(8,128)(2,1)S(1)}, u32[]{:S(2)}, u32[]{:S(2)}) collective-permute-start(bf16[2,1024,128]{2,1,0:T(8,128)(2,1)S(1)} %collective-permute-done.refs_0_), channel_id=1, source_target_pairs={{0,4},{4,0},{8,12},{12,8},{16,20},{20,16},{24,28},{28,24},{1,5},{5... | collective-permute-start | bytes 1572872 | tf_op jit(solution)/shard_map/ppermute | solution.py:313
  29.6 1.5 %collective-permute-done.2.refs_1_ = bf16[2,1024,128]{2,1,0:T(8,128)(2,1)S(1)} collective-permute-done((bf16[2,1024,128]{2,1,0:T(8,128)(2,1)S(1)}, bf16[2,1024,128]{2,1,0:T(8,128)(2,1)S(1)}, u32[]{:S(2)}, u32[]{:S(2)}) %collective-permute-start.2) | collective-permute-done | bytes 524320 | tf_op jit(solution)/shard_map/ppermute | solution.py:313
  31.1 0.7 collective-permute-done.3.refs_3_
  31.9 5.9 %shard_map.64 = bf16[128,1024]{1,0:T(8,128)(2,1)S(1)} custom-call(s32[4]{0:T(128)S(1)} %get-tuple-element.44.place, s32[8]{0:T(128)S(1)} %copy-done.1, s32[640]{0:T(1024)S(1)} %reshape.11.tasks, bf16[8,1024,128]{2,1,0:T(8,128)(2,1)S(1)} %copy-done, bf16[2,1024,128]{2,1,0:T(8,128)(2,1)S(1)} %collective-permute-done.refs_0_, ...), custom_call_target="tpu_custom_call" | custom-call | flops 128 | bytes 128 | tf_op jit(solution)/shard_map/pallas_call | solution.py:243
  37.8 0.4 convolution_convert_fusion.4
  38.3 1.4 %collective-permute-start.5 = (bf16[128,1024]{1,0:T(8,128)(2,1)S(1)}, bf16[128,1024]{1,0:T(8,128)(2,1)S(1)}, u32[]{:S(2)}, u32[]{:S(2)}) collective-permute-start(bf16[128,1024]{1,0:T(8,128)(2,1)S(1)} %convolution_convert_fusion.4), channel_id=1, source_target_pairs={{0,1},{1,0},{2,3},{3,2},{4,5},{5,4},{6,7},{7,6},{8,9},{9,8},{10,11... | collective-permute-start | bytes 786440 | tf_op jit(solution)/shard_map/ppermute | solution.py:338
  39.6 10.2 %shard_map.65 = bf16[256,1024]{1,0:T(8,128)(2,1)S(1)} custom-call(s32[4]{0:T(128)S(1)} %get-tuple-element.51.place, s32[8]{0:T(128)S(1)} %copy-done.1, s32[640]{0:T(1024)S(1)} %reshape.11.tasks, bf16[8,1024,128]{2,1,0:T(8,128)(2,1)S(1)} %copy-done, bf16[2,1024,128]{2,1,0:T(8,128)(2,1)S(1)} %collective-permute-done.refs_0_, ...), custom_call_target="tpu_custom_call" | custom-call | flops 256 | bytes 256 | tf_op jit(solution)/shard_map/pallas_call | solution.py:243
  49.9 0.7 convolution_convert_fusion.2
  50.6 0.2 collective-permute-start.6
  50.9 0.3 fusion.16
  51.2 2.4 %collective-permute-start.7 = (bf16[128,512]{1,0:T(8,128)(2,1)S(1)}, bf16[128,512]{1,0:T(8,128)(2,1)S(1)}, u32[]{:S(2)}, u32[]{:S(2)}) collective-permute-start(bf16[128,512]{1,0:T(8,128)(2,1)S(1)} %fusion.16), channel_id=1, source_target_pairs={{0,2},{1,3},{2,0},{3,1},{4,6},{5,7},{6,4},{7,5},{8,10},{9,11},{10,... | collective-permute-start | bytes 393224 | tf_op jit(solution)/shard_map/ppermute | solution.py:342
  53.5 11.5 %shard_map.66 = bf16[256,1024]{1,0:T(8,128)(2,1)S(1)} custom-call(s32[4]{0:T(128)S(1)} %get-tuple-element.58.place, s32[8]{0:T(128)S(1)} %copy-done.1, s32[640]{0:T(1024)S(1)} %reshape.11.tasks, bf16[8,1024,128]{2,1,0:T(8,128)(2,1)S(1)} %copy-done, bf16[2,1024,128]{2,1,0:T(8,128)(2,1)S(1)} %collective-permute-done.refs_0_, ...), custom_call_target="tpu_custom_call" | custom-call | flops 256 | bytes 256 | tf_op jit(solution)/shard_map/pallas_call | solution.py:243
  65.0 0.7 convolution_convert_fusion.1
  65.8 0.4 fusion.3
  66.2 1.4 %collective-permute-start.8 = (bf16[256,1024]{1,0:T(8,128)(2,1)S(1)}, bf16[256,1024]{1,0:T(8,128)(2,1)S(1)}, u32[]{:S(2)}, u32[]{:S(2)}) collective-permute-start(bf16[256,1024]{1,0:T(8,128)(2,1)S(1)} %convolution_convert_fusion.1), channel_id=1, source_target_pairs={{0,1},{1,0},{2,3},{3,2},{4,5},{5,4},{6,7},{7,6},{8,9},{9,8},{10,11... | collective-permute-start | bytes 1572872 | tf_op jit(solution)/shard_map/ppermute | solution.py:338
  67.6 11.4 %shard_map.67 = bf16[256,1024]{1,0:T(8,128)(2,1)S(1)} custom-call(s32[4]{0:T(128)S(1)} %get-tuple-element.67.place, s32[8]{0:T(128)S(1)} %copy-done.1, s32[640]{0:T(1024)S(1)} %reshape.11.tasks, bf16[8,1024,128]{2,1,0:T(8,128)(2,1)S(1)} %copy-done, bf16[2,1024,128]{2,1,0:T(8,128)(2,1)S(1)} %collective-permute-done.refs_0_, ...), custom_call_target="tpu_custom_call" | custom-call | flops 256 | bytes 256 | tf_op jit(solution)/shard_map/pallas_call | solution.py:243
  79.1 0.3 fusion.15
  79.4 0.7 convolution_convert_fusion
  80.1 3.6 %collective-permute-done.8 = bf16[256,1024]{1,0:T(8,128)(2,1)S(1)} collective-permute-done((bf16[256,1024]{1,0:T(8,128)(2,1)S(1)}, bf16[256,1024]{1,0:T(8,128)(2,1)S(1)}, u32[]{:S(2)}, u32[]{:S(2)}) %collective-permute-start.8) | collective-permute-done | bytes 524320 | tf_op jit(solution)/shard_map/ppermute | solution.py:338
  83.7 0.4 fusion.4
  84.2 1.8 %collective-permute-start.11 = (bf16[256,512]{1,0:T(8,128)(2,1)S(1)}, bf16[256,512]{1,0:T(8,128)(2,1)S(1)}, u32[]{:S(2)}, u32[]{:S(2)}) collective-permute-start(bf16[256,512]{1,0:T(8,128)(2,1)S(1)} %fusion.4), channel_id=1, source_target_pairs={{0,2},{1,3},{2,0},{3,1},{4,6},{5,7},{6,4},{7,5},{8,10},{9,11},{10,... | collective-permute-start | bytes 786440 | tf_op jit(solution)/shard_map/ppermute | solution.py:342
  86.0 7.1 %shard_map.68 = bf16[128,1024]{1,0:T(8,128)(2,1)S(1)} custom-call(s32[4]{0:T(128)S(1)} %pad_add_fusion.4.place, s32[8]{0:T(128)S(1)} %copy-done.1, s32[640]{0:T(1024)S(1)} %reshape.11.tasks, bf16[8,1024,128]{2,1,0:T(8,128)(2,1)S(1)} %copy-done, bf16[2,1024,128]{2,1,0:T(8,128)(2,1)S(1)} %collective-permute-done.refs_0_, ...), custom_call_target="tpu_custom_call" | custom-call | flops 128 | bytes 128 | tf_op jit(solution)/shard_map/pallas_call | solution.py:243
  93.1 0.4 convolution_convert_fusion.3
  93.6 0.4 fusion.11
  94.1 8.6 %collective-permute-done.10 = bf16[256,1024]{1,0:T(8,128)(2,1)S(1)} collective-permute-done((bf16[256,1024]{1,0:T(8,128)(2,1)S(1)}, bf16[256,1024]{1,0:T(8,128)(2,1)S(1)}, u32[]{:S(2)}, u32[]{:S(2)}) %collective-permute-start.10) | collective-permute-done | bytes 524320 | tf_op jit(solution)/shard_map/ppermute | solution.py:338
  102.7 1.4 %collective-permute-start.13 = (bf16[128,1024]{1,0:T(8,128)(2,1)S(1)}, bf16[128,1024]{1,0:T(8,128)(2,1)S(1)}, u32[]{:S(2)}, u32[]{:S(2)}) collective-permute-start(bf16[128,1024]{1,0:T(8,128)(2,1)S(1)} %convolution_convert_fusion.3), channel_id=1, source_target_pairs={{0,1},{1,0},{2,3},{3,2},{4,5},{5,4},{6,7},{7,6},{8,9},{9,8},{10,11... | collective-permute-start | bytes 786440 | tf_op jit(solution)/shard_map/ppermute | solution.py:356
  104.0 0.4 fusion.5
  104.5 1.6 %collective-permute-start.12 = (bf16[256,512]{1,0:T(8,128)(2,1)S(1)}, bf16[256,512]{1,0:T(8,128)(2,1)S(1)}, u32[]{:S(2)}, u32[]{:S(2)}) collective-permute-start(bf16[256,512]{1,0:T(8,128)(2,1)S(1)} %fusion.5), channel_id=1, source_target_pairs={{0,2},{1,3},{2,0},{3,1},{4,6},{5,7},{6,4},{7,5},{8,10},{9,11},{10,... | collective-permute-start | bytes 786440 | tf_op jit(solution)/shard_map/ppermute | solution.py:361
  106.1 0.4 fusion.9
  106.5 8.2 %collective-permute-done.13 = bf16[128,1024]{1,0:T(8,128)(2,1)S(1)} collective-permute-done((bf16[128,1024]{1,0:T(8,128)(2,1)S(1)}, bf16[128,1024]{1,0:T(8,128)(2,1)S(1)}, u32[]{:S(2)}, u32[]{:S(2)}) %collective-permute-start.13) | collective-permute-done | bytes 262176 | tf_op jit(solution)/shard_map/ppermute | solution.py:356
  114.8 0.3 fusion.19
  115.1 1.0 collective-permute-start.14
  116.1 3.0 %collective-permute-done.12 = bf16[256,512]{1,0:T(8,128)(2,1)S(1)} collective-permute-done((bf16[256,512]{1,0:T(8,128)(2,1)S(1)}, bf16[256,512]{1,0:T(8,128)(2,1)S(1)}, u32[]{:S(2)}, u32[]{:S(2)}) %collective-permute-start.12) | collective-permute-done | bytes 262176 | tf_op jit(solution)/shard_map/ppermute | solution.py:361
  119.0 0.4 fusion.7
  119.5 5.2 %collective-permute-done.14 = bf16[128,512]{1,0:T(8,128)(2,1)S(1)} collective-permute-done((bf16[128,512]{1,0:T(8,128)(2,1)S(1)}, bf16[128,512]{1,0:T(8,128)(2,1)S(1)}, u32[]{:S(2)}, u32[]{:S(2)}) %collective-permute-start.14) | collective-permute-done | bytes 131104 | tf_op jit(solution)/shard_map/ppermute | solution.py:361
  124.6 1.0 fusion.18
  (17 shorter events, 0.3 us)
Async XLA Ops:
  2.1 25.9 %collective-permute-start = (bf16[2,1024,128]{2,1,0:T(8,128)(2,1)S(1)}, bf16[2,1024,128]{2,1,0:T(8,128)(2,1)S(1)}, u32[]{:S(2)}, u32[]{:S(2)}) collective-permute-start(bf16[2,1024,128]{2,1,0:T(8,128)(2,1)S(1)} %pad_maximum_fusion.1.refs_4_), channel_id=1, source_target_pairs={{0,16},{4,20},{8,24},{12,28},{1,17},{5,21},{9,25},{13,29},{2,18},{... | collective-permute-start | bytes 1572872 | tf_op jit(solution)/shard_map/ppermute | solution.py:294
  3.4 24.6 %collective-permute-start.1 = (bf16[2,1024,128]{2,1,0:T(8,128)(2,1)S(1)}, bf16[2,1024,128]{2,1,0:T(8,128)(2,1)S(1)}, u32[]{:S(2)}, u32[]{:S(2)}) collective-permute-start(bf16[2,1024,128]{2,1,0:T(8,128)(2,1)S(1)} %pad_maximum_fusion.1.refs_4_), channel_id=1, source_target_pairs={{0,8},{4,12},{8,16},{12,20},{16,24},{20,28},{1,9},{5,13},{9,17},{1... | collective-permute-start | bytes 1572872 | tf_op jit(solution)/shard_map/ppermute | solution.py:294
  6.6 23.1 %collective-permute-start.4 = (bf16[2,1024,128]{2,1,0:T(8,128)(2,1)S(1)}, bf16[2,1024,128]{2,1,0:T(8,128)(2,1)S(1)}, u32[]{:S(2)}, u32[]{:S(2)}) collective-permute-start(bf16[2,1024,128]{2,1,0:T(8,128)(2,1)S(1)} %pad_maximum_fusion.1.refs_4_), channel_id=1, source_target_pairs={{0,4},{4,0},{8,12},{12,8},{16,20},{20,16},{24,28},{28,24},{1,5},{5... | collective-permute-start | bytes 1572872 | tf_op jit(solution)/shard_map/ppermute | solution.py:313
  11.3 20.6 %copy-start = (bf16[8,1024,128]{2,1,0:T(8,128)(2,1)S(1)}, bf16[8,1024,128]{2,1,0:T(8,128)(2,1)}, u32[]{:S(2)}) copy-start(bf16[8,1024,128]{2,1,0:T(8,128)(2,1)} %q_ref.9) | copy-start | bytes 6291460
  11.3 20.6 %copy-start.1 = (s32[8]{0:T(128)S(1)}, s32[8]{0:T(128)}, u32[]{:S(2)}) copy-start(s32[8]{0:T(128)} %lengths.9) | copy-start | bytes 100
  28.1 3.1 %collective-permute-start.2 = (bf16[2,1024,128]{2,1,0:T(8,128)(2,1)S(1)}, bf16[2,1024,128]{2,1,0:T(8,128)(2,1)S(1)}, u32[]{:S(2)}, u32[]{:S(2)}) collective-permute-start(bf16[2,1024,128]{2,1,0:T(8,128)(2,1)S(1)} %collective-permute-done.refs_0_), channel_id=1, source_target_pairs={{0,4},{4,0},{8,12},{12,8},{16,20},{20,16},{24,28},{28,24},{1,5},{5... | collective-permute-start | bytes 1572872 | tf_op jit(solution)/shard_map/ppermute | solution.py:313
  29.6 2.3 %collective-permute-start.3 = (bf16[2,1024,128]{2,1,0:T(8,128)(2,1)S(1)}, bf16[2,1024,128]{2,1,0:T(8,128)(2,1)S(1)}, u32[]{:S(2)}, u32[]{:S(2)}) collective-permute-start(bf16[2,1024,128]{2,1,0:T(8,128)(2,1)S(1)} %collective-permute-done.1.refs_2_), channel_id=1, source_target_pairs={{0,4},{4,0},{8,12},{12,8},{16,20},{20,16},{24,28},{28,24},{1,5},{5... | collective-permute-start | bytes 1572872 | tf_op jit(solution)/shard_map/ppermute | solution.py:313
  38.3 12.3 %collective-permute-start.5 = (bf16[128,1024]{1,0:T(8,128)(2,1)S(1)}, bf16[128,1024]{1,0:T(8,128)(2,1)S(1)}, u32[]{:S(2)}, u32[]{:S(2)}) collective-permute-start(bf16[128,1024]{1,0:T(8,128)(2,1)S(1)} %convolution_convert_fusion.4), channel_id=1, source_target_pairs={{0,1},{1,0},{2,3},{3,2},{4,5},{5,4},{6,7},{7,6},{8,9},{9,8},{10,11... | collective-permute-start | bytes 786440 | tf_op jit(solution)/shard_map/ppermute | solution.py:338
  50.6 15.1 %collective-permute-start.6 = (bf16[256,1024]{1,0:T(8,128)(2,1)S(1)}, bf16[256,1024]{1,0:T(8,128)(2,1)S(1)}, u32[]{:S(2)}, u32[]{:S(2)}) collective-permute-start(bf16[256,1024]{1,0:T(8,128)(2,1)S(1)} %convolution_convert_fusion.2), channel_id=1, source_target_pairs={{0,1},{1,0},{2,3},{3,2},{4,5},{5,4},{6,7},{7,6},{8,9},{9,8},{10,11... | collective-permute-start | bytes 1572872 | tf_op jit(solution)/shard_map/ppermute | solution.py:338
  51.2 15.0 %collective-permute-start.7 = (bf16[128,512]{1,0:T(8,128)(2,1)S(1)}, bf16[128,512]{1,0:T(8,128)(2,1)S(1)}, u32[]{:S(2)}, u32[]{:S(2)}) collective-permute-start(bf16[128,512]{1,0:T(8,128)(2,1)S(1)} %fusion.16), channel_id=1, source_target_pairs={{0,2},{1,3},{2,0},{3,1},{4,6},{5,7},{6,4},{7,5},{8,10},{9,11},{10,... | collective-permute-start | bytes 393224 | tf_op jit(solution)/shard_map/ppermute | solution.py:342
  66.2 17.5 %collective-permute-start.8 = (bf16[256,1024]{1,0:T(8,128)(2,1)S(1)}, bf16[256,1024]{1,0:T(8,128)(2,1)S(1)}, u32[]{:S(2)}, u32[]{:S(2)}) collective-permute-start(bf16[256,1024]{1,0:T(8,128)(2,1)S(1)} %convolution_convert_fusion.1), channel_id=1, source_target_pairs={{0,1},{1,0},{2,3},{3,2},{4,5},{5,4},{6,7},{7,6},{8,9},{9,8},{10,11... | collective-permute-start | bytes 1572872 | tf_op jit(solution)/shard_map/ppermute | solution.py:338
  67.6 16.6 %collective-permute-start.9 = (bf16[256,512]{1,0:T(8,128)(2,1)S(1)}, bf16[256,512]{1,0:T(8,128)(2,1)S(1)}, u32[]{:S(2)}, u32[]{:S(2)}) collective-permute-start(bf16[256,512]{1,0:T(8,128)(2,1)S(1)} %fusion.3), channel_id=1, source_target_pairs={{0,2},{1,3},{2,0},{3,1},{4,6},{5,7},{6,4},{7,5},{8,10},{9,11},{10,... | collective-permute-start | bytes 786440 | tf_op jit(solution)/shard_map/ppermute | solution.py:342
  84.1 18.6 %collective-permute-start.10 = (bf16[256,1024]{1,0:T(8,128)(2,1)S(1)}, bf16[256,1024]{1,0:T(8,128)(2,1)S(1)}, u32[]{:S(2)}, u32[]{:S(2)}) collective-permute-start(bf16[256,1024]{1,0:T(8,128)(2,1)S(1)} %convolution_convert_fusion), channel_id=1, source_target_pairs={{0,1},{1,0},{2,3},{3,2},{4,5},{5,4},{6,7},{7,6},{8,9},{9,8},{10,11... | collective-permute-start | bytes 1572872 | tf_op jit(solution)/shard_map/ppermute | solution.py:338
  84.2 18.5 %collective-permute-start.11 = (bf16[256,512]{1,0:T(8,128)(2,1)S(1)}, bf16[256,512]{1,0:T(8,128)(2,1)S(1)}, u32[]{:S(2)}, u32[]{:S(2)}) collective-permute-start(bf16[256,512]{1,0:T(8,128)(2,1)S(1)} %fusion.4), channel_id=1, source_target_pairs={{0,2},{1,3},{2,0},{3,1},{4,6},{5,7},{6,4},{7,5},{8,10},{9,11},{10,... | collective-permute-start | bytes 786440 | tf_op jit(solution)/shard_map/ppermute | solution.py:342
  102.7 12.1 %collective-permute-start.13 = (bf16[128,1024]{1,0:T(8,128)(2,1)S(1)}, bf16[128,1024]{1,0:T(8,128)(2,1)S(1)}, u32[]{:S(2)}, u32[]{:S(2)}) collective-permute-start(bf16[128,1024]{1,0:T(8,128)(2,1)S(1)} %convolution_convert_fusion.3), channel_id=1, source_target_pairs={{0,1},{1,0},{2,3},{3,2},{4,5},{5,4},{6,7},{7,6},{8,9},{9,8},{10,11... | collective-permute-start | bytes 786440 | tf_op jit(solution)/shard_map/ppermute | solution.py:356
  104.5 14.5 %collective-permute-start.12 = (bf16[256,512]{1,0:T(8,128)(2,1)S(1)}, bf16[256,512]{1,0:T(8,128)(2,1)S(1)}, u32[]{:S(2)}, u32[]{:S(2)}) collective-permute-start(bf16[256,512]{1,0:T(8,128)(2,1)S(1)} %fusion.5), channel_id=1, source_target_pairs={{0,2},{1,3},{2,0},{3,1},{4,6},{5,7},{6,4},{7,5},{8,10},{9,11},{10,... | collective-permute-start | bytes 786440 | tf_op jit(solution)/shard_map/ppermute | solution.py:361
  115.1 9.6 %collective-permute-start.14 = (bf16[128,512]{1,0:T(8,128)(2,1)S(1)}, bf16[128,512]{1,0:T(8,128)(2,1)S(1)}, u32[]{:S(2)}, u32[]{:S(2)}) collective-permute-start(bf16[128,512]{1,0:T(8,128)(2,1)S(1)} %fusion.19), channel_id=1, source_target_pairs={{0,2},{1,3},{2,0},{3,1},{4,6},{5,7},{6,4},{7,5},{8,10},{9,11},{10,... | collective-permute-start | bytes 393224 | tf_op jit(solution)/shard_map/ppermute | solution.py:361
  119.5 5.2 %copy-start.2 = (bf16[1024,512]{1,0:T(8,128)(2,1)}, bf16[1024,512]{1,0:T(8,128)(2,1)S(1)}, u32[]{:S(2)}) copy-start(bf16[1024,512]{1,0:T(8,128)(2,1)S(1)} %fusion.7) | copy-start | bytes 3145732

commit v6 on v5

--- a/solution.py
+++ b/solution.py
@@ -79,13 +79,11 @@
     hi = jnp.clip(
         (jnp.minimum(high_most, last_row + 1) - base + edge_tile - 1) // edge_tile, lo, tiles
     )
-    full_lo = (jnp.maximum(low_most, begin_last) - base + key_tile - 1) // key_tile
-    full_hi = (jnp.minimum(high_least, first_row + 1) - base) // key_tile
-    full_lo = jnp.maximum(full_lo, 0)
-    full_hi = jnp.minimum(full_hi, tiles // ratio)
-    some = full_hi > full_lo
-    inner_lo = jnp.where(some, full_lo * ratio, lo)
-    inner_hi = jnp.where(some, full_hi * ratio, lo)
+    far_lo = lo // ratio
+    far_hi = jnp.maximum((jnp.minimum(high_least, first_row) - base) // key_tile, far_lo)
+    clear_lo = (jnp.maximum(low_most, begin_last) - base + key_tile - 1) // key_tile
+    clear_lo = jnp.clip(clear_lo, far_lo, far_hi)
+    near_lo = jnp.maximum(lo, far_hi * ratio)
     factor = math.log2(math.e) / math.sqrt(width)
 
     def reset():
@@ -99,11 +97,10 @@
         slot = at // 2 * 2 + (parity if at % 2 == 0 else 1 - parity)
         copy = pltpu.make_async_copy(kv_refs[at], kv_all.at[slot], sems.at[at])
         first, last = slot * per_slot, (slot + 1) * per_slot
-        below = (lo < inner_lo) & (lo < last) & (inner_lo > first)
-        above = (inner_hi < hi) & (inner_hi < last) & (hi > first)
-        used = (lo < last) & (hi > first)
-        early.append((below | above, copy))
-        late.append((used & jnp.logical_not(below | above), copy))
+        soon = (near_lo < last) & (hi > first)
+        used = (far_lo * ratio < last) & (hi > first)
+        early.append((soon, copy))
+        late.append((used & jnp.logical_not(soon), copy))
     for needed, copy in early + late:
         pl.when(needed)(copy.start)
 
@@ -200,22 +197,10 @@
 
         pl.when(count > 0)(whole)
 
-    left = inner_lo - lo
-    sweep(
-        left + hi - inner_hi,
-        lambda turn: jnp.where(turn < left, lo + turn, inner_hi + turn - left),
-        edge_tile,
-        True,
-        False,
-    )
+    sweep(hi - near_lo, lambda turn: near_lo + turn, edge_tile, True, False)
     wait(late)
-    sweep(
-        (inner_hi - inner_lo) // ratio,
-        lambda turn: inner_lo // ratio + turn,
-        key_tile,
-        False,
-        True,
-    )
+    sweep(far_hi - clear_lo, lambda turn: clear_lo + turn, key_tile, False, True)
+    sweep(clear_lo - far_lo, lambda turn: far_lo + turn, key_tile, True, True)
     in_range = jnp.min(jnp.where(total[...] < SAFE_TOTAL, 1.0, 0.0))
 
     @pl.when(in_range < 0.5)

time: 127 us -> 128 us (level); the launches traced: 126 us -> 130 us
  Pallas kernels: 46.2 us -> 58 us
  waiting for transfers between devices: 47.2 us -> 36.3 us
  starting transfers between devices: 18.2 us -> 21.3 us
    pallas_call x5, Pallas kernels: 46.2 us -> 58 us  [attend(): pl.pallas_call(partial(attend_kernel, slots=slots, subs=subs, q_block=q_b...]
    ppermute x4, waiting for transfers between devices: 12.2 us -> 7.44 us  [local(): arrived[chunk - 1] = lax.ppermute(sent[chunk - 1], 'head', near)]
    ppermute x2, waiting for transfers between devices: 8.11 us -> 4.92 us  [local(): crossed[chunk] = lax.ppermute(other[chunk], 'head', far)]
    ppermute x1, waiting for transfers between devices: 8.22 us -> 5.24 us  [local(): arrived[count - 1] = lax.ppermute(sent[count - 1], 'head', near)]
    ppermute x1, starting transfers between devices: 1.36 us -> 4.13 us  [local(): arrived[count - 1] = lax.ppermute(sent[count - 1], 'head', near)]
  transfers between devices with their start and end apart: 15 -> 15, of which waited for: 8 -> 7; matrix products, arithmetic and copies ran while one was open for 8% -> 8% of each run, Pallas kernels for 32% -> 39%
where the time goes in v6:
time: 128 us; the launch traced here: 130 us
  Pallas kernels  58 us (45%)
  waiting for transfers between devices  36.3 us (28%)
  starting transfers between devices  21.3 us (17%)
  matrix products  7.6 us (6%)
  local copies, waits for them, and re-layouts  4.6 us (4%)
  other arithmetic  1.55 us (1%)
    pallas_call x5, Pallas kernels, attend(): pl.pallas_call(partial(attend_kernel, slots=slots, subs=subs, q_block=q_b...  58 us
    ppermute x2, waiting for transfers between devices, local(): spans.append(lax.ppermute(own, 'tok', pairs))  16.4 us
    ppermute x4, waiting for transfers between devices, local(): arrived[chunk - 1] = lax.ppermute(sent[chunk - 1], 'head', near)  7.44 us
    ppermute x1, waiting for transfers between devices, local(): arrived[count - 1] = lax.ppermute(sent[count - 1], 'head', near)  5.24 us
    ppermute x2, waiting for transfers between devices, local(): crossed[chunk] = lax.ppermute(other[chunk], 'head', far)  4.92 us
    ppermute x3, starting transfers between devices, local(): crossed[late] = lax.ppermute(other[late], 'head', far)  4.72 us
    ppermute x2, starting transfers between devices, local(): spans.append(lax.ppermute(own, 'tok', pairs))  4.41 us
    ppermute x1, starting transfers between devices, local(): arrived[count - 1] = lax.ppermute(sent[count - 1], 'head', near)  4.13 us
  transfers between devices with their start and end apart: 15, of which 7 were waited for; matrix products, arithmetic and copies ran while one was open for 8% of the time, Pallas kernels for 39%

profile of v6, /device:TPU:5, one launch (start us, length us, event | category | flops | bytes accessed | tf_op | source)
XLA Modules:
  0.0 129.6 jit_solution(6285135650091560856)
XLA Ops:
  0.0 1.1 copy.8
  1.1 1.0 pad_maximum_fusion.1.refs_4_
  2.1 1.3 collective-permute-start
  3.4 3.1 %collective-permute-start.1 = (bf16[2,1024,128]{2,1,0:T(8,128)(2,1)S(1)}, bf16[2,1024,128]{2,1,0:T(8,128)(2,1)S(1)}, u32[]{:S(2)}, u32[]{:S(2)}) collective-permute-start(bf16[2,1024,128]{2,1,0:T(8,128)(2,1)S(1)} %pad_maximum_fusion.1.refs_4_), channel_id=1, source_target_pairs={{0,8},{4,12},{8,16},{12,20},{16,24},{20,28},{1,9},{5,13},{9,17},{1... | collective-permute-start | bytes 1572872 | tf_op jit(solution)/shard_map/ppermute | solution.py:279
  6.6 1.0 collective-permute-start.4
  7.6 0.1 pad_add_fusion.2
  7.7 0.1 pad_add_fusion.4.place
  7.7 0.8 copy.9
  8.5 0.2 reshape.11.tasks
  8.8 0.1 pad_add_fusion
  8.8 2.5 %constant_dynamic-slice_fusion = (bf16[1024,512]{1,0:T(8,128)(2,1)S(1)}, bf16[1024,512]{1,0:T(8,128)(2,1)S(1)}, bf16[1024,512]{1,0:T(8,128)(2,1)S(1)}, bf16[1024,512]{1,0:T(8,128)(2,1)S(1)}) fusion(bf16[1024,2048]{1,0:T(8,128)(2,1)} %param.11, s32[]{:T(128)S(6)} %select_n.34, s32[]{:T(128)S(6)} %select_n.32, s32[]{:T(128)S(6)} %select_n.31, s32[]{:T(128)S(6)} %select_n.33), kind=kLoop, calls=%fused_computation.37 | loop fusion | bytes 8388624 | tf_op jit(solution)/shard_map/dynamic_slice | solution.py:282
  11.3 0.3 pad_maximum_fusion
  11.6 16.4 %collective-permute-done.refs_0_ = bf16[2,1024,128]{2,1,0:T(8,128)(2,1)S(1)} collective-permute-done((bf16[2,1024,128]{2,1,0:T(8,128)(2,1)S(1)}, bf16[2,1024,128]{2,1,0:T(8,128)(2,1)S(1)}, u32[]{:S(2)}, u32[]{:S(2)}) %collective-permute-start) | collective-permute-done | bytes 524320 | tf_op jit(solution)/shard_map/ppermute | solution.py:279
  28.1 1.5 %collective-permute-start.2 = (bf16[2,1024,128]{2,1,0:T(8,128)(2,1)S(1)}, bf16[2,1024,128]{2,1,0:T(8,128)(2,1)S(1)}, u32[]{:S(2)}, u32[]{:S(2)}) collective-permute-start(bf16[2,1024,128]{2,1,0:T(8,128)(2,1)S(1)} %collective-permute-done.refs_0_), channel_id=1, source_target_pairs={{0,4},{4,0},{8,12},{12,8},{16,20},{20,16},{24,28},{28,24},{1,5},{5... | collective-permute-start | bytes 1572872 | tf_op jit(solution)/shard_map/ppermute | solution.py:298
  29.6 1.5 %collective-permute-done.2.refs_1_ = bf16[2,1024,128]{2,1,0:T(8,128)(2,1)S(1)} collective-permute-done((bf16[2,1024,128]{2,1,0:T(8,128)(2,1)S(1)}, bf16[2,1024,128]{2,1,0:T(8,128)(2,1)S(1)}, u32[]{:S(2)}, u32[]{:S(2)}) %collective-permute-start.2) | collective-permute-done | bytes 524320 | tf_op jit(solution)/shard_map/ppermute | solution.py:298
  31.1 0.7 collective-permute-done.3.refs_3_
  31.9 8.0 %shard_map.64 = bf16[128,1024]{1,0:T(8,128)(2,1)S(1)} custom-call(s32[4]{0:T(128)S(1)} %get-tuple-element.44.place, s32[8]{0:T(128)S(1)} %copy-done.1, s32[640]{0:T(1024)S(1)} %reshape.11.tasks, bf16[8,1024,128]{2,1,0:T(8,128)(2,1)S(1)} %copy-done, bf16[2,1024,128]{2,1,0:T(8,128)(2,1)S(1)} %collective-permute-done.refs_0_, ...), custom_call_target="tpu_custom_call" | custom-call | flops 128 | bytes 128 | tf_op jit(solution)/shard_map/pallas_call | solution.py:228
  40.0 0.4 convolution_convert_fusion.4
  40.4 1.4 %collective-permute-start.5 = (bf16[128,1024]{1,0:T(8,128)(2,1)S(1)}, bf16[128,1024]{1,0:T(8,128)(2,1)S(1)}, u32[]{:S(2)}, u32[]{:S(2)}) collective-permute-start(bf16[128,1024]{1,0:T(8,128)(2,1)S(1)} %convolution_convert_fusion.4), channel_id=1, source_target_pairs={{0,1},{1,0},{2,3},{3,2},{4,5},{5,4},{6,7},{7,6},{8,9},{9,8},{10,11... | collective-permute-start | bytes 786440 | tf_op jit(solution)/shard_map/ppermute | solution.py:323
  41.8 14.0 %shard_map.65 = bf16[256,1024]{1,0:T(8,128)(2,1)S(1)} custom-call(s32[4]{0:T(128)S(1)} %get-tuple-element.51.place, s32[8]{0:T(128)S(1)} %copy-done.1, s32[640]{0:T(1024)S(1)} %reshape.11.tasks, bf16[8,1024,128]{2,1,0:T(8,128)(2,1)S(1)} %copy-done, bf16[2,1024,128]{2,1,0:T(8,128)(2,1)S(1)} %collective-permute-done.refs_0_, ...), custom_call_target="tpu_custom_call" | custom-call | flops 256 | bytes 256 | tf_op jit(solution)/shard_map/pallas_call | solution.py:228
  55.7 0.7 convolution_convert_fusion.2
  56.5 0.2 collective-permute-start.6
  56.7 0.3 fusion.16
  57.0 2.4 %collective-permute-start.7 = (bf16[128,512]{1,0:T(8,128)(2,1)S(1)}, bf16[128,512]{1,0:T(8,128)(2,1)S(1)}, u32[]{:S(2)}, u32[]{:S(2)}) collective-permute-start(bf16[128,512]{1,0:T(8,128)(2,1)S(1)} %fusion.16), channel_id=1, source_target_pairs={{0,2},{1,3},{2,0},{3,1},{4,6},{5,7},{6,4},{7,5},{8,10},{9,11},{10,... | collective-permute-start | bytes 393224 | tf_op jit(solution)/shard_map/ppermute | solution.py:327
  59.4 14.8 %shard_map.66 = bf16[256,1024]{1,0:T(8,128)(2,1)S(1)} custom-call(s32[4]{0:T(128)S(1)} %get-tuple-element.58.place, s32[8]{0:T(128)S(1)} %copy-done.1, s32[640]{0:T(1024)S(1)} %reshape.11.tasks, bf16[8,1024,128]{2,1,0:T(8,128)(2,1)S(1)} %copy-done, bf16[2,1024,128]{2,1,0:T(8,128)(2,1)S(1)} %collective-permute-done.refs_0_, ...), custom_call_target="tpu_custom_call" | custom-call | flops 256 | bytes 256 | tf_op jit(solution)/shard_map/pallas_call | solution.py:228
  74.2 0.7 convolution_convert_fusion.1
  75.0 0.4 fusion.3
  75.4 1.4 %collective-permute-start.8 = (bf16[256,1024]{1,0:T(8,128)(2,1)S(1)}, bf16[256,1024]{1,0:T(8,128)(2,1)S(1)}, u32[]{:S(2)}, u32[]{:S(2)}) collective-permute-start(bf16[256,1024]{1,0:T(8,128)(2,1)S(1)} %convolution_convert_fusion.1), channel_id=1, source_target_pairs={{0,1},{1,0},{2,3},{3,2},{4,5},{5,4},{6,7},{7,6},{8,9},{9,8},{10,11... | collective-permute-start | bytes 1572872 | tf_op jit(solution)/shard_map/ppermute | solution.py:323
  76.8 18.3 %shard_map.67 = bf16[256,1024]{1,0:T(8,128)(2,1)S(1)} custom-call(s32[4]{0:T(128)S(1)} %get-tuple-element.67.place, s32[8]{0:T(128)S(1)} %copy-done.1, s32[640]{0:T(1024)S(1)} %reshape.11.tasks, bf16[8,1024,128]{2,1,0:T(8,128)(2,1)S(1)} %copy-done, bf16[2,1024,128]{2,1,0:T(8,128)(2,1)S(1)} %collective-permute-done.refs_0_, ...), custom_call_target="tpu_custom_call" | custom-call | flops 256 | bytes 256 | tf_op jit(solution)/shard_map/pallas_call | solution.py:228
  95.2 0.3 fusion.15
  95.5 0.7 convolution_convert_fusion
  96.3 0.4 fusion.4
  96.7 0.2 collective-permute-start.10
  96.9 2.3 %collective-permute-start.11 = (bf16[256,512]{1,0:T(8,128)(2,1)S(1)}, bf16[256,512]{1,0:T(8,128)(2,1)S(1)}, u32[]{:S(2)}, u32[]{:S(2)}) collective-permute-start(bf16[256,512]{1,0:T(8,128)(2,1)S(1)} %fusion.4), channel_id=1, source_target_pairs={{0,2},{1,3},{2,0},{3,1},{4,6},{5,7},{6,4},{7,5},{8,10},{9,11},{10,... | collective-permute-start | bytes 786440 | tf_op jit(solution)/shard_map/ppermute | solution.py:327
  99.2 2.8 %shard_map.68 = bf16[128,1024]{1,0:T(8,128)(2,1)S(1)} custom-call(s32[4]{0:T(128)S(1)} %pad_add_fusion.4.place, s32[8]{0:T(128)S(1)} %copy-done.1, s32[640]{0:T(1024)S(1)} %reshape.11.tasks, bf16[8,1024,128]{2,1,0:T(8,128)(2,1)S(1)} %copy-done, bf16[2,1024,128]{2,1,0:T(8,128)(2,1)S(1)} %collective-permute-done.refs_0_, ...), custom_call_target="tpu_custom_call" | custom-call | flops 128 | bytes 128 | tf_op jit(solution)/shard_map/pallas_call | solution.py:228
  102.0 0.4 convolution_convert_fusion.3
  102.5 0.4 fusion.11
  103.0 7.4 %collective-permute-done.10 = bf16[256,1024]{1,0:T(8,128)(2,1)S(1)} collective-permute-done((bf16[256,1024]{1,0:T(8,128)(2,1)S(1)}, bf16[256,1024]{1,0:T(8,128)(2,1)S(1)}, u32[]{:S(2)}, u32[]{:S(2)}) %collective-permute-start.10) | collective-permute-done | bytes 524320 | tf_op jit(solution)/shard_map/ppermute | solution.py:323
  110.4 4.1 %collective-permute-start.13 = (bf16[128,1024]{1,0:T(8,128)(2,1)S(1)}, bf16[128,1024]{1,0:T(8,128)(2,1)S(1)}, u32[]{:S(2)}, u32[]{:S(2)}) collective-permute-start(bf16[128,1024]{1,0:T(8,128)(2,1)S(1)} %convolution_convert_fusion.3), channel_id=1, source_target_pairs={{0,1},{1,0},{2,3},{3,2},{4,5},{5,4},{6,7},{7,6},{8,9},{9,8},{10,11... | collective-permute-start | bytes 786440 | tf_op jit(solution)/shard_map/ppermute | solution.py:341
  114.5 0.4 fusion.5
  115.0 2.2 %collective-permute-start.12 = (bf16[256,512]{1,0:T(8,128)(2,1)S(1)}, bf16[256,512]{1,0:T(8,128)(2,1)S(1)}, u32[]{:S(2)}, u32[]{:S(2)}) collective-permute-start(bf16[256,512]{1,0:T(8,128)(2,1)S(1)} %fusion.5), channel_id=1, source_target_pairs={{0,2},{1,3},{2,0},{3,1},{4,6},{5,7},{6,4},{7,5},{8,10},{9,11},{10,... | collective-permute-start | bytes 786440 | tf_op jit(solution)/shard_map/ppermute | solution.py:346
  117.2 0.4 fusion.9
  117.6 5.2 %collective-permute-done.13 = bf16[128,1024]{1,0:T(8,128)(2,1)S(1)} collective-permute-done((bf16[128,1024]{1,0:T(8,128)(2,1)S(1)}, bf16[128,1024]{1,0:T(8,128)(2,1)S(1)}, u32[]{:S(2)}, u32[]{:S(2)}) %collective-permute-start.13) | collective-permute-done | bytes 262176 | tf_op jit(solution)/shard_map/ppermute | solution.py:341
  122.8 0.3 fusion.19
  123.2 2.5 %collective-permute-done.12 = bf16[256,512]{1,0:T(8,128)(2,1)S(1)} collective-permute-done((bf16[256,512]{1,0:T(8,128)(2,1)S(1)}, bf16[256,512]{1,0:T(8,128)(2,1)S(1)}, u32[]{:S(2)}, u32[]{:S(2)}) %collective-permute-start.12) | collective-permute-done | bytes 262176 | tf_op jit(solution)/shard_map/ppermute | solution.py:346
  125.8 0.4 fusion.7
  126.3 2.4 %collective-permute-done.14 = bf16[128,512]{1,0:T(8,128)(2,1)S(1)} collective-permute-done((bf16[128,512]{1,0:T(8,128)(2,1)S(1)}, bf16[128,512]{1,0:T(8,128)(2,1)S(1)}, u32[]{:S(2)}, u32[]{:S(2)}) %collective-permute-start.14) | collective-permute-done | bytes 131104 | tf_op jit(solution)/shard_map/ppermute | solution.py:346
  128.6 1.0 fusion.18
  (17 shorter events, 0.2 us)
Async XLA Ops:
  2.1 25.9 %collective-permute-start = (bf16[2,1024,128]{2,1,0:T(8,128)(2,1)S(1)}, bf16[2,1024,128]{2,1,0:T(8,128)(2,1)S(1)}, u32[]{:S(2)}, u32[]{:S(2)}) collective-permute-start(bf16[2,1024,128]{2,1,0:T(8,128)(2,1)S(1)} %pad_maximum_fusion.1.refs_4_), channel_id=1, source_target_pairs={{0,16},{4,20},{8,24},{12,28},{1,17},{5,21},{9,25},{13,29},{2,18},{... | collective-permute-start | bytes 1572872 | tf_op jit(solution)/shard_map/ppermute | solution.py:279
  3.4 24.6 %collective-permute-start.1 = (bf16[2,1024,128]{2,1,0:T(8,128)(2,1)S(1)}, bf16[2,1024,128]{2,1,0:T(8,128)(2,1)S(1)}, u32[]{:S(2)}, u32[]{:S(2)}) collective-permute-start(bf16[2,1024,128]{2,1,0:T(8,128)(2,1)S(1)} %pad_maximum_fusion.1.refs_4_), channel_id=1, source_target_pairs={{0,8},{4,12},{8,16},{12,20},{16,24},{20,28},{1,9},{5,13},{9,17},{1... | collective-permute-start | bytes 1572872 | tf_op jit(solution)/shard_map/ppermute | solution.py:279
  6.6 23.1 %collective-permute-start.4 = (bf16[2,1024,128]{2,1,0:T(8,128)(2,1)S(1)}, bf16[2,1024,128]{2,1,0:T(8,128)(2,1)S(1)}, u32[]{:S(2)}, u32[]{:S(2)}) collective-permute-start(bf16[2,1024,128]{2,1,0:T(8,128)(2,1)S(1)} %pad_maximum_fusion.1.refs_4_), channel_id=1, source_target_pairs={{0,4},{4,0},{8,12},{12,8},{16,20},{20,16},{24,28},{28,24},{1,5},{5... | collective-permute-start | bytes 1572872 | tf_op jit(solution)/shard_map/ppermute | solution.py:298
  11.3 20.6 %copy-start = (bf16[8,1024,128]{2,1,0:T(8,128)(2,1)S(1)}, bf16[8,1024,128]{2,1,0:T(8,128)(2,1)}, u32[]{:S(2)}) copy-start(bf16[8,1024,128]{2,1,0:T(8,128)(2,1)} %q_ref.9) | copy-start | bytes 6291460
  11.3 20.6 %copy-start.1 = (s32[8]{0:T(128)S(1)}, s32[8]{0:T(128)}, u32[]{:S(2)}) copy-start(s32[8]{0:T(128)} %lengths.9) | copy-start | bytes 100
  28.1 3.1 %collective-permute-start.2 = (bf16[2,1024,128]{2,1,0:T(8,128)(2,1)S(1)}, bf16[2,1024,128]{2,1,0:T(8,128)(2,1)S(1)}, u32[]{:S(2)}, u32[]{:S(2)}) collective-permute-start(bf16[2,1024,128]{2,1,0:T(8,128)(2,1)S(1)} %collective-permute-done.refs_0_), channel_id=1, source_target_pairs={{0,4},{4,0},{8,12},{12,8},{16,20},{20,16},{24,28},{28,24},{1,5},{5... | collective-permute-start | bytes 1572872 | tf_op jit(solution)/shard_map/ppermute | solution.py:298
  29.6 2.3 %collective-permute-start.3 = (bf16[2,1024,128]{2,1,0:T(8,128)(2,1)S(1)}, bf16[2,1024,128]{2,1,0:T(8,128)(2,1)S(1)}, u32[]{:S(2)}, u32[]{:S(2)}) collective-permute-start(bf16[2,1024,128]{2,1,0:T(8,128)(2,1)S(1)} %collective-permute-done.1.refs_2_), channel_id=1, source_target_pairs={{0,4},{4,0},{8,12},{12,8},{16,20},{20,16},{24,28},{28,24},{1,5},{5... | collective-permute-start | bytes 1572872 | tf_op jit(solution)/shard_map/ppermute | solution.py:298
  40.4 16.1 %collective-permute-start.5 = (bf16[128,1024]{1,0:T(8,128)(2,1)S(1)}, bf16[128,1024]{1,0:T(8,128)(2,1)S(1)}, u32[]{:S(2)}, u32[]{:S(2)}) collective-permute-start(bf16[128,1024]{1,0:T(8,128)(2,1)S(1)} %convolution_convert_fusion.4), channel_id=1, source_target_pairs={{0,1},{1,0},{2,3},{3,2},{4,5},{5,4},{6,7},{7,6},{8,9},{9,8},{10,11... | collective-permute-start | bytes 786440 | tf_op jit(solution)/shard_map/ppermute | solution.py:323
  56.5 18.5 %collective-permute-start.6 = (bf16[256,1024]{1,0:T(8,128)(2,1)S(1)}, bf16[256,1024]{1,0:T(8,128)(2,1)S(1)}, u32[]{:S(2)}, u32[]{:S(2)}) collective-permute-start(bf16[256,1024]{1,0:T(8,128)(2,1)S(1)} %convolution_convert_fusion.2), channel_id=1, source_target_pairs={{0,1},{1,0},{2,3},{3,2},{4,5},{5,4},{6,7},{7,6},{8,9},{9,8},{10,11... | collective-permute-start | bytes 1572872 | tf_op jit(solution)/shard_map/ppermute | solution.py:323
  57.0 18.4 %collective-permute-start.7 = (bf16[128,512]{1,0:T(8,128)(2,1)S(1)}, bf16[128,512]{1,0:T(8,128)(2,1)S(1)}, u32[]{:S(2)}, u32[]{:S(2)}) collective-permute-start(bf16[128,512]{1,0:T(8,128)(2,1)S(1)} %fusion.16), channel_id=1, source_target_pairs={{0,2},{1,3},{2,0},{3,1},{4,6},{5,7},{6,4},{7,5},{8,10},{9,11},{10,... | collective-permute-start | bytes 393224 | tf_op jit(solution)/shard_map/ppermute | solution.py:327
  75.4 20.8 %collective-permute-start.8 = (bf16[256,1024]{1,0:T(8,128)(2,1)S(1)}, bf16[256,1024]{1,0:T(8,128)(2,1)S(1)}, u32[]{:S(2)}, u32[]{:S(2)}) collective-permute-start(bf16[256,1024]{1,0:T(8,128)(2,1)S(1)} %convolution_convert_fusion.1), channel_id=1, source_target_pairs={{0,1},{1,0},{2,3},{3,2},{4,5},{5,4},{6,7},{7,6},{8,9},{9,8},{10,11... | collective-permute-start | bytes 1572872 | tf_op jit(solution)/shard_map/ppermute | solution.py:323
  76.8 19.9 %collective-permute-start.9 = (bf16[256,512]{1,0:T(8,128)(2,1)S(1)}, bf16[256,512]{1,0:T(8,128)(2,1)S(1)}, u32[]{:S(2)}, u32[]{:S(2)}) collective-permute-start(bf16[256,512]{1,0:T(8,128)(2,1)S(1)} %fusion.3), channel_id=1, source_target_pairs={{0,2},{1,3},{2,0},{3,1},{4,6},{5,7},{6,4},{7,5},{8,10},{9,11},{10,... | collective-permute-start | bytes 786440 | tf_op jit(solution)/shard_map/ppermute | solution.py:327
  96.7 13.7 %collective-permute-start.10 = (bf16[256,1024]{1,0:T(8,128)(2,1)S(1)}, bf16[256,1024]{1,0:T(8,128)(2,1)S(1)}, u32[]{:S(2)}, u32[]{:S(2)}) collective-permute-start(bf16[256,1024]{1,0:T(8,128)(2,1)S(1)} %convolution_convert_fusion), channel_id=1, source_target_pairs={{0,1},{1,0},{2,3},{3,2},{4,5},{5,4},{6,7},{7,6},{8,9},{9,8},{10,11... | collective-permute-start | bytes 1572872 | tf_op jit(solution)/shard_map/ppermute | solution.py:323
  96.9 13.4 %collective-permute-start.11 = (bf16[256,512]{1,0:T(8,128)(2,1)S(1)}, bf16[256,512]{1,0:T(8,128)(2,1)S(1)}, u32[]{:S(2)}, u32[]{:S(2)}) collective-permute-start(bf16[256,512]{1,0:T(8,128)(2,1)S(1)} %fusion.4), channel_id=1, source_target_pairs={{0,2},{1,3},{2,0},{3,1},{4,6},{5,7},{6,4},{7,5},{8,10},{9,11},{10,... | collective-permute-start | bytes 786440 | tf_op jit(solution)/shard_map/ppermute | solution.py:327
  110.4 12.5 %collective-permute-start.13 = (bf16[128,1024]{1,0:T(8,128)(2,1)S(1)}, bf16[128,1024]{1,0:T(8,128)(2,1)S(1)}, u32[]{:S(2)}, u32[]{:S(2)}) collective-permute-start(bf16[128,1024]{1,0:T(8,128)(2,1)S(1)} %convolution_convert_fusion.3), channel_id=1, source_target_pairs={{0,1},{1,0},{2,3},{3,2},{4,5},{5,4},{6,7},{7,6},{8,9},{9,8},{10,11... | collective-permute-start | bytes 786440 | tf_op jit(solution)/shard_map/ppermute | solution.py:341
  115.0 10.8 %collective-permute-start.12 = (bf16[256,512]{1,0:T(8,128)(2,1)S(1)}, bf16[256,512]{1,0:T(8,128)(2,1)S(1)}, u32[]{:S(2)}, u32[]{:S(2)}) collective-permute-start(bf16[256,512]{1,0:T(8,128)(2,1)S(1)} %fusion.5), channel_id=1, source_target_pairs={{0,2},{1,3},{2,0},{3,1},{4,6},{5,7},{6,4},{7,5},{8,10},{9,11},{10,... | collective-permute-start | bytes 786440 | tf_op jit(solution)/shard_map/ppermute | solution.py:346
  123.2 5.5 %collective-permute-start.14 = (bf16[128,512]{1,0:T(8,128)(2,1)S(1)}, bf16[128,512]{1,0:T(8,128)(2,1)S(1)}, u32[]{:S(2)}, u32[]{:S(2)}) collective-permute-start(bf16[128,512]{1,0:T(8,128)(2,1)S(1)} %fusion.19), channel_id=1, source_target_pairs={{0,2},{1,3},{2,0},{3,1},{4,6},{5,7},{6,4},{7,5},{8,10},{9,11},{10,... | collective-permute-start | bytes 393224 | tf_op jit(solution)/shard_map/ppermute | solution.py:346
  126.2 2.4 %copy-start.2 = (bf16[1024,512]{1,0:T(8,128)(2,1)}, bf16[1024,512]{1,0:T(8,128)(2,1)S(1)}, u32[]{:S(2)}) copy-start(bf16[1024,512]{1,0:T(8,128)(2,1)S(1)} %fusion.7) | copy-start | bytes 3145732

commit v7 on v6

--- a/solution.py
+++ b/solution.py
@@ -334,7 +334,7 @@
             late = chunk - LAG
             sent[chunk], arrived[late] = lax.optimization_barrier((sent[chunk], arrived[late]))
             other[late] = onward(attended[late], arrived[late])
-            if late - 1 in crossed:
+            if late - 1 in crossed and chunk < count - 1:
                 sent[chunk], crossed[late - 1] = lax.optimization_barrier(
                     (sent[chunk], crossed[late - 1])
                 )

time: 128 us -> 134 us (1.047)
  the two profiles are of different devices: /device:TPU:5 before, /device:TPU:4 now
where the time goes in v7:
time: 134 us; the launch traced here: 133 us
  waiting for transfers between devices  54.2 us (40%)
  Pallas kernels  46.4 us (35%)
  starting transfers between devices  18.2 us (14%)
  matrix products  7.6 us (6%)
  local copies, waits for them, and re-layouts  4.6 us (3%)
  other arithmetic  1.55 us (1%)
    pallas_call x5, Pallas kernels, attend(): pl.pallas_call(partial(attend_kernel, slots=slots, subs=subs, q_block=q_b...  46.4 us
    ppermute x2, waiting for transfers between devices, local(): spans.append(lax.ppermute(own, 'tok', pairs))  17.9 us
    ppermute x3, waiting for transfers between devices, local(): crossed[late] = lax.ppermute(other[late], 'head', far)  12.1 us
    ppermute x4, waiting for transfers between devices, local(): arrived[chunk - 1] = lax.ppermute(sent[chunk - 1], 'head', near)  9.54 us
    ppermute x4, starting transfers between devices, local(): arrived[chunk - 1] = lax.ppermute(sent[chunk - 1], 'head', near)  6.77 us
    ppermute x1, waiting for transfers between devices, local(): arrived[count - 1] = lax.ppermute(sent[count - 1], 'head', near)  6.73 us
    ppermute x2, waiting for transfers between devices, local(): crossed[chunk] = lax.ppermute(other[chunk], 'head', far)  5.77 us
    ppermute x2, starting transfers between devices, local(): spans.append(lax.ppermute(own, 'tok', pairs))  4.69 us
  transfers between devices with their start and end apart: 15, of which 8 were waited for; matrix products, arithmetic and copies ran while one was open for 7% of the time, Pallas kernels for 27%

profile of v7, /device:TPU:4, one launch (start us, length us, event | category | flops | bytes accessed | tf_op | source)
XLA Modules:
  0.0 133.0 jit_solution(7804352187458173126)
XLA Ops:
  0.0 1.1 copy.8
  1.1 1.0 pad_maximum_fusion.1.refs_4_
  2.1 1.3 collective-permute-start
  3.4 3.4 %collective-permute-start.1 = (bf16[2,1024,128]{2,1,0:T(8,128)(2,1)S(1)}, bf16[2,1024,128]{2,1,0:T(8,128)(2,1)S(1)}, u32[]{:S(2)}, u32[]{:S(2)}) collective-permute-start(bf16[2,1024,128]{2,1,0:T(8,128)(2,1)S(1)} %pad_maximum_fusion.1.refs_4_), channel_id=1, source_target_pairs={{0,8},{4,12},{8,16},{12,20},{16,24},{20,28},{1,9},{5,13},{9,17},{1... | collective-permute-start | bytes 1572872 | tf_op jit(solution)/shard_map/ppermute | solution.py:279
  6.9 0.1 pad_add_fusion.2
  7.0 0.1 pad_add_fusion.4.place
  7.1 0.8 copy.9
  7.9 0.2 reshape.11.tasks
  8.1 0.1 pad_add_fusion
  8.2 2.5 %constant_dynamic-slice_fusion = (bf16[1024,512]{1,0:T(8,128)(2,1)S(1)}, bf16[1024,512]{1,0:T(8,128)(2,1)S(1)}, bf16[1024,512]{1,0:T(8,128)(2,1)S(1)}, bf16[1024,512]{1,0:T(8,128)(2,1)S(1)}) fusion(bf16[1024,2048]{1,0:T(8,128)(2,1)} %param.11, s32[]{:T(128)S(6)} %select_n.34, s32[]{:T(128)S(6)} %select_n.32, s32[]{:T(128)S(6)} %select_n.31, s32[]{:T(128)S(6)} %select_n.33), kind=kLoop, calls=%fused_computation.37 | loop fusion | bytes 8388624 | tf_op jit(solution)/shard_map/dynamic_slice | solution.py:282
  10.7 0.3 pad_maximum_fusion
  11.0 17.9 %collective-permute-done.refs_0_ = bf16[2,1024,128]{2,1,0:T(8,128)(2,1)S(1)} collective-permute-done((bf16[2,1024,128]{2,1,0:T(8,128)(2,1)S(1)}, bf16[2,1024,128]{2,1,0:T(8,128)(2,1)S(1)}, u32[]{:S(2)}, u32[]{:S(2)}) %collective-permute-start) | collective-permute-done | bytes 524320 | tf_op jit(solution)/shard_map/ppermute | solution.py:279
  28.9 0.5 collective-permute-start.3
  29.4 1.4 %collective-permute-done.2.refs_1_ = bf16[2,1024,128]{2,1,0:T(8,128)(2,1)S(1)} collective-permute-done((bf16[2,1024,128]{2,1,0:T(8,128)(2,1)S(1)}, bf16[2,1024,128]{2,1,0:T(8,128)(2,1)S(1)}, u32[]{:S(2)}, u32[]{:S(2)}) %collective-permute-start.2) | collective-permute-done | bytes 524320 | tf_op jit(solution)/shard_map/ppermute | solution.py:298
  30.8 0.7 collective-permute-done.3.refs_3_
  31.6 8.0 %shard_map.64 = bf16[128,1024]{1,0:T(8,128)(2,1)S(1)} custom-call(s32[4]{0:T(128)S(1)} %get-tuple-element.42.place, s32[8]{0:T(128)S(1)} %copy-done.1, s32[640]{0:T(1024)S(1)} %reshape.11.tasks, bf16[8,1024,128]{2,1,0:T(8,128)(2,1)S(1)} %copy-done, bf16[2,1024,128]{2,1,0:T(8,128)(2,1)S(1)} %collective-permute-done.refs_0_, ...), custom_call_target="tpu_custom_call" | custom-call | flops 128 | bytes 128 | tf_op jit(solution)/shard_map/pallas_call | solution.py:228
  39.6 0.4 convolution_convert_fusion.4
  40.1 1.7 %collective-permute-start.5 = (bf16[128,1024]{1,0:T(8,128)(2,1)S(1)}, bf16[128,1024]{1,0:T(8,128)(2,1)S(1)}, u32[]{:S(2)}, u32[]{:S(2)}) collective-permute-start(bf16[128,1024]{1,0:T(8,128)(2,1)S(1)} %convolution_convert_fusion.4), channel_id=1, source_target_pairs={{0,1},{1,0},{2,3},{3,2},{4,5},{5,4},{6,7},{7,6},{8,9},{9,8},{10,11... | collective-permute-start | bytes 786440 | tf_op jit(solution)/shard_map/ppermute | solution.py:323
  41.8 14.0 %shard_map.65 = bf16[256,1024]{1,0:T(8,128)(2,1)S(1)} custom-call(s32[4]{0:T(128)S(1)} %get-tuple-element.49.place, s32[8]{0:T(128)S(1)} %copy-done.1, s32[640]{0:T(1024)S(1)} %reshape.11.tasks, bf16[8,1024,128]{2,1,0:T(8,128)(2,1)S(1)} %copy-done, bf16[2,1024,128]{2,1,0:T(8,128)(2,1)S(1)} %collective-permute-done.refs_0_, ...), custom_call_target="tpu_custom_call" | custom-call | flops 256 | bytes 256 | tf_op jit(solution)/shard_map/pallas_call | solution.py:228
  55.7 0.7 convolution_convert_fusion.2
  56.5 0.5 collective-permute-start.6
  57.0 0.3 fusion.16
  57.3 2.7 %collective-permute-start.7 = (bf16[128,512]{1,0:T(8,128)(2,1)S(1)}, bf16[128,512]{1,0:T(8,128)(2,1)S(1)}, u32[]{:S(2)}, u32[]{:S(2)}) collective-permute-start(bf16[128,512]{1,0:T(8,128)(2,1)S(1)} %fusion.16), channel_id=1, source_target_pairs={{0,2},{1,3},{2,0},{3,1},{4,6},{5,7},{6,4},{7,5},{8,10},{9,11},{10,... | collective-permute-start | bytes 393224 | tf_op jit(solution)/shard_map/ppermute | solution.py:327
  59.9 17.5 %shard_map.66 = bf16[256,1024]{1,0:T(8,128)(2,1)S(1)} custom-call(s32[4]{0:T(128)S(1)} %get-tuple-element.56.place, s32[8]{0:T(128)S(1)} %copy-done.1, s32[640]{0:T(1024)S(1)} %reshape.11.tasks, bf16[8,1024,128]{2,1,0:T(8,128)(2,1)S(1)} %copy-done, bf16[2,1024,128]{2,1,0:T(8,128)(2,1)S(1)} %collective-permute-done.refs_0_, ...), custom_call_target="tpu_custom_call" | custom-call | flops 256 | bytes 256 | tf_op jit(solution)/shard_map/pallas_call | solution.py:228
  77.4 0.7 convolution_convert_fusion.1
  78.2 0.4 fusion.3
  78.6 1.6 %collective-permute-start.8 = (bf16[256,1024]{1,0:T(8,128)(2,1)S(1)}, bf16[256,1024]{1,0:T(8,128)(2,1)S(1)}, u32[]{:S(2)}, u32[]{:S(2)}) collective-permute-start(bf16[256,1024]{1,0:T(8,128)(2,1)S(1)} %convolution_convert_fusion.1), channel_id=1, source_target_pairs={{0,1},{1,0},{2,3},{3,2},{4,5},{5,4},{6,7},{7,6},{8,9},{9,8},{10,11... | collective-permute-start | bytes 1572872 | tf_op jit(solution)/shard_map/ppermute | solution.py:323
  80.3 0.3 collective-permute-start.9
  80.6 4.1 %shard_map.67 = bf16[256,1024]{1,0:T(8,128)(2,1)S(1)} custom-call(s32[4]{0:T(128)S(1)} %get-tuple-element.65.place, s32[8]{0:T(128)S(1)} %copy-done.1, s32[640]{0:T(1024)S(1)} %reshape.11.tasks, bf16[8,1024,128]{2,1,0:T(8,128)(2,1)S(1)} %copy-done, bf16[2,1024,128]{2,1,0:T(8,128)(2,1)S(1)} %collective-permute-done.refs_0_, ...), custom_call_target="tpu_custom_call" | custom-call | flops 256 | bytes 256 | tf_op jit(solution)/shard_map/pallas_call | solution.py:228
  84.7 0.3 fusion.15
  85.1 0.7 convolution_convert_fusion
  85.8 9.5 %collective-permute-done.8 = bf16[256,1024]{1,0:T(8,128)(2,1)S(1)} collective-permute-done((bf16[256,1024]{1,0:T(8,128)(2,1)S(1)}, bf16[256,1024]{1,0:T(8,128)(2,1)S(1)}, u32[]{:S(2)}, u32[]{:S(2)}) %collective-permute-start.8) | collective-permute-done | bytes 524320 | tf_op jit(solution)/shard_map/ppermute | solution.py:323
  95.3 0.4 fusion.4
  95.8 2.8 %shard_map.68 = bf16[128,1024]{1,0:T(8,128)(2,1)S(1)} custom-call(s32[4]{0:T(128)S(1)} %pad_add_fusion.4.place, s32[8]{0:T(128)S(1)} %copy-done.1, s32[640]{0:T(1024)S(1)} %reshape.11.tasks, bf16[8,1024,128]{2,1,0:T(8,128)(2,1)S(1)} %copy-done, bf16[2,1024,128]{2,1,0:T(8,128)(2,1)S(1)} %collective-permute-done.refs_0_, ...), custom_call_target="tpu_custom_call" | custom-call | flops 128 | bytes 128 | tf_op jit(solution)/shard_map/pallas_call | solution.py:228
  98.6 0.4 convolution_convert_fusion.3
  99.0 3.0 %collective-permute-start.11 = (bf16[256,1024]{1,0:T(8,128)(2,1)S(1)}, bf16[256,1024]{1,0:T(8,128)(2,1)S(1)}, u32[]{:S(2)}, u32[]{:S(2)}) collective-permute-start(bf16[256,1024]{1,0:T(8,128)(2,1)S(1)} %convolution_convert_fusion), channel_id=1, source_target_pairs={{0,1},{1,0},{2,3},{3,2},{4,5},{5,4},{6,7},{7,6},{8,9},{9,8},{10,11... | collective-permute-start | bytes 1572872 | tf_op jit(solution)/shard_map/ppermute | solution.py:323
  102.0 1.6 %collective-permute-start.10 = (bf16[256,512]{1,0:T(8,128)(2,1)S(1)}, bf16[256,512]{1,0:T(8,128)(2,1)S(1)}, u32[]{:S(2)}, u32[]{:S(2)}) collective-permute-start(bf16[256,512]{1,0:T(8,128)(2,1)S(1)} %fusion.4), channel_id=1, source_target_pairs={{0,2},{1,3},{2,0},{3,1},{4,6},{5,7},{6,4},{7,5},{8,10},{9,11},{10,... | collective-permute-start | bytes 786440 | tf_op jit(solution)/shard_map/ppermute | solution.py:327
  103.6 0.4 fusion.11
  104.0 12.1 %collective-permute-done.10 = bf16[256,512]{1,0:T(8,128)(2,1)S(1)} collective-permute-done((bf16[256,512]{1,0:T(8,128)(2,1)S(1)}, bf16[256,512]{1,0:T(8,128)(2,1)S(1)}, u32[]{:S(2)}, u32[]{:S(2)}) %collective-permute-start.10) | collective-permute-done | bytes 262176 | tf_op jit(solution)/shard_map/ppermute | solution.py:327
  116.2 0.4 fusion.9
  116.7 0.4 fusion.5
  117.2 1.5 %collective-permute-start.12 = (bf16[256,512]{1,0:T(8,128)(2,1)S(1)}, bf16[256,512]{1,0:T(8,128)(2,1)S(1)}, u32[]{:S(2)}, u32[]{:S(2)}) collective-permute-start(bf16[256,512]{1,0:T(8,128)(2,1)S(1)} %fusion.5), channel_id=1, source_target_pairs={{0,2},{1,3},{2,0},{3,1},{4,6},{5,7},{6,4},{7,5},{8,10},{9,11},{10,... | collective-permute-start | bytes 786440 | tf_op jit(solution)/shard_map/ppermute | solution.py:346
  118.6 6.7 %collective-permute-done.13 = bf16[128,1024]{1,0:T(8,128)(2,1)S(1)} collective-permute-done((bf16[128,1024]{1,0:T(8,128)(2,1)S(1)}, bf16[128,1024]{1,0:T(8,128)(2,1)S(1)}, u32[]{:S(2)}, u32[]{:S(2)}) %collective-permute-start.13) | collective-permute-done | bytes 262176 | tf_op jit(solution)/shard_map/ppermute | solution.py:341
  125.4 0.3 fusion.19
  125.7 1.6 %collective-permute-done.12 = bf16[256,512]{1,0:T(8,128)(2,1)S(1)} collective-permute-done((bf16[256,512]{1,0:T(8,128)(2,1)S(1)}, bf16[256,512]{1,0:T(8,128)(2,1)S(1)}, u32[]{:S(2)}, u32[]{:S(2)}) %collective-permute-start.12) | collective-permute-done | bytes 262176 | tf_op jit(solution)/shard_map/ppermute | solution.py:346
  127.3 0.4 fusion.7
  127.8 4.2 %collective-permute-done.14 = bf16[128,512]{1,0:T(8,128)(2,1)S(1)} collective-permute-done((bf16[128,512]{1,0:T(8,128)(2,1)S(1)}, bf16[128,512]{1,0:T(8,128)(2,1)S(1)}, u32[]{:S(2)}, u32[]{:S(2)}) %collective-permute-start.14) | collective-permute-done | bytes 131104 | tf_op jit(solution)/shard_map/ppermute | solution.py:346
  132.0 1.0 fusion.18
  (17 shorter events, 0.3 us)
Async XLA Ops:
  2.1 26.8 %collective-permute-start = (bf16[2,1024,128]{2,1,0:T(8,128)(2,1)S(1)}, bf16[2,1024,128]{2,1,0:T(8,128)(2,1)S(1)}, u32[]{:S(2)}, u32[]{:S(2)}) collective-permute-start(bf16[2,1024,128]{2,1,0:T(8,128)(2,1)S(1)} %pad_maximum_fusion.1.refs_4_), channel_id=1, source_target_pairs={{0,16},{4,20},{8,24},{12,28},{1,17},{5,21},{9,25},{13,29},{2,18},{... | collective-permute-start | bytes 1572872 | tf_op jit(solution)/shard_map/ppermute | solution.py:279
  3.4 25.5 %collective-permute-start.1 = (bf16[2,1024,128]{2,1,0:T(8,128)(2,1)S(1)}, bf16[2,1024,128]{2,1,0:T(8,128)(2,1)S(1)}, u32[]{:S(2)}, u32[]{:S(2)}) collective-permute-start(bf16[2,1024,128]{2,1,0:T(8,128)(2,1)S(1)} %pad_maximum_fusion.1.refs_4_), channel_id=1, source_target_pairs={{0,8},{4,12},{8,16},{12,20},{16,24},{20,28},{1,9},{5,13},{9,17},{1... | collective-permute-start | bytes 1572872 | tf_op jit(solution)/shard_map/ppermute | solution.py:279
  6.8 22.6 %collective-permute-start.4 = (bf16[2,1024,128]{2,1,0:T(8,128)(2,1)S(1)}, bf16[2,1024,128]{2,1,0:T(8,128)(2,1)S(1)}, u32[]{:S(2)}, u32[]{:S(2)}) collective-permute-start(bf16[2,1024,128]{2,1,0:T(8,128)(2,1)S(1)} %pad_maximum_fusion.1.refs_4_), channel_id=1, source_target_pairs={{0,4},{4,0},{8,12},{12,8},{16,20},{20,16},{24,28},{28,24},{1,5},{5... | collective-permute-start | bytes 1572872 | tf_op jit(solution)/shard_map/ppermute | solution.py:298
  10.7 20.9 %copy-start = (bf16[8,1024,128]{2,1,0:T(8,128)(2,1)S(1)}, bf16[8,1024,128]{2,1,0:T(8,128)(2,1)}, u32[]{:S(2)}) copy-start(bf16[8,1024,128]{2,1,0:T(8,128)(2,1)} %q_ref.9) | copy-start | bytes 6291460
  10.7 20.9 %copy-start.1 = (s32[8]{0:T(128)S(1)}, s32[8]{0:T(128)}, u32[]{:S(2)}) copy-start(s32[8]{0:T(128)} %lengths.9) | copy-start | bytes 100
  28.9 1.9 %collective-permute-start.2 = (bf16[2,1024,128]{2,1,0:T(8,128)(2,1)S(1)}, bf16[2,1024,128]{2,1,0:T(8,128)(2,1)S(1)}, u32[]{:S(2)}, u32[]{:S(2)}) collective-permute-start(bf16[2,1024,128]{2,1,0:T(8,128)(2,1)S(1)} %collective-permute-done.refs_0_), channel_id=1, source_target_pairs={{0,4},{4,0},{8,12},{12,8},{16,20},{20,16},{24,28},{28,24},{1,5},{5... | collective-permute-start | bytes 1572872 | tf_op jit(solution)/shard_map/ppermute | solution.py:298
  28.9 2.7 %collective-permute-start.3 = (bf16[2,1024,128]{2,1,0:T(8,128)(2,1)S(1)}, bf16[2,1024,128]{2,1,0:T(8,128)(2,1)S(1)}, u32[]{:S(2)}, u32[]{:S(2)}) collective-permute-start(bf16[2,1024,128]{2,1,0:T(8,128)(2,1)S(1)} %collective-permute-done.1.refs_2_), channel_id=1, source_target_pairs={{0,4},{4,0},{8,12},{12,8},{16,20},{20,16},{24,28},{28,24},{1,5},{5... | collective-permute-start | bytes 1572872 | tf_op jit(solution)/shard_map/ppermute | solution.py:298
  40.1 16.3 %collective-permute-start.5 = (bf16[128,1024]{1,0:T(8,128)(2,1)S(1)}, bf16[128,1024]{1,0:T(8,128)(2,1)S(1)}, u32[]{:S(2)}, u32[]{:S(2)}) collective-permute-start(bf16[128,1024]{1,0:T(8,128)(2,1)S(1)} %convolution_convert_fusion.4), channel_id=1, source_target_pairs={{0,1},{1,0},{2,3},{3,2},{4,5},{5,4},{6,7},{7,6},{8,9},{9,8},{10,11... | collective-permute-start | bytes 786440 | tf_op jit(solution)/shard_map/ppermute | solution.py:323
  56.5 21.7 %collective-permute-start.6 = (bf16[256,1024]{1,0:T(8,128)(2,1)S(1)}, bf16[256,1024]{1,0:T(8,128)(2,1)S(1)}, u32[]{:S(2)}, u32[]{:S(2)}) collective-permute-start(bf16[256,1024]{1,0:T(8,128)(2,1)S(1)} %convolution_convert_fusion.2), channel_id=1, source_target_pairs={{0,1},{1,0},{2,3},{3,2},{4,5},{5,4},{6,7},{7,6},{8,9},{9,8},{10,11... | collective-permute-start | bytes 1572872 | tf_op jit(solution)/shard_map/ppermute | solution.py:323
  57.3 21.3 %collective-permute-start.7 = (bf16[128,512]{1,0:T(8,128)(2,1)S(1)}, bf16[128,512]{1,0:T(8,128)(2,1)S(1)}, u32[]{:S(2)}, u32[]{:S(2)}) collective-permute-start(bf16[128,512]{1,0:T(8,128)(2,1)S(1)} %fusion.16), channel_id=1, source_target_pairs={{0,2},{1,3},{2,0},{3,1},{4,6},{5,7},{6,4},{7,5},{8,10},{9,11},{10,... | collective-permute-start | bytes 393224 | tf_op jit(solution)/shard_map/ppermute | solution.py:327
  78.6 16.7 %collective-permute-start.8 = (bf16[256,1024]{1,0:T(8,128)(2,1)S(1)}, bf16[256,1024]{1,0:T(8,128)(2,1)S(1)}, u32[]{:S(2)}, u32[]{:S(2)}) collective-permute-start(bf16[256,1024]{1,0:T(8,128)(2,1)S(1)} %convolution_convert_fusion.1), channel_id=1, source_target_pairs={{0,1},{1,0},{2,3},{3,2},{4,5},{5,4},{6,7},{7,6},{8,9},{9,8},{10,11... | collective-permute-start | bytes 1572872 | tf_op jit(solution)/shard_map/ppermute | solution.py:323
  80.3 15.5 %collective-permute-start.9 = (bf16[256,512]{1,0:T(8,128)(2,1)S(1)}, bf16[256,512]{1,0:T(8,128)(2,1)S(1)}, u32[]{:S(2)}, u32[]{:S(2)}) collective-permute-start(bf16[256,512]{1,0:T(8,128)(2,1)S(1)} %fusion.3), channel_id=1, source_target_pairs={{0,2},{1,3},{2,0},{3,1},{4,6},{5,7},{6,4},{7,5},{8,10},{9,11},{10,... | collective-permute-start | bytes 786440 | tf_op jit(solution)/shard_map/ppermute | solution.py:327
  99.0 17.6 %collective-permute-start.11 = (bf16[256,1024]{1,0:T(8,128)(2,1)S(1)}, bf16[256,1024]{1,0:T(8,128)(2,1)S(1)}, u32[]{:S(2)}, u32[]{:S(2)}) collective-permute-start(bf16[256,1024]{1,0:T(8,128)(2,1)S(1)} %convolution_convert_fusion), channel_id=1, source_target_pairs={{0,1},{1,0},{2,3},{3,2},{4,5},{5,4},{6,7},{7,6},{8,9},{9,8},{10,11... | collective-permute-start | bytes 1572872 | tf_op jit(solution)/shard_map/ppermute | solution.py:323
  102.0 14.2 %collective-permute-start.10 = (bf16[256,512]{1,0:T(8,128)(2,1)S(1)}, bf16[256,512]{1,0:T(8,128)(2,1)S(1)}, u32[]{:S(2)}, u32[]{:S(2)}) collective-permute-start(bf16[256,512]{1,0:T(8,128)(2,1)S(1)} %fusion.4), channel_id=1, source_target_pairs={{0,2},{1,3},{2,0},{3,1},{4,6},{5,7},{6,4},{7,5},{8,10},{9,11},{10,... | collective-permute-start | bytes 786440 | tf_op jit(solution)/shard_map/ppermute | solution.py:327
  116.6 8.7 %collective-permute-start.13 = (bf16[128,1024]{1,0:T(8,128)(2,1)S(1)}, bf16[128,1024]{1,0:T(8,128)(2,1)S(1)}, u32[]{:S(2)}, u32[]{:S(2)}) collective-permute-start(bf16[128,1024]{1,0:T(8,128)(2,1)S(1)} %convolution_convert_fusion.3), channel_id=1, source_target_pairs={{0,1},{1,0},{2,3},{3,2},{4,5},{5,4},{6,7},{7,6},{8,9},{9,8},{10,11... | collective-permute-start | bytes 786440 | tf_op jit(solution)/shard_map/ppermute | solution.py:341
  117.2 10.2 %collective-permute-start.12 = (bf16[256,512]{1,0:T(8,128)(2,1)S(1)}, bf16[256,512]{1,0:T(8,128)(2,1)S(1)}, u32[]{:S(2)}, u32[]{:S(2)}) collective-permute-start(bf16[256,512]{1,0:T(8,128)(2,1)S(1)} %fusion.5), channel_id=1, source_target_pairs={{0,2},{1,3},{2,0},{3,1},{4,6},{5,7},{6,4},{7,5},{8,10},{9,11},{10,... | collective-permute-start | bytes 786440 | tf_op jit(solution)/shard_map/ppermute | solution.py:346
  125.7 6.3 %collective-permute-start.14 = (bf16[128,512]{1,0:T(8,128)(2,1)S(1)}, bf16[128,512]{1,0:T(8,128)(2,1)S(1)}, u32[]{:S(2)}, u32[]{:S(2)}) collective-permute-start(bf16[128,512]{1,0:T(8,128)(2,1)S(1)} %fusion.19), channel_id=1, source_target_pairs={{0,2},{1,3},{2,0},{3,1},{4,6},{5,7},{6,4},{7,5},{8,10},{9,11},{10,... | collective-permute-start | bytes 393224 | tf_op jit(solution)/shard_map/ppermute | solution.py:346
  127.8 4.2 %copy-start.2 = (bf16[1024,512]{1,0:T(8,128)(2,1)}, bf16[1024,512]{1,0:T(8,128)(2,1)S(1)}, u32[]{:S(2)}) copy-start(bf16[1024,512]{1,0:T(8,128)(2,1)S(1)} %fusion.7) | copy-start | bytes 3145732
